TPU v7x, 32 devices: a whole 2x2x4 slice. The times are simulated.
32 devices in a mesh: dp: 4 (over y, x), tensor: 8 (over z, core).
Axes of the slice: x: 2, y: 2, z: 4, core: 2. Of those that a mesh axis runs over, the one named last changes fastest.
Arguments:
- hidden: bfloat16 [2048, 53248], P('dp', 'tensor'), may hold values from -6 to 6
- cotangent: bfloat16 [2048, 16384], P('dp', 'tensor'), may hold values from -96 to 96
- prompt_group_index: int32 [2048], P('dp'), may hold values from 0 to 255
- answer_token_mask: int32 [2048], P('dp'), may hold values 0 or 1
- token_reward_order: int32 [2048], P('dp'), may hold values from 0 to 15
- source_lowdim_matrix: float32 [32, 53248], P(None, 'tensor'), may hold values from -0.02734375 to 0.02734375
- running_mean_source_matrix: float32 [32, 53248], P(None, 'tensor'), may hold values from -6 to 6
- running_variance_source_matrix: float32 [32, 53248], P(None, 'tensor'), may hold values from 0.01 to 1
- target_lowdim_matrix: float32 [32, 16384], P(None, 'tensor'), may hold values from -1 to 1
- running_mean_target_matrix: float32 [32, 16384], P(None, 'tensor'), may hold values from -0.6 to 0.6
- running_variance_target_matrix: float32 [32, 16384], P(None, 'tensor'), may hold values from 0.0001 to 0.01
- frozen_down_weight: bfloat16 [53248, 16384], P('tensor', 'dp'), may hold values from -0.02734375 to 0.02734375
- sampled_token_input: bfloat16 [512, 53248], P(None, 'tensor'), may hold values from -6 to 6
Outputs:
- rollout_out: bfloat16 [512, 16384], P(None, ('dp', 'tensor'))
- next_left_factor: float32 [32, 53248], P('dp', 'tensor')
- next_first_moment_left: float32 [32, 53248], P('dp', 'tensor')
- next_second_moment_left: float32 [32, 53248], P('dp', 'tensor')
- next_right_factor: float32 [32, 16384], P('dp', 'tensor')
- next_first_moment_right: float32 [32, 16384], P('dp', 'tensor')
- next_second_moment_right: float32 [32, 16384], P('dp', 'tensor')
All inputs are finite; a program needn't handle non-finite values. No bound on the sum of `answer_token_mask` on one device may be relied on, other than what follows from the above.
Results may differ from a plain program's by a relative error of at most 0.0063.
Values may be sent and summed in bfloat16 or wider, within the bound.
No kernel may reach another device: no remote copies, remote signals or barrier semaphores. Data moves between devices by JAX's collectives and lax.ppermute only.
A program may use at most 192 MiB of HBM per device.

v0:
```python
import functools

import jax
import jax.numpy as jnp
from jax import lax
from jax.experimental import pallas as pl
from jax.experimental.pallas import tpu as pltpu
from jax.sharding import PartitionSpec as P

adapter_scale = 2.0
bias_one = 1.0 - 0.9**10
bias_two = 1.0 - 0.999**10

F32 = jnp.float32
BF16 = jnp.bfloat16
LANES = 128
MIB = 1 << 20


def dot(a, b):
    return jnp.dot(a, b, preferred_element_type=F32)


def dot_nt(a, b):
    length = a.shape[1]
    cut = length // 512 * 256
    if cut < 512:
        return dot_nt_part(a, b, 0, length)
    return dot_nt_part(a, b, 0, cut) + dot_nt_part(a, b, cut, length)


def dot_nt_part(a, b, first, last):
    dims = (((1,), (1,)), ((), ()))
    return lax.dot_general(a[:, first:last], b[:, first:last], dims, preferred_element_type=F32)


def adaptive_moment_step(param, grad, first, second):
    first = 0.9 * first + 0.1 * grad
    second = 0.999 * second + 0.001 * grad * grad
    param = param - 0.004 * (first / bias_one) / (jnp.sqrt(second / bias_two) + 1e-08)
    return (param, first, second)


def tile_of(length, limit):
    units = length // LANES
    return LANES * max(u for u in range(1, limit // LANES + 1) if units % u == 0)


def split_bf16(value):
    high = value.astype(BF16)
    return high, (value - high.astype(F32)).astype(BF16)


def pick(index, choices):
    result = choices[0]
    for at in range(1, len(choices)):
        result = jnp.where(index == at, choices[at], result)
    return result


def shape(dims, kind):
    return jax.ShapeDtypeStruct(dims, kind)


ANY = pl.BlockSpec(memory_space=pl.ANY)
HBM = pl.BlockSpec(memory_space=pltpu.HBM)
VMEM = pl.BlockSpec(memory_space=pltpu.VMEM)


def call(kernel, name, held, far, outputs, far_outputs, scratch, flops, vmem, after=()):
    first = len(held) + len(far)
    moved = sum(a.size * a.dtype.itemsize for a in [*far, *far_outputs])

    def body(*refs):
        kernel(*refs[:first], *refs[first + len(after) :])

    return pl.pallas_call(
        body,
        name=name,
        out_shape=[*outputs, *far_outputs],
        in_specs=[VMEM] * len(held) + [HBM] * len(far) + [ANY] * len(after),
        out_specs=[VMEM] * len(outputs) + [HBM] * len(far_outputs),
        scratch_shapes=scratch,
        compiler_params=pltpu.CompilerParams(vmem_limit_bytes=vmem * MIB),
        cost_estimate=pl.CostEstimate(flops=flops, bytes_accessed=moved, transcendentals=0),
    )(*held, *far, *after)


def in_turn(fetches, ahead=2):
    for fetch in fetches[:ahead]:
        fetch.start()
    done = []

    def arrive():
        fetches[len(done)].wait()
        done.append(True)
        if len(done) - 1 + ahead < len(fetches):
            fetches[len(done) - 1 + ahead].start()

    return arrive


def project_kernel(peers, part, index, mask, order, far_hidden, far_a, far_cot, far_b, pieces, stats, *rest):
    packed, hidden, a, cot, b, arrived = rest
    rank = a.shape[0]
    width = hidden.shape[2]
    chunks = hidden.shape[0]

    pairs = [(far_a, a)]
    pairs += [(far_hidden.at[:, at * width : (at + 1) * width], hidden.at[at]) for at in range(chunks)]
    pairs += [(far_cot, cot), (far_b, b)]
    fetches = [pltpu.make_async_copy(*pair, arrived.at[at]) for at, pair in enumerate(pairs)]
    arrive = in_turn(fetches, 3)
    arrive()
    left = a[...].astype(BF16)
    total = None
    for at in range(chunks):
        arrive()
        product = dot_nt(hidden.at[at], left[:, at * width : (at + 1) * width])
        total = product if total is None else total + product
    arrive()
    arrive()
    high, low = split_bf16(b[...])
    both = dot_nt(cot, jnp.concatenate([high, low], axis=0))
    packed[:, 0:rank] = total
    packed[:, rank : 2 * rank] = both[:, :rank] + both[:, rank:]
    for k in range(peers):
        block = packed[k * part : (k + 1) * part, :]
        pieces[k] = jnp.concatenate([block[: part // 2], block[part // 2 :]], axis=1)
    groups, tokens = stats.shape[1], index.shape[1]
    member = (lax.broadcasted_iota(jnp.int32, (groups, tokens), 0) == index[...]).astype(F32)
    row = lax.broadcasted_iota(jnp.int32, (8, tokens), 0)
    values = jnp.where(row == 0, mask[...], 0)
    values = jnp.where(row == 1, mask[...] * order[...], values)
    values = jnp.where(row == 2, mask[...] * order[...] * order[...], values)
    stats[...] = dot_nt(values.astype(F32).astype(BF16), member.astype(BF16))


def weigh_kernel(peers, rank, all_index, all_mask, all_order, pieces, *rest):
    stats, (out, column) = rest[:-2], rest[-2:]
    part, tokens = out.shape[1], all_index.shape[1]
    groups = stats[0].shape[1]
    sums = stats[0][...]
    for other in stats[1:]:
        sums = sums + other[...]
    counts, firsts, squares = sums[0:1, :], sums[1:2, :], sums[2:3, :]
    safe = jnp.maximum(counts, 1.0)
    mean = firsts / safe
    spread = jnp.maximum(jnp.sqrt(jnp.maximum(squares / safe - mean * mean, 0.0)), 1.0)
    total = jnp.maximum(jnp.sum(counts, axis=1, keepdims=True), 1.0)

    row = lax.broadcasted_iota(jnp.int32, (LANES, tokens), 0)
    tall = jnp.where(row == 0, all_index[...], 0)
    tall = jnp.where(row == 1, all_mask[...], tall)
    tall = jnp.where(row == 2, all_order[...], tall)
    column[...] = jnp.transpose(tall.astype(F32))
    own = column[pl.ds(pl.multiple_of(lax.axis_index("tensor") * part, part), part), :]
    index, mask, order = own[:, 0:1], own[:, 1:2], own[:, 2:3]
    member = index == lax.broadcasted_iota(jnp.int32, (part, groups), 1).astype(F32)
    own_mean = jnp.sum(jnp.where(member, mean, 0.0), axis=1, keepdims=True)
    own_spread = jnp.sum(jnp.where(member, spread, 0.0), axis=1, keepdims=True)
    coefficient = -mask * (order - own_mean) / own_spread / total

    both = pieces[0]
    for at in range(1, peers):
        both = both + pieces[at]
    both = jnp.concatenate([both[:, : 2 * rank], both[:, 2 * rank : 4 * rank]], axis=0)
    both = both * coefficient
    back = both[:, rank:].astype(BF16).astype(F32)
    high, low = split_bf16(both[:, :rank])
    whole = [back, high.astype(F32), low.astype(F32), jnp.zeros((part, LANES - 3 * rank), F32)]
    share = jnp.concatenate(whole, axis=1).astype(BF16)
    for at in range(peers):
        out[at] = share


def gradient_kernel(replicas, rank, shares, far_hidden, far_cot, own_a, own_b, *rest):
    sent, (grad, hidden, cot, arrived) = rest[:-4], rest[-4:]
    rows = rank // replicas
    half = grad.shape[1] // 2
    me = lax.axis_index("dp")
    chunks, high, _ = hidden.shape

    pairs = [(far_hidden.at[at * high : (at + 1) * high, :], hidden.at[at]) for at in range(chunks)]
    pairs.append((far_cot, cot))
    fetches = [pltpu.make_async_copy(*pair, arrived.at[at]) for at, pair in enumerate(pairs)]
    arrive = in_turn(fetches)
    tall = jnp.concatenate([shares[at] for at in range(shares.shape[0])], axis=0)
    wide = jnp.transpose(tall.astype(F32)).astype(BF16)
    for at in range(chunks):
        arrive()
        product = adapter_scale * dot(wide[0:rank, at * high : (at + 1) * high], hidden[at])
        if at == 0:
            grad[...] = product
        else:
            grad[...] += product
    arrive()
    both = dot(wide[rank : 3 * rank, :], cot[...])
    whole = adapter_scale * (both[:rank] + both[rank:])
    pieces = [grad[j * rows : (j + 1) * rows, :] for j in range(replicas)]
    own_a[...] = pick(me, pieces)
    own_b[...] = whole
    folded = [whole[at : at + 2 * rows] for at in range(0, rank, 2 * rows)]
    folded = jnp.concatenate(folded, axis=1).astype(BF16)
    for k in range(1, replicas):
        piece = pick(lax.bitwise_xor(me, k), pieces)
        halves = jnp.concatenate([piece[:, :half], piece[:, half:]], axis=0)
        sent[k - 1][:, 0:half] = halves.astype(BF16)
        sent[k - 1][:, half:] = folded


def update_kernel(replicas, own_a, own_b, x, *rest):
    received, rest = rest[: replicas - 1], rest[replicas - 1 :]
    factors, (sent, out), results = rest[:6], rest[6:8], rest[8:14]
    (a, am, av, b, bm, bv), made, arrived, left = rest[14:20], rest[20:26], rest[26], rest[27]
    rows, inner = a.shape
    rank, columns = b.shape
    me = lax.axis_index("dp")

    def fetch(at):
        source = factors[at]
        if at < 3 and source.shape[0] != rows:
            source = source.at[pl.ds(pl.multiple_of(me * rows, rows), rows), :]
        return pltpu.make_async_copy(source, (a, am, av, b, bm, bv)[at], arrived.at[at])

    def keep(at):
        return pltpu.make_async_copy(made[at], results[at], arrived.at[at])

    for at in range(6):
        fetch(at).start()
    grad_a, grad_b = own_a[...], own_b[...]
    half = inner // 2
    for other in received:
        folded = other[...].astype(F32)
        grad_a = grad_a + jnp.concatenate([folded[:rows, :half], folded[rows:, :half]], axis=1)
        parts = [folded[:, at : at + columns] for at in range(half, folded.shape[1], columns)]
        grad_b = grad_b + jnp.concatenate(parts, axis=0)
    for at in range(6):
        fetch(at).wait()
    made[0][...], made[1][...], made[2][...] = adaptive_moment_step(a[...], grad_a, am[...], av[...])
    padding = jnp.zeros((left.shape[0] - rows, inner), F32)
    left[...] = jnp.concatenate([made[0][...], padding], axis=0).astype(BF16)
    next_b, first_b, second_b = adaptive_moment_step(b[...], grad_b, bm[...], bv[...])
    for array, result in zip((next_b, first_b, second_b), made[3:]):
        result[...] = pick(me, [array[j * rows : (j + 1) * rows] for j in range(replicas)])
    for at in range(6):
        keep(at).start()
    width = columns // replicas
    choices = [next_b[:, j * width : (j + 1) * width] for j in range(replicas)]
    sent[...] = pick(me, choices).astype(BF16)
    product = dot_nt(x, left)
    empty = jnp.zeros((product.shape[0], LANES - left.shape[0]), F32)
    product = jnp.transpose(jnp.concatenate([product, empty], axis=1))[0:rows, :]
    for at in range(out.shape[0]):
        out[at] = product
    for at in range(6):
        keep(at).wait()


def rollout_kernel(jobs, following, given, x, *rest):
    first = rest[0] if given else None
    w, *outs = rest[given:-2]
    held, arrived = rest[-2:]
    after = outs.pop() if following else None
    _, inner, tile = held.shape
    width = outs[0].shape[1]
    tiles = width // tile
    me = lax.axis_index("tensor")
    todo = [(job, at) for job in range(len(jobs)) for at in range(tiles)]

    def columns(job, at):
        differs, other = job
        device = lax.bitwise_xor(me, 2 * differs + other)
        return w.at[:, pl.ds(pl.multiple_of(device * width + at * tile, tile), tile)]

    fetches, blocks = [], [first] if given else []
    for number in range(len(blocks), len(todo)):
        job, at = todo[number]
        slot = number - given
        blocks.append(held.at[slot])
        fetches.append(pltpu.make_async_copy(columns(jobs[job], at), held.at[slot], arrived.at[slot]))
    if following:
        fetches.append(pltpu.make_async_copy(columns(following, 0), after, arrived.at[len(fetches)]))
    arrive = in_turn(fetches)
    cut = x.shape[0] // 2
    for number, (job, at) in enumerate(todo):
        if number or not given:
            arrive()
        block = blocks[number]
        for rows in (slice(0, cut), slice(cut, 2 * cut)):
            product = dot(x[rows, :], block[...])
            outs[job][rows, at * tile : (at + 1) * tile] = product.astype(outs[job].dtype)
    if following:
        arrive()


def join_kernel(*refs):
    total = refs[0][...].astype(F32)
    for leaf in refs[1:-1]:
        total = total + leaf[...].astype(F32)
    refs[-1][...] = total.astype(refs[-1].dtype)


def finish_kernel(replicas, peers, rank, factor, *rest):
    products, leaves, (out, made, kept) = rest[:replicas], rest[replicas:-3], rest[-3:]
    me = lax.axis_index("dp")
    held = [p[...] for p in products]
    product = [pick(lax.bitwise_xor(me, r), held) for r in range(replicas)]
    high, low = split_bf16(jnp.concatenate(product, axis=0))
    empty = jnp.zeros((LANES - 2 * rank, high.shape[1]), F32)
    wide = jnp.concatenate([high.astype(F32), low.astype(F32), empty], axis=0)
    tall = jnp.transpose(wide).astype(BF16)
    empty = jnp.zeros((LANES - 2 * rank, factor.shape[1]), BF16)
    total = adapter_scale * dot(tall, jnp.concatenate([factor[...], factor[...], empty], axis=0))
    for leaf in leaves:
        total = total + leaf[...].astype(F32)
    made[...] = total.astype(BF16)
    copy = pltpu.make_async_copy(made, out, kept)
    copy.start()
    copy.wait()


def shards(
    hidden,
    cotangent,
    prompt_group_index,
    answer_token_mask,
    token_reward_order,
    source_lowdim_matrix,
    running_mean_source_matrix,
    running_variance_source_matrix,
    target_lowdim_matrix,
    running_mean_target_matrix,
    running_variance_target_matrix,
    frozen_down_weight,
    sampled_token_input,
):
    replicas, peers = lax.axis_size("dp"), lax.axis_size("tensor")
    me_dp = lax.axis_index("dp")
    x, w = sampled_token_input, frozen_down_weight
    tokens, inner = hidden.shape
    columns = cotangent.shape[1]
    rank = source_lowdim_matrix.shape[0]
    rows = rank // replicas
    part = tokens // peers
    groups = tokens * replicas // 8
    rollout = x.shape[0]
    own_width = w.shape[1] // peers
    deep = tile_of(inner, 1664)

    def xor(array, k, axis="tensor"):
        return lax.ppermute(array, axis, [(i, i ^ k) for i in range(lax.axis_size(axis))])

    tok = [
        array.reshape(1, tokens) for array in (prompt_group_index, answer_token_mask, token_reward_order)
    ]
    pieces, stats = call(
        functools.partial(project_kernel, peers, part),
        "project",
        tok,
        [hidden, source_lowdim_matrix, cotangent, target_lowdim_matrix],
        [shape((peers, part // 2, LANES), F32), shape((8, groups), F32)],
        [],
        [
            pltpu.VMEM((tokens, 2 * rank), F32),
            pltpu.VMEM((inner // deep, tokens, deep), BF16),
            pltpu.VMEM((rank, inner), F32),
            pltpu.VMEM((tokens, columns), BF16),
            pltpu.VMEM((rank, columns), F32),
            pltpu.SemaphoreType.DMA((inner // deep + 3,)),
        ],
        2 * tokens * (inner + columns) * 256,
        54,
    )
    all_stats = [stats] + [xor(stats, k, "dp") for k in range(1, replicas)]
    pieces = lax.all_to_all(pieces, "tensor", 0, 0)

    (share,) = call(
        functools.partial(weigh_kernel, peers, rank),
        "weigh",
        [*tok, pieces, *all_stats],
        [],
        [shape((peers, part, LANES), BF16)],
        [],
        [pltpu.VMEM((tokens, LANES), F32)],
        2 * part * groups,
        16,
    )
    shares = lax.all_to_all(share, "tensor", 0, 0)

    chips = peers // 2
    tile = min(own_width, 256)
    crossed, arrived, leaves, handed = {}, {}, [], None

    def form(jobs, following, after, held_up=()):
        nonlocal handed, leaves
        given = handed is not None
        results = [shape((rollout, own_width), BF16 if other else F32) for _, other in jobs]
        slots = len(jobs) * own_width // tile - given
        if following:
            results.append(shape((inner, tile), BF16))
        *results, last = call(
            functools.partial(rollout_kernel, jobs, following, given),
            "rollout%d" % jobs[0][0],
            [x, handed] if given else [x],
            [w],
            results,
            [],
            [
                pltpu.VMEM((max(slots, 1), inner, tile), BF16),
                pltpu.SemaphoreType.DMA((slots + 1,)),
            ],
            2 * rollout * inner * own_width * len(jobs),
            34,
            after,
        )
        handed = last if following else None
        if not following:
            results.append(last)
        for (m, other), result in zip(jobs, results):
            if other:
                crossed[m] = xor(result, 1)
        for (m, other), result in zip(jobs, results):
            if other:
                continue
            leaves = [result, crossed[m]]
            bit = 1
            while bit < chips and not m & bit:
                leaves.append(arrived[m | bit])
                bit *= 2
            if m:
                joined = shape((rollout, own_width), BF16)
                (result,) = call(join_kernel, "join", leaves, [], [joined], [], [], 0, 8, held_up)
                arrived[m] = xor(result, 2 * bit)
            last = result
        return last

    half = chips // 2
    before = form([(chips - 1, 1), (chips - 1, 0), (chips - 2, 1)], None, [share], [shares])
    for m in range(chips - 2, half, -1):
        before = form([(m, 0), (m - 1, 1)], None, [before])

    own_a, own_b, *sent = call(
        functools.partial(gradient_kernel, replicas, rank),
        "gradient",
        [shares],
        [hidden, cotangent],
        [shape((rows, inner), F32), shape((rank, columns), F32)]
        + [shape((2 * rows, inner // 2 + columns * replicas // 2), BF16)] * (replicas - 1),
        [],
        [
            pltpu.VMEM((rank, inner), F32),
            pltpu.VMEM((4, tokens // 4, inner), BF16),
            pltpu.VMEM((tokens, columns), BF16),
            pltpu.SemaphoreType.DMA((5,)),
        ],
        2 * tokens * (inner + columns) * 256,
        54,
        [before],
    )
    received = [xor(array, k + 1, "dp") for k, array in enumerate(sent)]
    before = form([(half, 0), (half - 1, 1)], (half - 1, 0), [own_a])

    left = [source_lowdim_matrix, running_mean_source_matrix, running_variance_source_matrix]
    right = [target_lowdim_matrix, running_mean_target_matrix, running_variance_target_matrix]
    if rows % 8:
        left = [lax.dynamic_slice_in_dim(array, me_dp * rows, rows, 0) for array in left]
    own_left, own_right = shape((rows, inner), F32), shape((rows, columns), F32)
    sent_b, product, *updated = call(
        functools.partial(update_kernel, replicas),
        "update",
        [own_a, own_b, x, *received],
        [*left, *right],
        [shape((rank, columns // replicas), BF16), shape((peers, rows, rollout), F32)],
        [own_left] * 3 + [own_right] * 3,
        [pltpu.VMEM((rows, inner), F32)] * 3
        + [pltpu.VMEM((rank, columns), F32)] * 3
        + [pltpu.VMEM((rows, inner), F32)] * 3
        + [pltpu.VMEM((rows, columns), F32)] * 3
        + [pltpu.SemaphoreType.DMA((6,)), pltpu.VMEM((16, inner), BF16)],
        2 * rollout * inner * 256,
        28,
        [before],
    )
    pairs = [(dp * peers + at, at * replicas + dp) for dp in range(replicas) for at in range(peers)]
    factor = lax.ppermute(sent_b, ("dp", "tensor"), pairs)
    for m in range(half - 1, -1, -1):
        jobs = [(m, 0), (m - 1, 1)] if m else [(0, 0)]
        before = form(jobs, (m - 1, 0) if m else None, [before, product])
    product = jnp.sum(lax.all_to_all(product, "tensor", 0, 0), axis=0)
    products = [product] + [xor(product, k, "dp") for k in range(1, replicas)]

    (result,) = call(
        functools.partial(finish_kernel, replicas, peers, rank),
        "finish",
        [factor, *products, *leaves],
        [],
        [],
        [shape((rollout, own_width), BF16)],
        [pltpu.VMEM((rollout, own_width), BF16), pltpu.SemaphoreType.DMA(())],
        2 * rollout * own_width * 256,
        16,
    )
    return (result, *updated)


def solution(mesh):
    placed = (
        P("dp", "tensor"),
        P("dp", "tensor"),
        P("dp"),
        P("dp"),
        P("dp"),
        P(None, "tensor"),
        P(None, "tensor"),
        P(None, "tensor"),
        P(None, "tensor"),
        P(None, "tensor"),
        P(None, "tensor"),
        P("tensor", "dp"),
        P(None, "tensor"),
    )
    return jax.shard_map(
        shards,
        mesh=mesh,
        in_specs=placed,
        out_specs=(P(None, ("dp", "tensor")), *[P("dp", "tensor")] * 6),
        check_vma=False,
    )
```

profile of v0, /device:TPU:0, one launch (start us, length us, event | category | flops | bytes accessed | tf_op | source)
XLA Modules:
  0.0 146.1 jit_solution(9846684517372876376)
XLA Ops:
  0.7 7.4 %project.1 = (f32[8,32,128]{2,1,0:T(8,128)}, f32[8,256]{1,0:T(8,128)}) custom-call(s32[1,512]{1,0:T(1,128)} %bitcast.3, s32[1,512]{1,0:T(1,128)} %bitcast.5, s32[1,512]{1,0:T(1,128)} %bitcast.7, bf16[512,6656]{1,0:T(8,128)(2,1)} %refs_1_.4, f32[32,6656]{1,0:T(8,128)} %refs_6_.3, bf16[512,2048]{1,0:T(8,128)(2,1)} %refs_2_.4, f32[32,2048]{1,0:T(8,128)} %refs_9_.1), custom_call_target="tpu_custom_call" | custom-call | flops 2281701376 | bytes 10027008 | tf_op jit(solution)/shard_map/project/pallas_call | solution.py:77
  8.1 6.3 %all-to-all-start = ((f32[8,32,128]{2,1,0:T(8,128)}), f32[8,32,128]{2,1,0:T(8,128)S(1)}, u32[]{:S(2)}, u32[]{:S(2)}) async-start(f32[8,32,128]{2,1,0:T(8,128)} %get-tuple-element.31), calls=%async_computation | async-start | bytes 262144 | tf_op jit(solution)/shard_map/all_to_all | solution.py:376
  14.4 1.5 %collective-permute-start = (f32[8,256]{1,0:T(8,128)}, f32[8,256]{1,0:T(8,128)S(1)}, u32[]{:S(2)}, u32[]{:S(2)}) collective-permute-start(f32[8,256]{1,0:T(8,128)} %get-tuple-element.32.refs_4_), channel_id=1, source_target_pairs={{0,8},{8,0},{16,24},{24,16},{1,9},{9,1},{17,25},{25,17},{2,10},{10... | collective-permute-start | bytes 24584 | tf_op jit(solution)/shard_map/ppermute | solution.py:352
  15.9 1.5 %collective-permute-start.1 = (f32[8,256]{1,0:T(8,128)}, f32[8,256]{1,0:T(8,128)S(1)}, u32[]{:S(2)}, u32[]{:S(2)}) collective-permute-start(f32[8,256]{1,0:T(8,128)} %get-tuple-element.32.refs_4_), channel_id=1, source_target_pairs={{0,16},{8,24},{16,0},{24,8},{1,17},{9,25},{17,1},{25,9},{2,18},{10... | collective-permute-start | bytes 24584 | tf_op jit(solution)/shard_map/ppermute | solution.py:352
  17.4 0.5 collective-permute-start.2
  17.9 0.4 collective-permute-done.refs_5_
  18.3 1.5 %collective-permute-done.1.refs_6_ = f32[8,256]{1,0:T(8,128)S(1)} collective-permute-done((f32[8,256]{1,0:T(8,128)}, f32[8,256]{1,0:T(8,128)S(1)}, u32[]{:S(2)}, u32[]{:S(2)}) %collective-permute-start.1) | collective-permute-done | bytes 8224 | tf_op jit(solution)/shard_map/ppermute | solution.py:352
  19.8 2.4 %collective-permute-done.2.refs_7_ = f32[8,256]{1,0:T(8,128)S(1)} collective-permute-done((f32[8,256]{1,0:T(8,128)}, f32[8,256]{1,0:T(8,128)S(1)}, u32[]{:S(2)}, u32[]{:S(2)}) %collective-permute-start.2) | collective-permute-done | bytes 8224 | tf_op jit(solution)/shard_map/ppermute | solution.py:352
  22.2 0.0 all-to-all-done.refs_3_
  22.2 0.7 copy-done.21
  22.9 1.2 weigh.1.refs_2_
  24.1 2.9 %copy-done = bf16[512,6656]{1,0:T(8,128)(2,1)S(1)} copy-done((bf16[512,6656]{1,0:T(8,128)(2,1)S(1)}, bf16[512,6656]{1,0:T(8,128)(2,1)}, u32[]{:S(2)}) %copy-start) | copy-done | bytes 6815768
  27.1 13.6 %rollout3.1 = (bf16[512,512]{1,0:T(8,128)(2,1)}, f32[512,512]{1,0:T(8,128)S(1)}, bf16[512,512]{1,0:T(8,128)(2,1)S(1)}) custom-call(bf16[512,6656]{1,0:T(8,128)(2,1)S(1)} %copy-done, bf16[6656,4096]{1,0:T(8,128)(2,1)} %refs_2_.7, bf16[8,64,128]{2,1,0:T(8,128)(2,1)} %weigh.1.refs_2_), custom_call_target="tpu_custom_call" | custom-call | flops 10468982784 | bytes 54525952 | tf_op jit(solution)/shard_map/rollout3/pallas_call | solution.py:77
  40.6 0.1 collective-permute-start.3
  40.7 5.2 %all-to-all-start.1 = ((bf16[8,64,128]{2,1,0:T(8,128)(2,1)}), bf16[8,64,128]{2,1,0:T(8,128)(2,1)S(1)}, u32[]{:S(2)}, u32[]{:S(2)}) async-start(bf16[8,64,128]{2,1,0:T(8,128)(2,1)} %weigh.1.refs_2_), calls=%async_computation.1 | async-start | bytes 262144 | tf_op jit(solution)/shard_map/all_to_all | solution.py:389
  45.9 0.5 collective-permute-start.7
  46.4 6.3 %all-to-all-done.1.refs_2_.refs_0_ = bf16[8,64,128]{2,1,0:T(8,128)(2,1)S(1)} async-done(((bf16[8,64,128]{2,1,0:T(8,128)(2,1)}), bf16[8,64,128]{2,1,0:T(8,128)(2,1)S(1)}, u32[]{:S(2)}, u32[]{:S(2)}) %all-to-all-start.1) | async-done | bytes 131104 | tf_op jit(solution)/shard_map/all_to_all | solution.py:389
  52.7 0.0 collective-permute-done.3.refs_1_
  52.7 0.1 join.3.refs_3_
  52.8 0.0 copy-start.9
  52.8 1.0 collective-permute-start.8
  53.8 7.9 %gradient.1 = (f32[8,6656]{1,0:T(8,128)}, f32[32,2048]{1,0:T(8,128)}, bf16[16,7424]{1,0:T(8,128)(2,1)}, bf16[16,7424]{1,0:T(8,128)(2,1)}, bf16[16,7424]{1,0:T(8,128)(2,1)}) custom-call(bf16[8,64,128]{2,1,0:T(8,128)(2,1)} %copy-done.10, bf16[512,6656]{1,0:T(8,128)(2,1)} %refs_1_.4, bf16[512,2048]{1,0:T(8,128)(2,1)} %refs_2_.4, bf16[512,512]{1,0:T(8,128)(2,1)} %copy-done.9), custom_call_target="tpu_custom_call" | custom-call | flops 2281701376 | bytes 8912896 | tf_op jit(solution)/shard_map/gradient/pallas_call | solution.py:77
  61.7 0.6 collective-permute-start.4
  62.3 0.5 collective-permute-start.5
  62.8 2.4 %collective-permute-start.6 = (bf16[16,7424]{1,0:T(8,128)(2,1)}, bf16[16,7424]{1,0:T(8,128)(2,1)S(1)}, u32[]{:S(2)}, u32[]{:S(2)}) collective-permute-start(bf16[16,7424]{1,0:T(8,128)(2,1)} %get-tuple-element.39), channel_id=1, source_target_pairs={{0,24},{8,16},{16,8},{24,0},{1,25},{9,17},{17,9},{25,1},{2,26},{10... | collective-permute-start | bytes 712712 | tf_op jit(solution)/shard_map/ppermute | solution.py:352
  65.2 0.9 copy-done.12
  66.2 0.0 copy-start.15
  66.2 0.0 copy-start.16
  66.2 10.6 %rollout2.1 = (f32[512,512]{1,0:T(8,128)S(1)}, bf16[512,512]{1,0:T(8,128)(2,1)}, bf16[6656,256]{1,0:T(8,128)(2,1)S(1)}) custom-call(bf16[512,6656]{1,0:T(8,128)(2,1)S(1)} %copy-done.1, bf16[6656,4096]{1,0:T(8,128)(2,1)} %refs_2_.7, f32[8,6656]{1,0:T(8,128)S(1)} %copy-done.12), custom_call_target="tpu_custom_call" | custom-call | flops 6979321856 | bytes 54525952 | tf_op jit(solution)/shard_map/rollout2/pallas_call | solution.py:77
  76.9 1.7 %copy-done.5 = bf16[6656,256]{1,0:T(8,128)(2,1)} copy-done((bf16[6656,256]{1,0:T(8,128)(2,1)}, bf16[6656,256]{1,0:T(8,128)(2,1)S(1)}, u32[]{:S(2)}) %copy-start.5) | copy-done | bytes 3407896
  78.6 0.2 join.4.refs_12_.refs_3_
  78.9 4.7 %update.1 = (bf16[32,512]{1,0:T(8,128)(2,1)S(1)}, f32[8,8,512]{2,1,0:T(8,128)}, f32[8,6656]{1,0:T(8,128)}, f32[8,6656]{1,0:T(8,128)}, f32[8,6656]{1,0:T(8,128)},...) custom-call(f32[8,6656]{1,0:T(8,128)S(1)} %copy-done.12, f32[32,2048]{1,0:T(8,128)S(1)} %copy-done.17, ...), custom_call_target="tpu_custom_call" | custom-call | flops 1744830464 | bytes 4177920 | tf_op jit(solution)/shard_map/update/pallas_call | solution.py:77
  83.6 3.6 %all-to-all-start.2 = ((f32[8,8,512]{2,1,0:T(8,128)}), f32[8,8,512]{2,1,0:T(8,128)S(1)}, u32[]{:S(2)}, u32[]{:S(2)}) async-start(f32[8,8,512]{2,1,0:T(8,128)} %get-tuple-element.43.refs_4_), calls=%async_computation.2 | async-start | bytes 262144 | tf_op jit(solution)/shard_map/all_to_all | solution.py:490
  87.2 0.0 copy-start.2
  87.2 2.9 %copy-done.2 = bf16[512,6656]{1,0:T(8,128)(2,1)S(1)} copy-done((bf16[512,6656]{1,0:T(8,128)(2,1)S(1)}, bf16[512,6656]{1,0:T(8,128)(2,1)}, u32[]{:S(2)}) %copy-start.2) | copy-done | bytes 6815768
  90.1 2.0 %copy-done.6 = bf16[6656,256]{1,0:T(8,128)(2,1)S(1)} copy-done((bf16[6656,256]{1,0:T(8,128)(2,1)S(1)}, bf16[6656,256]{1,0:T(8,128)(2,1)}, u32[]{:S(2)}) %copy-start.6) | copy-done | bytes 3407896
  92.1 9.4 %rollout1.1 = (f32[512,512]{1,0:T(8,128)S(1)}, bf16[512,512]{1,0:T(8,128)(2,1)S(1)}, bf16[6656,256]{1,0:T(8,128)(2,1)S(1)}) custom-call(bf16[512,6656]{1,0:T(8,128)(2,1)S(1)} %copy-done.2, bf16[6656,256]{1,0:T(8,128)(2,1)S(1)} %copy-done.6, bf16[6656,4096]{1,0:T(8,128)(2,1)} %refs_2_.7, bf16[512,512]{1,0:T(8,128)(2,1)S(1)} %join.4.refs_12_.refs_3_, ...), custom_call_target="tpu_custom_call" | custom-call | flops 6979321856 | bytes 54525952 | tf_op jit(solution)/shard_map/rollout1/pallas_call | solution.py:77
  101.5 1.7 %copy-done.7 = bf16[6656,256]{1,0:T(8,128)(2,1)} copy-done((bf16[6656,256]{1,0:T(8,128)(2,1)}, bf16[6656,256]{1,0:T(8,128)(2,1)S(1)}, u32[]{:S(2)}) %copy-start.7) | copy-done | bytes 3407896
  103.2 0.1 join.5.refs_3_
  103.3 1.8 %collective-permute-start.15 = (bf16[512,512]{1,0:T(8,128)(2,1)S(1)}, bf16[512,512]{1,0:T(8,128)(2,1)S(1)}, u32[]{:S(2)}, u32[]{:S(2)}) collective-permute-start(bf16[512,512]{1,0:T(8,128)(2,1)S(1)} %join.5.refs_3_), channel_id=1, source_target_pairs={{0,2},{1,3},{2,0},{3,1},{4,6},{5,7},{6,4},{7,5},{8,10},{9,11},{10,... | collective-permute-start | bytes 1572872 | tf_op jit(solution)/shard_map/ppermute | solution.py:352
  105.1 2.4 %collective-permute-start.16 = (bf16[512,512]{1,0:T(8,128)(2,1)S(1)}, bf16[512,512]{1,0:T(8,128)(2,1)S(1)}, u32[]{:S(2)}, u32[]{:S(2)}) collective-permute-start(bf16[512,512]{1,0:T(8,128)(2,1)S(1)} %join.4.refs_12_.refs_3_), channel_id=1, source_target_pairs={{0,4},{1,5},{2,6},{3,7},{4,0},{5,1},{6,2},{7,3},{8,12},{9,13},{10,... | collective-permute-start | bytes 1572872 | tf_op jit(solution)/shard_map/ppermute | solution.py:352
  107.5 0.7 collective-permute-start.9
  108.2 3.2 %collective-permute-start.10 = (f32[8,512]{1,0:T(8,128)S(1)}, f32[8,512]{1,0:T(8,128)S(1)}, u32[]{:S(2)}, u32[]{:S(2)}) collective-permute-start(f32[8,512]{1,0:T(8,128)S(1)} %reduce_sum.9.refs_1_), channel_id=1, source_target_pairs={{0,8},{8,0},{16,24},{24,16},{1,9},{9,1},{17,25},{25,17},{2,10},{10... | collective-permute-start | bytes 49160 | tf_op jit(solution)/shard_map/ppermute | solution.py:352
  111.3 22.8 %collective-permute-start.11 = (f32[8,512]{1,0:T(8,128)S(1)}, f32[8,512]{1,0:T(8,128)S(1)}, u32[]{:S(2)}, u32[]{:S(2)}) collective-permute-start(f32[8,512]{1,0:T(8,128)S(1)} %reduce_sum.9.refs_1_), channel_id=1, source_target_pairs={{0,16},{8,24},{16,0},{24,8},{1,17},{9,25},{17,1},{25,9},{2,18},{10... | collective-permute-start | bytes 49160 | tf_op jit(solution)/shard_map/ppermute | solution.py:352
  134.1 2.9 %copy-done.3 = bf16[512,6656]{1,0:T(8,128)(2,1)S(1)} copy-done((bf16[512,6656]{1,0:T(8,128)(2,1)S(1)}, bf16[512,6656]{1,0:T(8,128)(2,1)}, u32[]{:S(2)}) %copy-start.3) | copy-done | bytes 6815768
  137.0 2.0 %copy-done.8 = bf16[6656,256]{1,0:T(8,128)(2,1)S(1)} copy-done((bf16[6656,256]{1,0:T(8,128)(2,1)S(1)}, bf16[6656,256]{1,0:T(8,128)(2,1)}, u32[]{:S(2)}) %copy-start.8) | copy-done | bytes 3407896
  139.0 5.6 %rollout0.1.refs_5_ = f32[512,512]{1,0:T(8,128)S(1)} custom-call(bf16[512,6656]{1,0:T(8,128)(2,1)S(1)} %copy-done.3, bf16[6656,256]{1,0:T(8,128)(2,1)S(1)} %copy-done.8, bf16[6656,4096]{1,0:T(8,128)(2,1)} %refs_2_.7, bf16[512,512]{1,0:T(8,128)(2,1)S(1)} %join.5.refs_3_, f32[8,8,512]{2,1,0:T(8,128)} %get-tuple-element.43.refs_4_), custom_call_target="tpu_custom_call" | custom-call | flops 3489660928 | bytes 54525952 | tf_op jit(solution)/shard_map/rollout0/pallas_call | solution.py:77
  144.6 1.3 finish.1
  (49 shorter events, 0.1 us)
Async XLA Ops:
  0.6 21.6 %copy-start.18 = (s32[512]{0:T(512)S(1)}, s32[512]{0:T(512)}, u32[]{:S(2)}) copy-start(s32[512]{0:T(512)} %param.15) | copy-start | bytes 6148
  0.6 21.6 %copy-start.19 = (s32[512]{0:T(512)S(1)}, s32[512]{0:T(512)}, u32[]{:S(2)}) copy-start(s32[512]{0:T(512)} %param.16) | copy-start | bytes 6148
  0.7 21.6 %copy-start.20 = (s32[512]{0:T(512)S(1)}, s32[512]{0:T(512)}, u32[]{:S(2)}) copy-start(s32[512]{0:T(512)} %param.17) | copy-start | bytes 6148
  8.1 14.1 %all-to-all-start = ((f32[8,32,128]{2,1,0:T(8,128)}), f32[8,32,128]{2,1,0:T(8,128)S(1)}, u32[]{:S(2)}, u32[]{:S(2)}) async-start(f32[8,32,128]{2,1,0:T(8,128)} %get-tuple-element.31), calls=%async_computation | async-start | bytes 262144 | tf_op jit(solution)/shard_map/all_to_all | solution.py:376
  14.4 3.9 %collective-permute-start = (f32[8,256]{1,0:T(8,128)}, f32[8,256]{1,0:T(8,128)S(1)}, u32[]{:S(2)}, u32[]{:S(2)}) collective-permute-start(f32[8,256]{1,0:T(8,128)} %get-tuple-element.32.refs_4_), channel_id=1, source_target_pairs={{0,8},{8,0},{16,24},{24,16},{1,9},{9,1},{17,25},{25,17},{2,10},{10... | collective-permute-start | bytes 24584 | tf_op jit(solution)/shard_map/ppermute | solution.py:352
  15.9 3.9 %collective-permute-start.1 = (f32[8,256]{1,0:T(8,128)}, f32[8,256]{1,0:T(8,128)S(1)}, u32[]{:S(2)}, u32[]{:S(2)}) collective-permute-start(f32[8,256]{1,0:T(8,128)} %get-tuple-element.32.refs_4_), channel_id=1, source_target_pairs={{0,16},{8,24},{16,0},{24,8},{1,17},{9,25},{17,1},{25,9},{2,18},{10... | collective-permute-start | bytes 24584 | tf_op jit(solution)/shard_map/ppermute | solution.py:352
  17.4 4.8 %collective-permute-start.2 = (f32[8,256]{1,0:T(8,128)}, f32[8,256]{1,0:T(8,128)S(1)}, u32[]{:S(2)}, u32[]{:S(2)}) collective-permute-start(f32[8,256]{1,0:T(8,128)} %get-tuple-element.32.refs_4_), channel_id=1, source_target_pairs={{0,24},{8,16},{16,8},{24,0},{1,25},{9,17},{17,9},{25,1},{2,26},{10... | collective-permute-start | bytes 24584 | tf_op jit(solution)/shard_map/ppermute | solution.py:352
  22.2 0.7 copy-start.21
  24.1 2.9 %copy-start = (bf16[512,6656]{1,0:T(8,128)(2,1)S(1)}, bf16[512,6656]{1,0:T(8,128)(2,1)}, u32[]{:S(2)}) copy-start(bf16[512,6656]{1,0:T(8,128)(2,1)} %refs_0_.7) | copy-start | bytes 20447236
  40.6 12.1 %collective-permute-start.3 = (bf16[512,512]{1,0:T(8,128)(2,1)}, bf16[512,512]{1,0:T(8,128)(2,1)S(1)}, u32[]{:S(2)}, u32[]{:S(2)}) collective-permute-start(bf16[512,512]{1,0:T(8,128)(2,1)} %get-tuple-element.34), channel_id=1, source_target_pairs={{0,1},{1,0},{2,3},{3,2},{4,5},{5,4},{6,7},{7,6},{8,9},{9,8},{10,11... | collective-permute-start | bytes 1572872 | tf_op jit(solution)/shard_map/ppermute | solution.py:352
  40.7 12.0 %all-to-all-start.1 = ((bf16[8,64,128]{2,1,0:T(8,128)(2,1)}), bf16[8,64,128]{2,1,0:T(8,128)(2,1)S(1)}, u32[]{:S(2)}, u32[]{:S(2)}) async-start(bf16[8,64,128]{2,1,0:T(8,128)(2,1)} %weigh.1.refs_2_), calls=%async_computation.1 | async-start | bytes 262144 | tf_op jit(solution)/shard_map/all_to_all | solution.py:389
  45.9 32.6 %collective-permute-start.7 = (bf16[512,512]{1,0:T(8,128)(2,1)S(1)}, bf16[512,512]{1,0:T(8,128)(2,1)S(1)}, u32[]{:S(2)}, u32[]{:S(2)}) collective-permute-start(bf16[512,512]{1,0:T(8,128)(2,1)S(1)} %get-tuple-element.41), channel_id=1, source_target_pairs={{0,1},{1,0},{2,3},{3,2},{4,5},{5,4},{6,7},{7,6},{8,9},{9,8},{10,11... | collective-permute-start | bytes 1572872 | tf_op jit(solution)/shard_map/ppermute | solution.py:352
  52.7 1.1 copy-start.10
  52.7 12.5 %copy-start.1 = (bf16[512,6656]{1,0:T(8,128)(2,1)S(1)}, bf16[512,6656]{1,0:T(8,128)(2,1)}, u32[]{:S(2)}) copy-start(bf16[512,6656]{1,0:T(8,128)(2,1)} %refs_0_.7) | copy-start | bytes 20447236
  52.8 1.0 copy-start.9
  52.8 25.8 %collective-permute-start.8 = (bf16[512,512]{1,0:T(8,128)(2,1)S(1)}, bf16[512,512]{1,0:T(8,128)(2,1)S(1)}, u32[]{:S(2)}, u32[]{:S(2)}) collective-permute-start(bf16[512,512]{1,0:T(8,128)(2,1)S(1)} %join.3.refs_3_), channel_id=1, source_target_pairs={{0,2},{1,3},{2,0},{3,1},{4,6},{5,7},{6,4},{7,5},{8,10},{9,11},{10,... | collective-permute-start | bytes 1572872 | tf_op jit(solution)/shard_map/ppermute | solution.py:352
  61.7 17.1 %collective-permute-start.4 = (bf16[16,7424]{1,0:T(8,128)(2,1)}, bf16[16,7424]{1,0:T(8,128)(2,1)S(1)}, u32[]{:S(2)}, u32[]{:S(2)}) collective-permute-start(bf16[16,7424]{1,0:T(8,128)(2,1)} %get-tuple-element.37), channel_id=1, source_target_pairs={{0,8},{8,0},{16,24},{24,16},{1,9},{9,1},{17,25},{25,17},{2,10},{10... | collective-permute-start | bytes 712712 | tf_op jit(solution)/shard_map/ppermute | solution.py:352
  62.3 16.5 %collective-permute-start.5 = (bf16[16,7424]{1,0:T(8,128)(2,1)}, bf16[16,7424]{1,0:T(8,128)(2,1)S(1)}, u32[]{:S(2)}, u32[]{:S(2)}) collective-permute-start(bf16[16,7424]{1,0:T(8,128)(2,1)} %get-tuple-element.38), channel_id=1, source_target_pairs={{0,16},{8,24},{16,0},{24,8},{1,17},{9,25},{17,1},{25,9},{2,18},{10... | collective-permute-start | bytes 712712 | tf_op jit(solution)/shard_map/ppermute | solution.py:352
  62.8 16.0 %collective-permute-start.6 = (bf16[16,7424]{1,0:T(8,128)(2,1)}, bf16[16,7424]{1,0:T(8,128)(2,1)S(1)}, u32[]{:S(2)}, u32[]{:S(2)}) collective-permute-start(bf16[16,7424]{1,0:T(8,128)(2,1)} %get-tuple-element.39), channel_id=1, source_target_pairs={{0,24},{8,16},{16,8},{24,0},{1,25},{9,17},{17,9},{25,1},{2,26},{10... | collective-permute-start | bytes 712712 | tf_op jit(solution)/shard_map/ppermute | solution.py:352
  65.2 0.9 copy-start.12
  66.2 12.6 %copy-start.4 = (f32[32,6656]{1,0:T(8,128)S(1)}, f32[32,6656]{1,0:T(8,128)}, u32[]{:S(2)}) copy-start(f32[32,6656]{1,0:T(8,128)} %refs_6_.3) | copy-start | bytes 2555908
  66.2 12.7 %copy-start.11 = (f32[32,2048]{1,0:T(8,128)S(1)}, f32[32,2048]{1,0:T(8,128)}, u32[]{:S(2)}) copy-start(f32[32,2048]{1,0:T(8,128)} %refs_9_.1) | copy-start | bytes 786436
  66.2 12.7 %copy-start.13 = (f32[32,6656]{1,0:T(8,128)S(1)}, f32[32,6656]{1,0:T(8,128)}, u32[]{:S(2)}) copy-start(f32[32,6656]{1,0:T(8,128)} %refs_7_.1) | copy-start | bytes 2555908
  66.2 12.7 %copy-start.14 = (f32[32,6656]{1,0:T(8,128)S(1)}, f32[32,6656]{1,0:T(8,128)}, u32[]{:S(2)}) copy-start(f32[32,6656]{1,0:T(8,128)} %refs_8_.1) | copy-start | bytes 2555908
  66.2 12.7 %copy-start.15 = (f32[32,2048]{1,0:T(8,128)S(1)}, f32[32,2048]{1,0:T(8,128)}, u32[]{:S(2)}) copy-start(f32[32,2048]{1,0:T(8,128)} %refs_10_.1) | copy-start | bytes 786436
  66.2 12.7 %copy-start.16 = (f32[32,2048]{1,0:T(8,128)S(1)}, f32[32,2048]{1,0:T(8,128)}, u32[]{:S(2)}) copy-start(f32[32,2048]{1,0:T(8,128)} %refs_11_.1) | copy-start | bytes 786436
  66.2 12.7 %copy-start.17 = (f32[32,2048]{1,0:T(8,128)S(1)}, f32[32,2048]{1,0:T(8,128)}, u32[]{:S(2)}) copy-start(f32[32,2048]{1,0:T(8,128)} %get-tuple-element.36.refs_1_) | copy-start | bytes 786436
  76.9 1.7 %copy-start.5 = (bf16[6656,256]{1,0:T(8,128)(2,1)}, bf16[6656,256]{1,0:T(8,128)(2,1)S(1)}, u32[]{:S(2)}) copy-start(bf16[6656,256]{1,0:T(8,128)(2,1)S(1)} %get-tuple-element.44.refs_1_) | copy-start | bytes 10223620
  78.6 24.7 %collective-permute-start.13 = (bf16[512,512]{1,0:T(8,128)(2,1)}, bf16[512,512]{1,0:T(8,128)(2,1)S(1)}, u32[]{:S(2)}, u32[]{:S(2)}) collective-permute-start(bf16[512,512]{1,0:T(8,128)(2,1)} %get-tuple-element.47), channel_id=1, source_target_pairs={{0,1},{1,0},{2,3},{3,2},{4,5},{5,4},{6,7},{7,6},{8,9},{9,8},{10,11... | collective-permute-start | bytes 1572872 | tf_op jit(solution)/shard_map/ppermute | solution.py:352
  83.6 24.6 %all-to-all-start.2 = ((f32[8,8,512]{2,1,0:T(8,128)}), f32[8,8,512]{2,1,0:T(8,128)S(1)}, u32[]{:S(2)}, u32[]{:S(2)}) async-start(f32[8,8,512]{2,1,0:T(8,128)} %get-tuple-element.43.refs_4_), calls=%async_computation.2 | async-start | bytes 262144 | tf_op jit(solution)/shard_map/all_to_all | solution.py:490
  87.2 2.9 %copy-start.2 = (bf16[512,6656]{1,0:T(8,128)(2,1)S(1)}, bf16[512,6656]{1,0:T(8,128)(2,1)}, u32[]{:S(2)}) copy-start(bf16[512,6656]{1,0:T(8,128)(2,1)} %refs_0_.7) | copy-start | bytes 20447236
  90.1 2.0 %copy-start.6 = (bf16[6656,256]{1,0:T(8,128)(2,1)S(1)}, bf16[6656,256]{1,0:T(8,128)(2,1)}, u32[]{:S(2)}) copy-start(bf16[6656,256]{1,0:T(8,128)(2,1)} %copy-done.5) | copy-start | bytes 10223620
  101.5 1.7 %copy-start.7 = (bf16[6656,256]{1,0:T(8,128)(2,1)}, bf16[6656,256]{1,0:T(8,128)(2,1)S(1)}, u32[]{:S(2)}) copy-start(bf16[6656,256]{1,0:T(8,128)(2,1)S(1)} %get-tuple-element.45.refs_1_) | copy-start | bytes 10223620
  103.3 41.3 %collective-permute-start.15 = (bf16[512,512]{1,0:T(8,128)(2,1)S(1)}, bf16[512,512]{1,0:T(8,128)(2,1)S(1)}, u32[]{:S(2)}, u32[]{:S(2)}) collective-permute-start(bf16[512,512]{1,0:T(8,128)(2,1)S(1)} %join.5.refs_3_), channel_id=1, source_target_pairs={{0,2},{1,3},{2,0},{3,1},{4,6},{5,7},{6,4},{7,5},{8,10},{9,11},{10,... | collective-permute-start | bytes 1572872 | tf_op jit(solution)/shard_map/ppermute | solution.py:352
  105.1 39.5 %collective-permute-start.14 = (bf16[512,512]{1,0:T(8,128)(2,1)S(1)}, bf16[512,512]{1,0:T(8,128)(2,1)S(1)}, u32[]{:S(2)}, u32[]{:S(2)}) collective-permute-start(bf16[512,512]{1,0:T(8,128)(2,1)S(1)} %get-tuple-element.48), channel_id=1, source_target_pairs={{0,1},{1,0},{2,3},{3,2},{4,5},{5,4},{6,7},{7,6},{8,9},{9,8},{10,11... | collective-permute-start | bytes 1572872 | tf_op jit(solution)/shard_map/ppermute | solution.py:352
  105.1 39.5 %collective-permute-start.16 = (bf16[512,512]{1,0:T(8,128)(2,1)S(1)}, bf16[512,512]{1,0:T(8,128)(2,1)S(1)}, u32[]{:S(2)}, u32[]{:S(2)}) collective-permute-start(bf16[512,512]{1,0:T(8,128)(2,1)S(1)} %join.4.refs_12_.refs_3_), channel_id=1, source_target_pairs={{0,4},{1,5},{2,6},{3,7},{4,0},{5,1},{6,2},{7,3},{8,12},{9,13},{10,... | collective-permute-start | bytes 1572872 | tf_op jit(solution)/shard_map/ppermute | solution.py:352
  107.5 3.9 %collective-permute-start.9 = (bf16[32,512]{1,0:T(8,128)(2,1)S(1)}, bf16[32,512]{1,0:T(8,128)(2,1)S(1)}, u32[]{:S(2)}, u32[]{:S(2)}) collective-permute-start(bf16[32,512]{1,0:T(8,128)(2,1)S(1)} %get-tuple-element.42), channel_id=1, source_target_pairs={{0,0},{1,4},{2,8},{3,12},{4,16},{5,20},{6,24},{7,28},{8,1},{9,5},{... | collective-permute-start | bytes 98312 | tf_op jit(solution)/shard_map/ppermute | solution.py:486
  108.2 25.9 %collective-permute-start.10 = (f32[8,512]{1,0:T(8,128)S(1)}, f32[8,512]{1,0:T(8,128)S(1)}, u32[]{:S(2)}, u32[]{:S(2)}) collective-permute-start(f32[8,512]{1,0:T(8,128)S(1)} %reduce_sum.9.refs_1_), channel_id=1, source_target_pairs={{0,8},{8,0},{16,24},{24,16},{1,9},{9,1},{17,25},{25,17},{2,10},{10... | collective-permute-start | bytes 49160 | tf_op jit(solution)/shard_map/ppermute | solution.py:352
  111.3 33.2 %collective-permute-start.11 = (f32[8,512]{1,0:T(8,128)S(1)}, f32[8,512]{1,0:T(8,128)S(1)}, u32[]{:S(2)}, u32[]{:S(2)}) collective-permute-start(f32[8,512]{1,0:T(8,128)S(1)} %reduce_sum.9.refs_1_), channel_id=1, source_target_pairs={{0,16},{8,24},{16,0},{24,8},{1,17},{9,25},{17,1},{25,9},{2,18},{10... | collective-permute-start | bytes 49160 | tf_op jit(solution)/shard_map/ppermute | solution.py:352
  134.1 10.5 %collective-permute-start.12 = (f32[8,512]{1,0:T(8,128)S(1)}, f32[8,512]{1,0:T(8,128)S(1)}, u32[]{:S(2)}, u32[]{:S(2)}) collective-permute-start(f32[8,512]{1,0:T(8,128)S(1)} %reduce_sum.9.refs_1_), channel_id=1, source_target_pairs={{0,24},{8,16},{16,8},{24,0},{1,25},{9,17},{17,9},{25,1},{2,26},{10... | collective-permute-start | bytes 49160 | tf_op jit(solution)/shard_map/ppermute | solution.py:352
  134.1 2.9 %copy-start.3 = (bf16[512,6656]{1,0:T(8,128)(2,1)S(1)}, bf16[512,6656]{1,0:T(8,128)(2,1)}, u32[]{:S(2)}) copy-start(bf16[512,6656]{1,0:T(8,128)(2,1)} %refs_0_.7) | copy-start | bytes 20447236
  137.0 2.0 %copy-start.8 = (bf16[6656,256]{1,0:T(8,128)(2,1)S(1)}, bf16[6656,256]{1,0:T(8,128)(2,1)}, u32[]{:S(2)}) copy-start(bf16[6656,256]{1,0:T(8,128)(2,1)} %copy-done.7) | copy-start | bytes 10223620
where the time goes:
time: 147 us; the launch traced here: 146 us
  Pallas kernels  62.1 us (42%)
  starting transfers between devices  54.5 us (37%)
  local copies, waits for them, and re-layouts  17.8 us (12%)
  waiting for transfers between devices  10.6 us (7%)
    pallas_call x12, Pallas kernels, call(): pl.pallas_call(body, name=name, out_shape=[*outputs, *far_outputs], in_sp...  62.1 us
    ppermute x16, starting transfers between devices, xor(): lax.ppermute(array, axis, [(i, i ^ k) for i in range(lax.axis_size(axis))])  38.7 us
    unnamed x44, local copies, waits for them, and re-layouts  17.8 us
    all_to_all x1, starting transfers between devices, shards(): pieces = lax.all_to_all(pieces, 'tensor', 0, 0)  6.33 us
    all_to_all x1, waiting for transfers between devices, shards(): shares = lax.all_to_all(share, 'tensor', 0, 0)  6.28 us
    all_to_all x1, starting transfers between devices, shards(): shares = lax.all_to_all(share, 'tensor', 0, 0)  5.2 us
    ppermute x16, waiting for transfers between devices, xor(): lax.ppermute(array, axis, [(i, i ^ k) for i in range(lax.axis_size(axis))])  4.31 us
    all_to_all x1, starting transfers between devices, shards(): product = jnp.sum(lax.all_to_all(product, 'tensor', 0, 0), axis=0)  3.6 us
  transfers between devices with their start and end apart: 20, of which 4 were waited for; matrix products, arithmetic and copies ran while one was open for 0% of the time, Pallas kernels for 26%

commit v1 on v0

v1 whole, which is shorter than its diff:
```python
import functools

import jax
import jax.numpy as jnp
from jax import lax
from jax.experimental import pallas as pl
from jax.experimental.pallas import tpu as pltpu
from jax.sharding import PartitionSpec as P

adapter_scale = 2.0
bias_one = 1.0 - 0.9**10
bias_two = 1.0 - 0.999**10

F32 = jnp.float32
BF16 = jnp.bfloat16
LANES = 128
MIB = 1 << 20


def dot(a, b):
    return jnp.dot(a, b, preferred_element_type=F32)


def dot_nt(a, b):
    length = a.shape[1]
    cut = length // 512 * 256
    if cut < 512:
        return dot_nt_part(a, b, 0, length)
    return dot_nt_part(a, b, 0, cut) + dot_nt_part(a, b, cut, length)


def dot_nt_part(a, b, first, last):
    dims = (((1,), (1,)), ((), ()))
    return lax.dot_general(a[:, first:last], b[:, first:last], dims, preferred_element_type=F32)


def adaptive_moment_step(param, grad, first, second):
    first = 0.9 * first + 0.1 * grad
    second = 0.999 * second + 0.001 * grad * grad
    param = param - 0.004 * (first / bias_one) / (jnp.sqrt(second / bias_two) + 1e-08)
    return (param, first, second)


def tile_of(length, limit):
    units = length // LANES
    return LANES * max(u for u in range(1, limit // LANES + 1) if units % u == 0)


def split_bf16(value):
    high = value.astype(BF16)
    return high, (value - high.astype(F32)).astype(BF16)


def pick(index, choices):
    result = choices[0]
    for at in range(1, len(choices)):
        result = jnp.where(index == at, choices[at], result)
    return result


def shape(dims, kind):
    return jax.ShapeDtypeStruct(dims, kind)


ANY = pl.BlockSpec(memory_space=pl.ANY)
HBM = pl.BlockSpec(memory_space=pltpu.HBM)
VMEM = pl.BlockSpec(memory_space=pltpu.VMEM)


def call(kernel, name, held, far, outputs, far_outputs, scratch, flops, vmem, after=()):
    first = len(held) + len(far)
    moved = sum(a.size * a.dtype.itemsize for a in [*far, *far_outputs])

    def body(*refs):
        kernel(*refs[:first], *refs[first + len(after) :])

    return pl.pallas_call(
        body,
        name=name,
        out_shape=[*outputs, *far_outputs],
        in_specs=[VMEM] * len(held) + [HBM] * len(far) + [ANY] * len(after),
        out_specs=[VMEM] * len(outputs) + [HBM] * len(far_outputs),
        scratch_shapes=scratch,
        compiler_params=pltpu.CompilerParams(vmem_limit_bytes=vmem * MIB),
        cost_estimate=pl.CostEstimate(flops=flops, bytes_accessed=moved, transcendentals=0),
    )(*held, *far, *after)


def in_turn(fetches, ahead=2):
    for fetch in fetches[:ahead]:
        fetch.start()
    done = []

    def arrive():
        fetches[len(done)].wait()
        done.append(True)
        if len(done) - 1 + ahead < len(fetches):
            fetches[len(done) - 1 + ahead].start()

    return arrive


def project_kernel(index, mask, order, far_hidden, far_a, far_cot, far_b, far_x, *rest):
    packed, stats, hidden, cot, x, a, b, arrived = rest
    rank = a.shape[0]
    inner = hidden.shape[1]
    chunks = arrived.shape[0] - 4
    width = inner // chunks
    pairs = [(far_a, a)]
    for at in range(chunks):
        columns = slice(at * width, (at + 1) * width)
        pairs.append((far_hidden.at[:, columns], hidden.at[:, columns]))
    pairs += [(far_cot, cot), (far_b, b), (far_x, x)]
    fetches = [pltpu.make_async_copy(*pair, arrived.at[at]) for at, pair in enumerate(pairs)]
    arrive = in_turn(fetches, 3)
    arrive()
    left = a[...].astype(BF16)
    total = None
    for at in range(chunks):
        arrive()
        columns = slice(at * width, (at + 1) * width)
        product = dot_nt(hidden.at[:, columns], left[:, columns])
        total = product if total is None else total + product
    arrive()
    arrive()
    high, low = split_bf16(b[...])
    both = dot_nt(cot, jnp.concatenate([high, low], axis=0))
    both = jnp.concatenate([total, both[:, :rank] + both[:, rank:]], axis=1)
    half = both.shape[0] // 2
    packed[...] = jnp.concatenate([both[:half], both[half:]], axis=1)
    groups, tokens = stats.shape[1], index.shape[1]
    member = (lax.broadcasted_iota(jnp.int32, (groups, tokens), 0) == index[...]).astype(F32)
    row = lax.broadcasted_iota(jnp.int32, (8, tokens), 0)
    values = jnp.where(row == 0, mask[...], 0)
    values = jnp.where(row == 1, mask[...] * order[...], values)
    values = jnp.where(row == 2, mask[...] * order[...] * order[...], values)
    stats[...] = dot_nt(values.astype(F32).astype(BF16), member.astype(BF16))
    arrive()


def gradient_kernel(replicas, rank, all_index, all_mask, all_order, packed, arrived, hidden, cot, *rest):
    stats, (own_a, own_b, *sent) = rest[:replicas], rest[replicas:-2]
    column, grad = rest[-2:]
    rows = rank // replicas
    me = lax.axis_index("dp")
    tokens, inner = hidden.shape
    groups = stats[0].shape[1]
    half = inner // 2
    sums = stats[0][...]
    for other in stats[1:]:
        sums = sums + other[...]
    counts, firsts, squares = sums[0:1, :], sums[1:2, :], sums[2:3, :]
    safe = jnp.maximum(counts, 1.0)
    mean = firsts / safe
    spread = jnp.maximum(jnp.sqrt(jnp.maximum(squares / safe - mean * mean, 0.0)), 1.0)
    total = jnp.maximum(jnp.sum(counts, axis=1, keepdims=True), 1.0)

    row = lax.broadcasted_iota(jnp.int32, (LANES, tokens), 0)
    tall = jnp.where(row == 0, all_index[...], 0)
    tall = jnp.where(row == 1, all_mask[...], tall)
    tall = jnp.where(row == 2, all_order[...], tall)
    column[...] = jnp.transpose(tall.astype(F32))
    index, mask, order = column[:, 0:1], column[:, 1:2], column[:, 2:3]
    member = index == lax.broadcasted_iota(jnp.int32, (tokens, groups), 1).astype(F32)
    own_mean = jnp.sum(jnp.where(member, mean, 0.0), axis=1, keepdims=True)
    own_spread = jnp.sum(jnp.where(member, spread, 0.0), axis=1, keepdims=True)
    coefficient = -mask * (order - own_mean) / own_spread / total

    both = packed[...] + arrived[...]
    both = jnp.concatenate([both[:, : 2 * rank], both[:, 2 * rank : 4 * rank]], axis=0)
    both = both * coefficient
    back = both[:, rank:].astype(BF16).astype(F32)
    high, low = split_bf16(both[:, :rank])
    empty = jnp.zeros((tokens, LANES - 3 * rank), F32)
    tall = jnp.concatenate([back, high.astype(F32), low.astype(F32), empty], axis=1)
    wide = jnp.transpose(tall).astype(BF16)
    grad[...] = adapter_scale * dot(wide[0:rank, :], hidden[...])
    both = dot(wide[rank : 3 * rank, :], cot[...])
    whole = adapter_scale * (both[:rank] + both[rank:])
    pieces = [grad[j * rows : (j + 1) * rows, :] for j in range(replicas)]
    own_a[...] = pick(me, pieces)
    own_b[...] = whole
    folded = [whole[at : at + 2 * rows] for at in range(0, rank, 2 * rows)]
    folded = jnp.concatenate(folded, axis=1).astype(BF16)
    for k in range(1, replicas):
        piece = pick(lax.bitwise_xor(me, k), pieces)
        halves = jnp.concatenate([piece[:, :half], piece[:, half:]], axis=0)
        sent[k - 1][:, 0:half] = halves.astype(BF16)
        sent[k - 1][:, half:] = folded


def update_kernel(replicas, own_a, own_b, x, *rest):
    received, rest = rest[: replicas - 1], rest[replicas - 1 :]
    factors, (sent, out), results = rest[:6], rest[6:8], rest[8:14]
    (a, am, av, b, bm, bv), made, arrived, left = rest[14:20], rest[20:26], rest[26], rest[27]
    rows, inner = a.shape
    rank, columns = b.shape
    me = lax.axis_index("dp")

    def fetch(at):
        source = factors[at]
        if at < 3 and source.shape[0] != rows:
            source = source.at[pl.ds(pl.multiple_of(me * rows, rows), rows), :]
        return pltpu.make_async_copy(source, (a, am, av, b, bm, bv)[at], arrived.at[at])

    def keep(at):
        return pltpu.make_async_copy(made[at], results[at], arrived.at[at])

    for at in range(6):
        fetch(at).start()
    grad_a, grad_b = own_a[...], own_b[...]
    half = inner // 2
    for other in received:
        folded = other[...].astype(F32)
        grad_a = grad_a + jnp.concatenate([folded[:rows, :half], folded[rows:, :half]], axis=1)
        parts = [folded[:, at : at + columns] for at in range(half, folded.shape[1], columns)]
        grad_b = grad_b + jnp.concatenate(parts, axis=0)
    for at in range(6):
        fetch(at).wait()
    made[0][...], made[1][...], made[2][...] = adaptive_moment_step(a[...], grad_a, am[...], av[...])
    padding = jnp.zeros((left.shape[0] - rows, inner), F32)
    left[...] = jnp.concatenate([made[0][...], padding], axis=0).astype(BF16)
    next_b, first_b, second_b = adaptive_moment_step(b[...], grad_b, bm[...], bv[...])
    for array, result in zip((next_b, first_b, second_b), made[3:]):
        result[...] = pick(me, [array[j * rows : (j + 1) * rows] for j in range(replicas)])
    for at in range(6):
        keep(at).start()
    width = columns // replicas
    choices = [next_b[:, j * width : (j + 1) * width] for j in range(replicas)]
    sent[...] = pick(me, choices).astype(BF16)
    product = dot_nt(x, left)
    empty = jnp.zeros((product.shape[0], LANES - left.shape[0]), F32)
    out[...] = jnp.transpose(jnp.concatenate([product, empty], axis=1))[0:rows, :]
    for at in range(6):
        keep(at).wait()


def rollout_kernel(differs, following, first, x, *rest):
    if following is None:
        given, out = rest
    elif first:
        w, out, after, given, arrived = rest
    else:
        given, w, out, after, arrived = rest
    me = lax.axis_index("tensor")
    width = out.shape[1]

    def fetch(differs, held, at):
        start = pl.multiple_of(lax.bitwise_xor(me, differs) * width, width)
        return pltpu.make_async_copy(w.at[:, pl.ds(start, width)], held, arrived.at[at])

    if first:
        own = fetch(differs, given, 0)
        own.start()
        own.wait()
    if following is not None:
        next_one = fetch(following, after, 1)
        next_one.start()
    out[...] = dot(x[...], given[...]).astype(out.dtype)
    if following is not None:
        next_one.wait()


def gather_kernel(bit, mine, arrived, out):
    later = lax.bitwise_and(lax.shift_right_logical(lax.axis_index("dp"), bit), 1) == 1
    first = jnp.where(later, arrived[...], mine[...])
    out[...] = jnp.concatenate([first, jnp.where(later, mine[...], arrived[...])], axis=0)


def join_kernel(*refs):
    total = refs[0][...].astype(F32)
    for leaf in refs[1:-1]:
        total = total + leaf[...].astype(F32)
    refs[-1][...] = total.astype(refs[-1].dtype)


def finish_kernel(rank, factor, mine, arrived, *rest):
    leaves, (out, made, kept) = rest[:-3], rest[-3:]
    high, low = split_bf16(mine[...] + arrived[...])
    empty = jnp.zeros((LANES - 2 * rank, high.shape[1]), F32)
    wide = jnp.concatenate([high.astype(F32), low.astype(F32), empty], axis=0)
    tall = jnp.transpose(wide).astype(BF16)
    empty = jnp.zeros((LANES - 2 * rank, factor.shape[1]), BF16)
    total = adapter_scale * dot(tall, jnp.concatenate([factor[...], factor[...], empty], axis=0))
    for leaf in leaves:
        total = total + leaf[...].astype(F32)
    made[...] = total.astype(BF16)
    copy = pltpu.make_async_copy(made, out, kept)
    copy.start()
    copy.wait()


def shards(
    hidden,
    cotangent,
    prompt_group_index,
    answer_token_mask,
    token_reward_order,
    source_lowdim_matrix,
    running_mean_source_matrix,
    running_variance_source_matrix,
    target_lowdim_matrix,
    running_mean_target_matrix,
    running_variance_target_matrix,
    frozen_down_weight,
    sampled_token_input,
):
    replicas, peers = lax.axis_size("dp"), lax.axis_size("tensor")
    me_dp = lax.axis_index("dp")
    x, w = sampled_token_input, frozen_down_weight
    tokens, inner = hidden.shape
    columns = cotangent.shape[1]
    rank = source_lowdim_matrix.shape[0]
    rows = rank // replicas
    groups = tokens * replicas // 8
    rollout = x.shape[0]
    own_width = w.shape[1] // peers
    deep = tile_of(inner, 1664)

    def xor(array, k, axis="tensor"):
        return lax.ppermute(array, axis, [(i, i ^ k) for i in range(lax.axis_size(axis))])

    def add(arrays, after=()):
        (total,) = call(
            join_kernel, "join", arrays, [], [shape(arrays[0].shape, arrays[-1].dtype)], [], [], 0, 8, after
        )
        return total

    chips = peers // 2
    todo = [(m, other) for m in range(chips - 1, -1, -1) for other in (1, 0)]
    crossed, arrived, own, waiting, handed = {}, {}, {}, [], None

    def form(eighths, after):
        nonlocal handed
        for _ in range(eighths * len(todo_all) // 8):
            m, other = todo.pop(0)
            following = 2 * todo[0][0] + todo[0][1] if todo else None
            result = shape((rollout, own_width), BF16 if other else F32)
            block = shape((inner, own_width), BF16)
            held = [x_held] if handed is None else [x_held, handed]
            scratch = [pltpu.VMEM(block.shape, BF16)] if handed is None else []
            scratch += [pltpu.SemaphoreType.DMA((2,))] if following is not None else []
            result, *handed = call(
                functools.partial(rollout_kernel, 2 * m + other, following, handed is None),
                "rollout%d%d" % (m, other),
                held,
                [w] if following is not None else [],
                [result] + ([block] if following is not None else []),
                [],
                scratch,
                2 * rollout * inner * own_width,
                20,
                after,
            )
            handed = handed[0] if handed else None
            if other:
                crossed[m] = xor(result, 1)
            else:
                own[m] = result
                waiting.append(m)
            after = [result]
        return after

    def leaves_of(m):
        bits = [1 << at for at in range(chips.bit_length() - 1)]
        lower = [bit for bit in bits if not m or bit < m & -m]
        return [own[m], crossed[m], *[arrived[m | bit] for bit in lower]]

    def send_on(after):
        while waiting:
            m = waiting.pop(0)
            total = add(leaves_of(m), after)
            arrived[m] = xor(total, 2 * (m & -m))
            after = [total]
        return after

    todo_all = list(todo)

    tok = [
        array.reshape(1, tokens) for array in (prompt_group_index, answer_token_mask, token_reward_order)
    ]
    packed, stats, hidden_held, cot_held, x_held = call(
        project_kernel,
        "project",
        tok,
        [hidden, source_lowdim_matrix, cotangent, target_lowdim_matrix, x],
        [
            shape((tokens // 2, LANES), F32),
            shape((8, groups), F32),
            shape(hidden.shape, BF16),
            shape(cotangent.shape, BF16),
            shape(x.shape, BF16),
        ],
        [],
        [
            pltpu.VMEM((rank, inner), F32),
            pltpu.VMEM((rank, columns), F32),
            pltpu.SemaphoreType.DMA((inner // deep + 4,)),
        ],
        2 * tokens * (inner + columns) * 256,
        45,
    )
    all_stats = [stats] + [xor(stats, k, "dp") for k in range(1, replicas)]
    tensor_bits = [1 << at for at in range(peers.bit_length() - 1)]
    received = xor(packed, tensor_bits[0])
    after = form(1, [packed])
    for bit in tensor_bits[1:]:
        packed = add([packed, received], after)
        received = xor(packed, bit)
        after = form(1, [packed]) if bit in (2, 4) else [packed]
    after = send_on(after)

    own_a, own_b, *sent = call(
        functools.partial(gradient_kernel, replicas, rank),
        "gradient",
        [*tok, packed, received, hidden_held, cot_held, *all_stats],
        [],
        [shape((rows, inner), F32), shape((rank, columns), F32)]
        + [shape((2 * rows, inner // 2 + columns * replicas // 2), BF16)] * (replicas - 1),
        [],
        [pltpu.VMEM((tokens, LANES), F32), pltpu.VMEM((rank, inner), F32)],
        2 * tokens * (inner + columns) * 256,
        16,
        after,
    )
    received = [xor(array, k + 1, "dp") for k, array in enumerate(sent)]
    after = form(1, send_on(form(1, [own_a])))

    left = [source_lowdim_matrix, running_mean_source_matrix, running_variance_source_matrix]
    right = [target_lowdim_matrix, running_mean_target_matrix, running_variance_target_matrix]
    if rows % 8:
        left = [lax.dynamic_slice_in_dim(array, me_dp * rows, rows, 0) for array in left]
    own_left, own_right = shape((rows, inner), F32), shape((rows, columns), F32)
    sent_b, product, *updated = call(
        functools.partial(update_kernel, replicas),
        "update",
        [own_a, own_b, x_held, *received],
        [*left, *right],
        [shape((rank, columns // replicas), BF16), shape((rows, rollout), F32)],
        [own_left] * 3 + [own_right] * 3,
        [pltpu.VMEM((rows, inner), F32)] * 3
        + [pltpu.VMEM((rank, columns), F32)] * 3
        + [pltpu.VMEM((rows, inner), F32)] * 3
        + [pltpu.VMEM((rows, columns), F32)] * 3
        + [pltpu.SemaphoreType.DMA((6,)), pltpu.VMEM((16, inner), BF16)],
        2 * rollout * inner * 256,
        24,
        after,
    )
    pairs = [(dp * peers + at, at * replicas + dp) for dp in range(replicas) for at in range(peers)]
    factor = lax.ppermute(sent_b, ("dp", "tensor"), pairs)
    after = [product]
    for at in range(replicas.bit_length() - 1):
        received = xor(product, 1 << at, "dp")
        if at < 2:
            after = form(1, after) if todo else after
        both = shape((2 * product.shape[0], rollout), F32)
        (product,) = call(
            functools.partial(gather_kernel, at), "gather", [product, received], [], [both], [], [], 0, 8, after
        )
        after = [product]
        if at < 1:
            after = send_on(after)
    for at, bit in enumerate(tensor_bits):
        received = xor(product, bit)
        if at == 0 and todo:
            after = form(len(todo) * 8 // len(todo_all), after)
        if at < len(tensor_bits) - 1:
            product = add([product, received], after + [factor] * (at == len(tensor_bits) - 2))
            after = [product]
    send_on_last = [m for m in waiting if m]
    waiting[:] = send_on_last
    send_on(after)

    (result,) = call(
        functools.partial(finish_kernel, rank),
        "finish",
        [factor, product, received, *leaves_of(0)],
        [],
        [],
        [shape((rollout, own_width), BF16)],
        [pltpu.VMEM((rollout, own_width), BF16), pltpu.SemaphoreType.DMA(())],
        2 * rollout * own_width * 256,
        16,
    )
    return (result, *updated)


def solution(mesh):
    placed = (
        P("dp", "tensor"),
        P("dp", "tensor"),
        P("dp"),
        P("dp"),
        P("dp"),
        P(None, "tensor"),
        P(None, "tensor"),
        P(None, "tensor"),
        P(None, "tensor"),
        P(None, "tensor"),
        P(None, "tensor"),
        P("tensor", "dp"),
        P(None, "tensor"),
    )
    return jax.shard_map(
        shards,
        mesh=mesh,
        in_specs=placed,
        out_specs=(P(None, ("dp", "tensor")), *[P("dp", "tensor")] * 6),
        check_vma=False,
    )
```

time: 147 us -> 115 us (0.78)
  starting transfers between devices: 54.5 us -> 21.6 us
  local copies, waits for them, and re-layouts: 17.8 us -> 8.73 us
  waiting for transfers between devices: 10.6 us -> 19 us
  Pallas kernels: 62.1 us -> 64.1 us
    ppermute x16 -> x21, starting transfers between devices: 38.7 us -> 21 us  [xor(): lax.ppermute(array, axis, [(i, i ^ k) for i in range(lax.axis_size(axis))])]
    all_to_all x3 -> x0, starting transfers between devices: 15.1 us -> none  [the longest x1 6.33 us: shards(): pieces = lax.all_to_all(pieces, 'tensor', 0, 0)]
    ppermute x16 -> x21, waiting for transfers between devices: 4.31 us -> 19 us  [xor(): lax.ppermute(array, axis, [(i, i ^ k) for i in range(lax.axis_size(axis))])]
    unnamed x44 -> x38, local copies, waits for them, and re-layouts: 17.8 us -> 8.73 us
    all_to_all x3 -> x0, waiting for transfers between devices: 6.28 us -> none  [the longest x1 6.28 us: shards(): shares = lax.all_to_all(share, 'tensor', 0, 0)]
    pallas_call x12 -> x21, Pallas kernels: 62.1 us -> 64.1 us  [call(): pl.pallas_call(body, name=name, out_shape=[*outputs, *far_outputs], in_sp...]
  transfers between devices with their start and end apart: 20 -> 22, of which waited for: 4 -> 4; matrix products, arithmetic and copies ran while one was open for 0% -> 0% of each run, Pallas kernels for 26% -> 44%
where the time goes in v1:
time: 115 us
  Pallas kernels  64.1 us (56%)
  starting transfers between devices  21.6 us (19%)
  waiting for transfers between devices  19 us (17%)
  local copies, waits for them, and re-layouts  8.73 us (8%)
  between operations  1.21 us (1%)
    pallas_call x21, Pallas kernels, call(): pl.pallas_call(body, name=name, out_shape=[*outputs, *far_outputs], in_sp...  64.1 us
    ppermute x21, starting transfers between devices, xor(): lax.ppermute(array, axis, [(i, i ^ k) for i in range(lax.axis_size(axis))])  21 us
    ppermute x21, waiting for transfers between devices, xor(): lax.ppermute(array, axis, [(i, i ^ k) for i in range(lax.axis_size(axis))])  19 us
    unnamed x38, local copies, waits for them, and re-layouts  8.73 us
  transfers between devices with their start and end apart: 22, of which 4 were waited for; matrix products, arithmetic and copies ran while one was open for 0% of the time, Pallas kernels for 44%

profile of v1, /device:TPU:0, one launch (start us, length us, event | category | flops | bytes accessed | tf_op | source)
XLA Modules:
  0.0 114.7 jit_solution(16923171295904282015)
XLA Ops:
  0.6 0.0 copy-start.2
  0.6 1.1 %copy-done.2 = f32[32,6656]{1,0:T(8,128)S(1)} copy-done((f32[32,6656]{1,0:T(8,128)S(1)}, f32[32,6656]{1,0:T(8,128)}, u32[]{:S(2)}) %copy-start.2) | copy-done | bytes 851992
  1.8 1.6 %copy-done.4 = bf16[512,2048]{1,0:T(8,128)(2,1)S(1)} copy-done((bf16[512,2048]{1,0:T(8,128)(2,1)S(1)}, bf16[512,2048]{1,0:T(8,128)(2,1)}, u32[]{:S(2)}) %copy-start.4) | copy-done | bytes 2097176
  3.4 0.9 copy-done.5
  4.3 0.7 copy-done.11
  5.0 0.7 copy-done.13
  5.7 0.7 copy-done.15
  6.4 11.9 %project.1 = (f32[256,128]{1,0:T(8,128)S(1)}, f32[8,256]{1,0:T(8,128)S(1)}, bf16[512,6656]{1,0:T(8,128)(2,1)}, bf16[512,2048]{1,0:T(8,128)(2,1)S(1)}, bf16[512,6656]{1,0:T(8,128)(2,1)}) custom-call(s32[1,512]{1,0:T(1,128)S(1)} %bitcast.5, s32[1,512]{1,0:T(1,128)S(1)} %bitcast.7, s32[1,512]{1,0:T(1,128)S(1)} %bitcast.9, bf16[512,6656]{1,0:T(8,128)(2,1)} %refs_3_.1, ...), custom_call_target="tpu_custom_call" | custom-call | flops 2281701376 | bytes 16842752 | tf_op jit(solution)/shard_map/project/pallas_call | solution.py:77
  18.2 3.0 %collective-permute-start.3 = (f32[8,256]{1,0:T(8,128)S(1)}, f32[8,256]{1,0:T(8,128)S(1)}, u32[]{:S(2)}, u32[]{:S(2)}) collective-permute-start(f32[8,256]{1,0:T(8,128)S(1)} %get-tuple-element.46.refs_7_), channel_id=1, source_target_pairs={{0,8},{8,0},{16,24},{24,16},{1,9},{9,1},{17,25},{25,17},{2,10},{10... | collective-permute-start | bytes 24584 | tf_op jit(solution)/shard_map/ppermute | solution.py:321
  21.2 1.5 %collective-permute-start.4 = (f32[8,256]{1,0:T(8,128)S(1)}, f32[8,256]{1,0:T(8,128)S(1)}, u32[]{:S(2)}, u32[]{:S(2)}) collective-permute-start(f32[8,256]{1,0:T(8,128)S(1)} %get-tuple-element.46.refs_7_), channel_id=1, source_target_pairs={{0,16},{8,24},{16,0},{24,8},{1,17},{9,25},{17,1},{25,9},{2,18},{10... | collective-permute-start | bytes 24584 | tf_op jit(solution)/shard_map/ppermute | solution.py:321
  22.8 0.0 collective-permute-start.5
  22.8 2.9 %copy-done = bf16[512,6656]{1,0:T(8,128)(2,1)S(1)} copy-done((bf16[512,6656]{1,0:T(8,128)(2,1)S(1)}, bf16[512,6656]{1,0:T(8,128)(2,1)}, u32[]{:S(2)}) %copy-start) | copy-done | bytes 6815768
  25.7 6.8 %rollout31.1 = (bf16[512,512]{1,0:T(8,128)(2,1)S(1)}, bf16[6656,512]{1,0:T(8,128)(2,1)S(1)}) custom-call(bf16[512,6656]{1,0:T(8,128)(2,1)S(1)} %copy-done, bf16[6656,4096]{1,0:T(8,128)(2,1)} %refs_2_.11, f32[256,128]{1,0:T(8,128)S(1)} %get-tuple-element.39.refs_2_.refs_0_), custom_call_target="tpu_custom_call" | custom-call | flops 3489660928 | bytes 54525952 | tf_op jit(solution)/shard_map/rollout31/pallas_call | solution.py:77
  32.5 0.6 collective-permute-start.6
  33.1 2.1 %collective-permute-start.1 = (f32[256,128]{1,0:T(8,128)S(1)}, f32[256,128]{1,0:T(8,128)S(1)}, u32[]{:S(2)}, u32[]{:S(2)}) collective-permute-start(f32[256,128]{1,0:T(8,128)S(1)} %join.7.refs_3_.refs_0_), channel_id=1, source_target_pairs={{0,2},{1,3},{2,0},{3,1},{4,6},{5,7},{6,4},{7,5},{8,10},{9,11},{10,... | collective-permute-start | bytes 393224 | tf_op jit(solution)/shard_map/ppermute | solution.py:321
  35.2 6.5 %rollout30.1 = (f32[512,512]{1,0:T(8,128)S(1)}, bf16[6656,512]{1,0:T(8,128)(2,1)S(1)}) custom-call(bf16[512,6656]{1,0:T(8,128)(2,1)S(1)} %copy-done.1, bf16[6656,512]{1,0:T(8,128)(2,1)S(1)} %get-tuple-element.42.refs_1_, bf16[6656,4096]{1,0:T(8,128)(2,1)} %refs_2_.11, f32[256,128]{1,0:T(8,128)S(1)} %join.7.refs_3_.refs_0_), custom_call_target="tpu_custom_call" | custom-call | flops 3489660928 | bytes 54525952 | tf_op jit(solution)/shard_map/rollout30/pallas_call | solution.py:77
  41.7 2.7 %collective-permute-start.2 = (f32[256,128]{1,0:T(8,128)S(1)}, f32[256,128]{1,0:T(8,128)S(1)}, u32[]{:S(2)}, u32[]{:S(2)}) collective-permute-start(f32[256,128]{1,0:T(8,128)S(1)} %join.8.refs_3_), channel_id=1, source_target_pairs={{0,4},{1,5},{2,6},{3,7},{4,0},{5,1},{6,2},{7,3},{8,12},{9,13},{10,... | collective-permute-start | bytes 393224 | tf_op jit(solution)/shard_map/ppermute | solution.py:321
  44.4 3.7 %rollout21.1 = (bf16[512,512]{1,0:T(8,128)(2,1)S(1)}, bf16[6656,512]{1,0:T(8,128)(2,1)S(1)}) custom-call(bf16[512,6656]{1,0:T(8,128)(2,1)S(1)} %copy-done.1, bf16[6656,512]{1,0:T(8,128)(2,1)S(1)} %get-tuple-element.47.refs_1_, bf16[6656,4096]{1,0:T(8,128)(2,1)} %refs_2_.11, f32[256,128]{1,0:T(8,128)S(1)} %join.8.refs_3_), custom_call_target="tpu_custom_call" | custom-call | flops 3489660928 | bytes 54525952 | tf_op jit(solution)/shard_map/rollout21/pallas_call | solution.py:77
  48.1 0.1 collective-permute-start.10
  48.2 0.1 join.9.refs_11_
  48.3 0.5 collective-permute-start.11
  48.8 1.7 %collective-permute-done.2.refs_4_ = f32[256,128]{1,0:T(8,128)S(1)} collective-permute-done((f32[256,128]{1,0:T(8,128)S(1)}, f32[256,128]{1,0:T(8,128)S(1)}, u32[]{:S(2)}, u32[]{:S(2)}) %collective-permute-start.2) | collective-permute-done | bytes 131104 | tf_op jit(solution)/shard_map/ppermute | solution.py:321
  50.5 2.9 %gradient.1 = (f32[8,6656]{1,0:T(8,128)S(1)}, f32[32,2048]{1,0:T(8,128)S(1)}, bf16[16,7424]{1,0:T(8,128)(2,1)S(1)}, bf16[16,7424]{1,0:T(8,128)(2,1)S(1)}, bf16[16,7424]{1,0:T(8,128)(2,1)S(1)}) custom-call(s32[1,512]{1,0:T(1,128)S(1)} %bitcast.6, s32[1,512]{1,0:T(1,128)S(1)} %bitcast.8, s32[1,512]{1,0:T(1,128)S(1)} %bitcast.10, f32[256,128]{1,0:T(8,128)S(1)} %join.8.refs_3_, ...), custom_call_target="tpu_custom_call" | custom-call | flops 2281701376 | tf_op jit(solution)/shard_map/gradient/pallas_call | solution.py:77
  53.4 1.6 %collective-permute-start.7 = (bf16[16,7424]{1,0:T(8,128)(2,1)S(1)}, bf16[16,7424]{1,0:T(8,128)(2,1)S(1)}, u32[]{:S(2)}, u32[]{:S(2)}) collective-permute-start(bf16[16,7424]{1,0:T(8,128)(2,1)S(1)} %get-tuple-element.51), channel_id=1, source_target_pairs={{0,8},{8,0},{16,24},{24,16},{1,9},{9,1},{17,25},{25,17},{2,10},{10... | collective-permute-start | bytes 712712 | tf_op jit(solution)/shard_map/ppermute | solution.py:321
  55.0 1.5 %collective-permute-start.8 = (bf16[16,7424]{1,0:T(8,128)(2,1)S(1)}, bf16[16,7424]{1,0:T(8,128)(2,1)S(1)}, u32[]{:S(2)}, u32[]{:S(2)}) collective-permute-start(bf16[16,7424]{1,0:T(8,128)(2,1)S(1)} %get-tuple-element.52), channel_id=1, source_target_pairs={{0,16},{8,24},{16,0},{24,8},{1,17},{9,25},{17,1},{25,9},{2,18},{10... | collective-permute-start | bytes 712712 | tf_op jit(solution)/shard_map/ppermute | solution.py:321
  56.5 0.4 collective-permute-start.9
  56.9 6.5 %rollout20.1 = (f32[512,512]{1,0:T(8,128)S(1)}, bf16[6656,512]{1,0:T(8,128)(2,1)S(1)}) custom-call(bf16[512,6656]{1,0:T(8,128)(2,1)S(1)} %copy-done.1, bf16[6656,512]{1,0:T(8,128)(2,1)S(1)} %get-tuple-element.54.refs_1_, bf16[6656,4096]{1,0:T(8,128)(2,1)} %refs_2_.11, f32[8,6656]{1,0:T(8,128)S(1)} %get-tuple-element.49.refs_3_.refs_0_), custom_call_target="tpu_custom_call" | custom-call | flops 3489660928 | bytes 54525952 | tf_op jit(solution)/shard_map/rollout20/pallas_call | solution.py:77
  63.4 0.2 join.10.refs_3_
  63.6 3.9 %rollout11.1 = (bf16[512,512]{1,0:T(8,128)(2,1)S(1)}, bf16[6656,512]{1,0:T(8,128)(2,1)S(1)}) custom-call(bf16[512,6656]{1,0:T(8,128)(2,1)S(1)} %copy-done.1, bf16[6656,512]{1,0:T(8,128)(2,1)S(1)} %get-tuple-element.55.refs_1_, bf16[6656,4096]{1,0:T(8,128)(2,1)} %refs_2_.11, bf16[512,512]{1,0:T(8,128)(2,1)S(1)} %join.10.refs_3_), custom_call_target="tpu_custom_call" | custom-call | flops 3489660928 | bytes 54525952 | tf_op jit(solution)/shard_map/rollout11/pallas_call | solution.py:77
  67.5 0.1 collective-permute-start.15
  67.6 0.1 collective-permute-start.21
  67.8 4.0 %update.1 = (bf16[32,512]{1,0:T(8,128)(2,1)S(1)}, f32[8,512]{1,0:T(8,128)S(1)}, f32[8,6656]{1,0:T(8,128)}, f32[8,6656]{1,0:T(8,128)}, f32[8,6656]{1,0:T(8,128)},...) custom-call(f32[8,6656]{1,0:T(8,128)S(1)} %get-tuple-element.49.refs_3_.refs_0_, ...), custom_call_target="tpu_custom_call" | custom-call | flops 1744830464 | bytes 4177920 | tf_op jit(solution)/shard_map/update/pallas_call | solution.py:77
  71.8 1.6 %collective-permute-start.13 = (f32[8,512]{1,0:T(8,128)S(1)}, f32[8,512]{1,0:T(8,128)S(1)}, u32[]{:S(2)}, u32[]{:S(2)}) collective-permute-start(f32[8,512]{1,0:T(8,128)S(1)} %get-tuple-element.59.refs_3_.refs_0_), channel_id=1, source_target_pairs={{0,8},{8,0},{16,24},{24,16},{1,9},{9,1},{17,25},{25,17},{2,10},{10... | collective-permute-start | bytes 49160 | tf_op jit(solution)/shard_map/ppermute | solution.py:321
  73.4 6.5 %rollout10.1 = (f32[512,512]{1,0:T(8,128)S(1)}, bf16[6656,512]{1,0:T(8,128)(2,1)S(1)}) custom-call(bf16[512,6656]{1,0:T(8,128)(2,1)S(1)} %copy-done.1, bf16[6656,512]{1,0:T(8,128)(2,1)S(1)} %get-tuple-element.60.refs_1_, bf16[6656,4096]{1,0:T(8,128)(2,1)} %refs_2_.11, f32[8,512]{1,0:T(8,128)S(1)} %get-tuple-element.59.refs_3_.refs_0_), custom_call_target="tpu_custom_call" | custom-call | flops 3489660928 | bytes 54525952 | tf_op jit(solution)/shard_map/rollout10/pallas_call | solution.py:77
  79.9 0.1 join.11.refs_3_
  80.0 6.3 %rollout01.1 = (bf16[512,512]{1,0:T(8,128)(2,1)S(1)}, bf16[6656,512]{1,0:T(8,128)(2,1)S(1)}) custom-call(bf16[512,6656]{1,0:T(8,128)(2,1)S(1)} %copy-done.1, bf16[6656,512]{1,0:T(8,128)(2,1)S(1)} %get-tuple-element.62.refs_1_, bf16[6656,4096]{1,0:T(8,128)(2,1)} %refs_2_.11, bf16[512,512]{1,0:T(8,128)(2,1)S(1)} %join.11.refs_3_), custom_call_target="tpu_custom_call" | custom-call | flops 3489660928 | bytes 54525952 | tf_op jit(solution)/shard_map/rollout01/pallas_call | solution.py:77
  86.3 0.2 collective-permute-start.19
  86.5 3.1 %collective-permute-start.20 = (bf16[512,512]{1,0:T(8,128)(2,1)S(1)}, bf16[512,512]{1,0:T(8,128)(2,1)S(1)}, u32[]{:S(2)}, u32[]{:S(2)}) collective-permute-start(bf16[512,512]{1,0:T(8,128)(2,1)S(1)} %join.11.refs_3_), channel_id=1, source_target_pairs={{0,2},{1,3},{2,0},{3,1},{4,6},{5,7},{6,4},{7,5},{8,10},{9,11},{10,... | collective-permute-start | bytes 1572872 | tf_op jit(solution)/shard_map/ppermute | solution.py:321
  89.6 1.5 %collective-permute-start.14 = (f32[16,512]{1,0:T(8,128)S(1)}, f32[16,512]{1,0:T(8,128)S(1)}, u32[]{:S(2)}, u32[]{:S(2)}) collective-permute-start(f32[16,512]{1,0:T(8,128)S(1)} %gather.2.refs_2_.refs_0_), channel_id=1, source_target_pairs={{0,16},{8,24},{16,0},{24,8},{1,17},{9,25},{17,1},{25,9},{2,18},{10... | collective-permute-start | bytes 98312 | tf_op jit(solution)/shard_map/ppermute | solution.py:321
  91.1 2.4 %collective-permute-done.14.refs_1_ = f32[16,512]{1,0:T(8,128)S(1)} collective-permute-done((f32[16,512]{1,0:T(8,128)S(1)}, f32[16,512]{1,0:T(8,128)S(1)}, u32[]{:S(2)}, u32[]{:S(2)}) %collective-permute-start.14) | collective-permute-done | bytes 32800 | tf_op jit(solution)/shard_map/ppermute | solution.py:321
  93.5 0.1 collective-permute-start.16
  93.6 3.7 %rollout00.1.refs_2_.refs_3_ = f32[512,512]{1,0:T(8,128)S(1)} custom-call(bf16[512,6656]{1,0:T(8,128)(2,1)S(1)} %copy-done.1, bf16[6656,512]{1,0:T(8,128)(2,1)S(1)} %get-tuple-element.64.refs_1_, f32[32,512]{1,0:T(8,128)S(1)} %gather.3.refs_2_.refs_0_), custom_call_target="tpu_custom_call" | custom-call | flops 3489660928 | tf_op jit(solution)/shard_map/rollout00/pallas_call | solution.py:77
  97.3 0.1 collective-permute-start.17
  97.5 0.7 collective-permute-start.12
  98.1 9.3 %collective-permute-done.17.refs_1_ = f32[32,512]{1,0:T(8,128)S(1)} collective-permute-done((f32[32,512]{1,0:T(8,128)S(1)}, f32[32,512]{1,0:T(8,128)S(1)}, u32[]{:S(2)}, u32[]{:S(2)}) %collective-permute-start.17) | collective-permute-done | bytes 65568 | tf_op jit(solution)/shard_map/ppermute | solution.py:321
  107.4 0.1 collective-permute-start.18
  107.5 5.7 %collective-permute-done.18.refs_2_ = f32[32,512]{1,0:T(8,128)S(1)} collective-permute-done((f32[32,512]{1,0:T(8,128)S(1)}, f32[32,512]{1,0:T(8,128)S(1)}, u32[]{:S(2)}, u32[]{:S(2)}) %collective-permute-start.18) | collective-permute-done | bytes 65568 | tf_op jit(solution)/shard_map/ppermute | solution.py:321
  113.2 1.3 %finish.1 = bf16[512,512]{1,0:T(8,128)(2,1)} custom-call(bf16[32,512]{1,0:T(8,128)(2,1)S(1)} %collective-permute-done.12.refs_3_.refs_0_, f32[32,512]{1,0:T(8,128)S(1)} %join.13.refs_1_, f32[32,512]{1,0:T(8,128)S(1)} %collective-permute-done.18.refs_2_, f32[512,512]{1,0:T(8,128)S(1)} %rollout00.1.refs_2_.refs_3_, ...), custom_call_target="tpu_custom_call" | custom-call | flops 134217728 | bytes 524288 | tf_op jit(solution)/shard_map/finish/pallas_call | solution.py:77
  (56 shorter events, 0.2 us)
Async XLA Ops:
  0.6 1.2 %copy-start.2 = (f32[32,6656]{1,0:T(8,128)S(1)}, f32[32,6656]{1,0:T(8,128)}, u32[]{:S(2)}) copy-start(f32[32,6656]{1,0:T(8,128)} %refs_6_.3) | copy-start | bytes 2555908
  1.8 1.6 %copy-start.4 = (bf16[512,2048]{1,0:T(8,128)(2,1)S(1)}, bf16[512,2048]{1,0:T(8,128)(2,1)}, u32[]{:S(2)}) copy-start(bf16[512,2048]{1,0:T(8,128)(2,1)} %refs_5_.1) | copy-start | bytes 6291460
  3.4 0.9 copy-start.5
  4.3 0.7 copy-start.11
  5.0 0.7 copy-start.13
  5.7 0.7 copy-start.15
  18.2 30.0 %collective-permute-start.3 = (f32[8,256]{1,0:T(8,128)S(1)}, f32[8,256]{1,0:T(8,128)S(1)}, u32[]{:S(2)}, u32[]{:S(2)}) collective-permute-start(f32[8,256]{1,0:T(8,128)S(1)} %get-tuple-element.46.refs_7_), channel_id=1, source_target_pairs={{0,8},{8,0},{16,24},{24,16},{1,9},{9,1},{17,25},{25,17},{2,10},{10... | collective-permute-start | bytes 24584 | tf_op jit(solution)/shard_map/ppermute | solution.py:321
  21.2 27.5 %collective-permute-start.4 = (f32[8,256]{1,0:T(8,128)S(1)}, f32[8,256]{1,0:T(8,128)S(1)}, u32[]{:S(2)}, u32[]{:S(2)}) collective-permute-start(f32[8,256]{1,0:T(8,128)S(1)} %get-tuple-element.46.refs_7_), channel_id=1, source_target_pairs={{0,16},{8,24},{16,0},{24,8},{1,17},{9,25},{17,1},{25,9},{2,18},{10... | collective-permute-start | bytes 24584 | tf_op jit(solution)/shard_map/ppermute | solution.py:321
  22.8 26.0 %collective-permute-start.5 = (f32[8,256]{1,0:T(8,128)S(1)}, f32[8,256]{1,0:T(8,128)S(1)}, u32[]{:S(2)}, u32[]{:S(2)}) collective-permute-start(f32[8,256]{1,0:T(8,128)S(1)} %get-tuple-element.46.refs_7_), channel_id=1, source_target_pairs={{0,24},{8,16},{16,8},{24,0},{1,25},{9,17},{17,9},{25,1},{2,26},{10... | collective-permute-start | bytes 24584 | tf_op jit(solution)/shard_map/ppermute | solution.py:321
  22.8 10.3 %collective-permute-start = (f32[256,128]{1,0:T(8,128)S(1)}, f32[256,128]{1,0:T(8,128)S(1)}, u32[]{:S(2)}, u32[]{:S(2)}) collective-permute-start(f32[256,128]{1,0:T(8,128)S(1)} %get-tuple-element.39.refs_2_.refs_0_), channel_id=1, source_target_pairs={{0,1},{1,0},{2,3},{3,2},{4,5},{5,4},{6,7},{7,6},{8,9},{9,8},{10,11... | collective-permute-start | bytes 393224 | tf_op jit(solution)/shard_map/ppermute | solution.py:321
  22.8 2.9 %copy-start = (bf16[512,6656]{1,0:T(8,128)(2,1)S(1)}, bf16[512,6656]{1,0:T(8,128)(2,1)}, u32[]{:S(2)}) copy-start(bf16[512,6656]{1,0:T(8,128)(2,1)} %get-tuple-element.40.refs_0_.refs_2_) | copy-start | bytes 20447236
  25.7 9.5 %copy-start.1 = (bf16[512,6656]{1,0:T(8,128)(2,1)S(1)}, bf16[512,6656]{1,0:T(8,128)(2,1)}, u32[]{:S(2)}) copy-start(bf16[512,6656]{1,0:T(8,128)(2,1)} %get-tuple-element.40.refs_0_.refs_2_) | copy-start | bytes 20447236
  32.5 15.6 %collective-permute-start.6 = (bf16[512,512]{1,0:T(8,128)(2,1)S(1)}, bf16[512,512]{1,0:T(8,128)(2,1)S(1)}, u32[]{:S(2)}, u32[]{:S(2)}) collective-permute-start(bf16[512,512]{1,0:T(8,128)(2,1)S(1)} %get-tuple-element.41.refs_2_), channel_id=1, source_target_pairs={{0,1},{1,0},{2,3},{3,2},{4,5},{5,4},{6,7},{7,6},{8,9},{9,8},{10,11... | collective-permute-start | bytes 1572872 | tf_op jit(solution)/shard_map/ppermute | solution.py:321
  33.1 8.6 %collective-permute-start.1 = (f32[256,128]{1,0:T(8,128)S(1)}, f32[256,128]{1,0:T(8,128)S(1)}, u32[]{:S(2)}, u32[]{:S(2)}) collective-permute-start(f32[256,128]{1,0:T(8,128)S(1)} %join.7.refs_3_.refs_0_), channel_id=1, source_target_pairs={{0,2},{1,3},{2,0},{3,1},{4,6},{5,7},{6,4},{7,5},{8,10},{9,11},{10,... | collective-permute-start | bytes 393224 | tf_op jit(solution)/shard_map/ppermute | solution.py:321
  35.2 15.3 %slice-start = ((s8[6815744]{0:T(1024)(128)(4,1)}), s8[4194304]{0:T(1024)(128)(4,1)S(1)}, s32[]{:S(2)}) async-start(s8[6815744]{0:T(1024)(128)(4,1)} %bitcast.3), calls=%async_computation | async-start | bytes 8388608
  41.7 8.8 %collective-permute-start.2 = (f32[256,128]{1,0:T(8,128)S(1)}, f32[256,128]{1,0:T(8,128)S(1)}, u32[]{:S(2)}, u32[]{:S(2)}) collective-permute-start(f32[256,128]{1,0:T(8,128)S(1)} %join.8.refs_3_), channel_id=1, source_target_pairs={{0,4},{1,5},{2,6},{3,7},{4,0},{5,1},{6,2},{7,3},{8,12},{9,13},{10,... | collective-permute-start | bytes 393224 | tf_op jit(solution)/shard_map/ppermute | solution.py:321
  44.3 6.1 %slice-start.1 = ((s8[6815744]{0:T(1024)(128)(4,1)}), s8[2621440]{0:T(1024)(128)(4,1)S(1)}, s32[]{:S(2)}) async-start(s8[6815744]{0:T(1024)(128)(4,1)} %bitcast.3), calls=%async_computation.1 | async-start | bytes 5242880
  44.4 6.1 %copy-start.12 = (s32[512]{0:T(512)S(1)}, s32[512]{0:T(512)}, u32[]{:S(2)}) copy-start(s32[512]{0:T(512)} %param.15) | copy-start | bytes 6148
  44.4 6.1 %copy-start.14 = (s32[512]{0:T(512)S(1)}, s32[512]{0:T(512)}, u32[]{:S(2)}) copy-start(s32[512]{0:T(512)} %param.16) | copy-start | bytes 6148
  44.4 6.1 %copy-start.16 = (s32[512]{0:T(512)S(1)}, s32[512]{0:T(512)}, u32[]{:S(2)}) copy-start(s32[512]{0:T(512)} %param.17) | copy-start | bytes 6148
  48.1 15.3 %collective-permute-start.10 = (bf16[512,512]{1,0:T(8,128)(2,1)S(1)}, bf16[512,512]{1,0:T(8,128)(2,1)S(1)}, u32[]{:S(2)}, u32[]{:S(2)}) collective-permute-start(bf16[512,512]{1,0:T(8,128)(2,1)S(1)} %get-tuple-element.48.refs_2_), channel_id=1, source_target_pairs={{0,1},{1,0},{2,3},{3,2},{4,5},{5,4},{6,7},{7,6},{8,9},{9,8},{10,11... | collective-permute-start | bytes 1572872 | tf_op jit(solution)/shard_map/ppermute | solution.py:321
  48.3 15.1 %collective-permute-start.11 = (bf16[512,512]{1,0:T(8,128)(2,1)S(1)}, bf16[512,512]{1,0:T(8,128)(2,1)S(1)}, u32[]{:S(2)}, u32[]{:S(2)}) collective-permute-start(bf16[512,512]{1,0:T(8,128)(2,1)S(1)} %join.9.refs_11_), channel_id=1, source_target_pairs={{0,2},{1,3},{2,0},{3,1},{4,6},{5,7},{6,4},{7,5},{8,10},{9,11},{10,... | collective-permute-start | bytes 1572872 | tf_op jit(solution)/shard_map/ppermute | solution.py:321
  53.4 14.3 %collective-permute-start.7 = (bf16[16,7424]{1,0:T(8,128)(2,1)S(1)}, bf16[16,7424]{1,0:T(8,128)(2,1)S(1)}, u32[]{:S(2)}, u32[]{:S(2)}) collective-permute-start(bf16[16,7424]{1,0:T(8,128)(2,1)S(1)} %get-tuple-element.51), channel_id=1, source_target_pairs={{0,8},{8,0},{16,24},{24,16},{1,9},{9,1},{17,25},{25,17},{2,10},{10... | collective-permute-start | bytes 712712 | tf_op jit(solution)/shard_map/ppermute | solution.py:321
  55.0 12.7 %collective-permute-start.8 = (bf16[16,7424]{1,0:T(8,128)(2,1)S(1)}, bf16[16,7424]{1,0:T(8,128)(2,1)S(1)}, u32[]{:S(2)}, u32[]{:S(2)}) collective-permute-start(bf16[16,7424]{1,0:T(8,128)(2,1)S(1)} %get-tuple-element.52), channel_id=1, source_target_pairs={{0,16},{8,24},{16,0},{24,8},{1,17},{9,25},{17,1},{25,9},{2,18},{10... | collective-permute-start | bytes 712712 | tf_op jit(solution)/shard_map/ppermute | solution.py:321
  56.5 11.2 %collective-permute-start.9 = (bf16[16,7424]{1,0:T(8,128)(2,1)S(1)}, bf16[16,7424]{1,0:T(8,128)(2,1)S(1)}, u32[]{:S(2)}, u32[]{:S(2)}) collective-permute-start(bf16[16,7424]{1,0:T(8,128)(2,1)S(1)} %get-tuple-element.53), channel_id=1, source_target_pairs={{0,24},{8,16},{16,8},{24,0},{1,25},{9,17},{17,9},{25,1},{2,26},{10... | collective-permute-start | bytes 712712 | tf_op jit(solution)/shard_map/ppermute | solution.py:321
  63.6 4.1 %copy-start.3 = (f32[32,6656]{1,0:T(8,128)S(1)}, f32[32,6656]{1,0:T(8,128)}, u32[]{:S(2)}) copy-start(f32[32,6656]{1,0:T(8,128)} %refs_6_.3) | copy-start | bytes 2555908
  63.6 4.1 %copy-start.6 = (f32[32,2048]{1,0:T(8,128)S(1)}, f32[32,2048]{1,0:T(8,128)}, u32[]{:S(2)}) copy-start(f32[32,2048]{1,0:T(8,128)} %refs_9_.1) | copy-start | bytes 786436
  63.6 4.1 %copy-start.7 = (f32[32,6656]{1,0:T(8,128)S(1)}, f32[32,6656]{1,0:T(8,128)}, u32[]{:S(2)}) copy-start(f32[32,6656]{1,0:T(8,128)} %refs_7_.3) | copy-start | bytes 2555908
  63.6 4.1 %copy-start.8 = (f32[32,6656]{1,0:T(8,128)S(1)}, f32[32,6656]{1,0:T(8,128)}, u32[]{:S(2)}) copy-start(f32[32,6656]{1,0:T(8,128)} %refs_8_.1) | copy-start | bytes 2555908
  63.6 4.1 %copy-start.9 = (f32[32,2048]{1,0:T(8,128)S(1)}, f32[32,2048]{1,0:T(8,128)}, u32[]{:S(2)}) copy-start(f32[32,2048]{1,0:T(8,128)} %refs_10_.1) | copy-start | bytes 786436
  63.6 4.1 %copy-start.10 = (f32[32,2048]{1,0:T(8,128)S(1)}, f32[32,2048]{1,0:T(8,128)}, u32[]{:S(2)}) copy-start(f32[32,2048]{1,0:T(8,128)} %refs_11_.1) | copy-start | bytes 786436
  67.5 12.4 %collective-permute-start.15 = (bf16[512,512]{1,0:T(8,128)(2,1)S(1)}, bf16[512,512]{1,0:T(8,128)(2,1)S(1)}, u32[]{:S(2)}, u32[]{:S(2)}) collective-permute-start(bf16[512,512]{1,0:T(8,128)(2,1)S(1)} %get-tuple-element.57.refs_12_), channel_id=1, source_target_pairs={{0,1},{1,0},{2,3},{3,2},{4,5},{5,4},{6,7},{7,6},{8,9},{9,8},{10,11... | collective-permute-start | bytes 1572872 | tf_op jit(solution)/shard_map/ppermute | solution.py:321
  67.6 39.9 %collective-permute-start.21 = (bf16[512,512]{1,0:T(8,128)(2,1)S(1)}, bf16[512,512]{1,0:T(8,128)(2,1)S(1)}, u32[]{:S(2)}, u32[]{:S(2)}) collective-permute-start(bf16[512,512]{1,0:T(8,128)(2,1)S(1)} %join.10.refs_3_), channel_id=1, source_target_pairs={{0,4},{1,5},{2,6},{3,7},{4,0},{5,1},{6,2},{7,3},{8,12},{9,13},{10,... | collective-permute-start | bytes 1572872 | tf_op jit(solution)/shard_map/ppermute | solution.py:321
  71.8 8.1 %collective-permute-start.13 = (f32[8,512]{1,0:T(8,128)S(1)}, f32[8,512]{1,0:T(8,128)S(1)}, u32[]{:S(2)}, u32[]{:S(2)}) collective-permute-start(f32[8,512]{1,0:T(8,128)S(1)} %get-tuple-element.59.refs_3_.refs_0_), channel_id=1, source_target_pairs={{0,8},{8,0},{16,24},{24,16},{1,9},{9,1},{17,25},{25,17},{2,10},{10... | collective-permute-start | bytes 49160 | tf_op jit(solution)/shard_map/ppermute | solution.py:321
  86.3 26.9 %collective-permute-start.19 = (bf16[512,512]{1,0:T(8,128)(2,1)S(1)}, bf16[512,512]{1,0:T(8,128)(2,1)S(1)}, u32[]{:S(2)}, u32[]{:S(2)}) collective-permute-start(bf16[512,512]{1,0:T(8,128)(2,1)S(1)} %get-tuple-element.63.refs_2_), channel_id=1, source_target_pairs={{0,1},{1,0},{2,3},{3,2},{4,5},{5,4},{6,7},{7,6},{8,9},{9,8},{10,11... | collective-permute-start | bytes 1572872 | tf_op jit(solution)/shard_map/ppermute | solution.py:321
  86.5 26.7 %collective-permute-start.20 = (bf16[512,512]{1,0:T(8,128)(2,1)S(1)}, bf16[512,512]{1,0:T(8,128)(2,1)S(1)}, u32[]{:S(2)}, u32[]{:S(2)}) collective-permute-start(bf16[512,512]{1,0:T(8,128)(2,1)S(1)} %join.11.refs_3_), channel_id=1, source_target_pairs={{0,2},{1,3},{2,0},{3,1},{4,6},{5,7},{6,4},{7,5},{8,10},{9,11},{10,... | collective-permute-start | bytes 1572872 | tf_op jit(solution)/shard_map/ppermute | solution.py:321
  89.6 3.9 %collective-permute-start.14 = (f32[16,512]{1,0:T(8,128)S(1)}, f32[16,512]{1,0:T(8,128)S(1)}, u32[]{:S(2)}, u32[]{:S(2)}) collective-permute-start(f32[16,512]{1,0:T(8,128)S(1)} %gather.2.refs_2_.refs_0_), channel_id=1, source_target_pairs={{0,16},{8,24},{16,0},{24,8},{1,17},{9,25},{17,1},{25,9},{2,18},{10... | collective-permute-start | bytes 98312 | tf_op jit(solution)/shard_map/ppermute | solution.py:321
  93.5 3.8 %collective-permute-start.16 = (f32[32,512]{1,0:T(8,128)S(1)}, f32[32,512]{1,0:T(8,128)S(1)}, u32[]{:S(2)}, u32[]{:S(2)}) collective-permute-start(f32[32,512]{1,0:T(8,128)S(1)} %gather.3.refs_2_.refs_0_), channel_id=1, source_target_pairs={{0,1},{1,0},{2,3},{3,2},{4,5},{5,4},{6,7},{7,6},{8,9},{9,8},{10,11... | collective-permute-start | bytes 196616 | tf_op jit(solution)/shard_map/ppermute | solution.py:321
  97.3 10.1 %collective-permute-start.17 = (f32[32,512]{1,0:T(8,128)S(1)}, f32[32,512]{1,0:T(8,128)S(1)}, u32[]{:S(2)}, u32[]{:S(2)}) collective-permute-start(f32[32,512]{1,0:T(8,128)S(1)} %join.12.refs_0_.refs_2_), channel_id=1, source_target_pairs={{0,2},{1,3},{2,0},{3,1},{4,6},{5,7},{6,4},{7,5},{8,10},{9,11},{10,... | collective-permute-start | bytes 196616 | tf_op jit(solution)/shard_map/ppermute | solution.py:321
  97.5 0.7 collective-permute-start.12
  107.4 5.8 %collective-permute-start.18 = (f32[32,512]{1,0:T(8,128)S(1)}, f32[32,512]{1,0:T(8,128)S(1)}, u32[]{:S(2)}, u32[]{:S(2)}) collective-permute-start(f32[32,512]{1,0:T(8,128)S(1)} %join.13.refs_1_), channel_id=1, source_target_pairs={{0,4},{1,5},{2,6},{3,7},{4,0},{5,1},{6,2},{7,3},{8,12},{9,13},{10,... | collective-permute-start | bytes 196616 | tf_op jit(solution)/shard_map/ppermute | solution.py:321

commit v2 on v1

--- a/solution.py
+++ b/solution.py
@@ -81,7 +81,7 @@
         in_specs=[VMEM] * len(held) + [HBM] * len(far) + [ANY] * len(after),
         out_specs=[VMEM] * len(outputs) + [HBM] * len(far_outputs),
         scratch_shapes=scratch,
-        compiler_params=pltpu.CompilerParams(vmem_limit_bytes=vmem * MIB),
+        compiler_params=pltpu.CompilerParams(vmem_limit_bytes=int(vmem * MIB)),
         cost_estimate=pl.CostEstimate(flops=flops, bytes_accessed=moved, transcendentals=0),
     )(*held, *far, *after)
 
@@ -100,20 +100,24 @@
     return arrive
 
 
-def project_kernel(index, mask, order, far_hidden, far_a, far_cot, far_b, far_x, *rest):
-    packed, stats, hidden, cot, x, a, b, arrived = rest
+def project_kernel(differs, *rest):
+    far_tok, (far_hidden, far_a, far_cot, far_b, far_x, w) = rest[:3], rest[3:9]
+    packed, stats, tok, hidden, cot, x, block, index, mask, order, a, b, arrived = rest[9:]
     rank = a.shape[0]
     inner = hidden.shape[1]
-    chunks = arrived.shape[0] - 4
+    chunks = arrived.shape[0] - 8
     width = inner // chunks
-    pairs = [(far_a, a)]
+    start = lax.bitwise_xor(lax.axis_index("tensor"), differs) * block.shape[1]
+    first = w.at[:, pl.ds(pl.multiple_of(start, block.shape[1]), block.shape[1])]
+    pairs = [*zip(far_tok, (index, mask, order)), (far_a, a)]
     for at in range(chunks):
         columns = slice(at * width, (at + 1) * width)
         pairs.append((far_hidden.at[:, columns], hidden.at[:, columns]))
-    pairs += [(far_cot, cot), (far_b, b), (far_x, x)]
+    pairs += [(far_cot, cot), (far_b, b), (first, block), (far_x, x)]
     fetches = [pltpu.make_async_copy(*pair, arrived.at[at]) for at, pair in enumerate(pairs)]
-    arrive = in_turn(fetches, 3)
-    arrive()
+    arrive = in_turn(fetches, 6)
+    for _ in range(4):
+        arrive()
     left = a[...].astype(BF16)
     total = None
     for at in range(chunks):
@@ -135,10 +139,13 @@
     values = jnp.where(row == 1, mask[...] * order[...], values)
     values = jnp.where(row == 2, mask[...] * order[...] * order[...], values)
     stats[...] = dot_nt(values.astype(F32).astype(BF16), member.astype(BF16))
+    for at, array in enumerate((index, mask, order)):
+        tok[at : at + 1, :] = array[...]
     arrive()
-
-
-def gradient_kernel(replicas, rank, all_index, all_mask, all_order, packed, arrived, hidden, cot, *rest):
+    arrive()
+
+
+def gradient_kernel(replicas, rank, tok, packed, arrived, hidden, cot, *rest):
     stats, (own_a, own_b, *sent) = rest[:replicas], rest[replicas:-2]
     column, grad = rest[-2:]
     rows = rank // replicas
@@ -156,9 +163,9 @@
     total = jnp.maximum(jnp.sum(counts, axis=1, keepdims=True), 1.0)
 
     row = lax.broadcasted_iota(jnp.int32, (LANES, tokens), 0)
-    tall = jnp.where(row == 0, all_index[...], 0)
-    tall = jnp.where(row == 1, all_mask[...], tall)
-    tall = jnp.where(row == 2, all_order[...], tall)
+    tall = jnp.where(row == 0, tok[0:1, :], 0)
+    tall = jnp.where(row == 1, tok[1:2, :], tall)
+    tall = jnp.where(row == 2, tok[2:3, :], tall)
     column[...] = jnp.transpose(tall.astype(F32))
     index, mask, order = column[:, 0:1], column[:, 1:2], column[:, 2:3]
     member = index == lax.broadcasted_iota(jnp.int32, (tokens, groups), 1).astype(F32)
@@ -235,26 +242,17 @@
         keep(at).wait()
 
 
-def rollout_kernel(differs, following, first, x, *rest):
+def rollout_kernel(following, x, given, *rest):
     if following is None:
-        given, out = rest
-    elif first:
-        w, out, after, given, arrived = rest
+        (out,) = rest
     else:
-        given, w, out, after, arrived = rest
+        w, out, after, arrived = rest
     me = lax.axis_index("tensor")
     width = out.shape[1]
 
-    def fetch(differs, held, at):
-        start = pl.multiple_of(lax.bitwise_xor(me, differs) * width, width)
-        return pltpu.make_async_copy(w.at[:, pl.ds(start, width)], held, arrived.at[at])
-
-    if first:
-        own = fetch(differs, given, 0)
-        own.start()
-        own.wait()
     if following is not None:
-        next_one = fetch(following, after, 1)
+        start = pl.multiple_of(lax.bitwise_xor(me, following) * width, width)
+        next_one = pltpu.make_async_copy(w.at[:, pl.ds(start, width)], after, arrived)
         next_one.start()
     out[...] = dot(x[...], given[...]).astype(out.dtype)
     if following is not None:
@@ -328,7 +326,7 @@
 
     chips = peers // 2
     todo = [(m, other) for m in range(chips - 1, -1, -1) for other in (1, 0)]
-    crossed, arrived, own, waiting, handed = {}, {}, {}, [], None
+    crossed, arrived, own, waiting = {}, {}, {}, []
 
     def form(eighths, after):
         nonlocal handed
@@ -337,17 +335,14 @@
             following = 2 * todo[0][0] + todo[0][1] if todo else None
             result = shape((rollout, own_width), BF16 if other else F32)
             block = shape((inner, own_width), BF16)
-            held = [x_held] if handed is None else [x_held, handed]
-            scratch = [pltpu.VMEM(block.shape, BF16)] if handed is None else []
-            scratch += [pltpu.SemaphoreType.DMA((2,))] if following is not None else []
             result, *handed = call(
-                functools.partial(rollout_kernel, 2 * m + other, following, handed is None),
+                functools.partial(rollout_kernel, following),
                 "rollout%d%d" % (m, other),
-                held,
+                [x_held, handed],
                 [w] if following is not None else [],
                 [result] + ([block] if following is not None else []),
                 [],
-                scratch,
+                [pltpu.SemaphoreType.DMA(())] if following is not None else [],
                 2 * rollout * inner * own_width,
                 20,
                 after,
@@ -379,26 +374,29 @@
     tok = [
         array.reshape(1, tokens) for array in (prompt_group_index, answer_token_mask, token_reward_order)
     ]
-    packed, stats, hidden_held, cot_held, x_held = call(
-        project_kernel,
+    packed, stats, tok_held, hidden_held, cot_held, x_held, handed = call(
+        functools.partial(project_kernel, 2 * todo[0][0] + todo[0][1]),
         "project",
-        tok,
-        [hidden, source_lowdim_matrix, cotangent, target_lowdim_matrix, x],
+        [],
+        [*tok, hidden, source_lowdim_matrix, cotangent, target_lowdim_matrix, x, w],
         [
             shape((tokens // 2, LANES), F32),
             shape((8, groups), F32),
+            shape((8, tokens), jnp.int32),
             shape(hidden.shape, BF16),
             shape(cotangent.shape, BF16),
             shape(x.shape, BF16),
+            shape((inner, own_width), BF16),
         ],
         [],
-        [
+        [pltpu.VMEM((1, tokens), jnp.int32)] * 3
+        + [
             pltpu.VMEM((rank, inner), F32),
             pltpu.VMEM((rank, columns), F32),
-            pltpu.SemaphoreType.DMA((inner // deep + 4,)),
+            pltpu.SemaphoreType.DMA((inner // deep + 8,)),
         ],
         2 * tokens * (inner + columns) * 256,
-        45,
+        38.6,
     )
     all_stats = [stats] + [xor(stats, k, "dp") for k in range(1, replicas)]
     tensor_bits = [1 << at for at in range(peers.bit_length() - 1)]
@@ -413,7 +411,7 @@
     own_a, own_b, *sent = call(
         functools.partial(gradient_kernel, replicas, rank),
         "gradient",
-        [*tok, packed, received, hidden_held, cot_held, *all_stats],
+        [tok_held, packed, received, hidden_held, cot_held, *all_stats],
         [],
         [shape((rows, inner), F32), shape((rank, columns), F32)]
         + [shape((2 * rows, inner // 2 + columns * replicas // 2), BF16)] * (replicas - 1),
@@ -424,7 +422,7 @@
         after,
     )
     received = [xor(array, k + 1, "dp") for k, array in enumerate(sent)]
-    after = form(1, send_on(form(1, [own_a])))
+    after = send_on(form(1, [own_a]))
 
     left = [source_lowdim_matrix, running_mean_source_matrix, running_variance_source_matrix]
     right = [target_lowdim_matrix, running_mean_target_matrix, running_variance_target_matrix]
@@ -453,23 +451,24 @@
     for at in range(replicas.bit_length() - 1):
         received = xor(product, 1 << at, "dp")
         if at < 2:
-            after = form(1, after) if todo else after
+            after = form(1, after)
+        if at == replicas.bit_length() - 2:
+            after = after + [factor]
         both = shape((2 * product.shape[0], rollout), F32)
         (product,) = call(
             functools.partial(gather_kernel, at), "gather", [product, received], [], [both], [], [], 0, 8, after
         )
         after = [product]
-        if at < 1:
-            after = send_on(after)
     for at, bit in enumerate(tensor_bits):
         received = xor(product, bit)
-        if at == 0 and todo:
-            after = form(len(todo) * 8 // len(todo_all), after)
+        if at < 2 and todo:
+            after = form(1 if at == 0 else len(todo) * 8 // len(todo_all), after)
         if at < len(tensor_bits) - 1:
-            product = add([product, received], after + [factor] * (at == len(tensor_bits) - 2))
+            product = add([product, received], after)
             after = [product]
-    send_on_last = [m for m in waiting if m]
-    waiting[:] = send_on_last
+        if at == 0:
+            after = send_on(after)
+    waiting.remove(0)
     send_on(after)
 
     (result,) = call(

time: 115 us -> 121 us (1.052)
  starting transfers between devices: 21.6 us -> 26 us
  local copies, waits for them, and re-layouts: 8.73 us -> 11.6 us
  Pallas kernels: 64.1 us -> 61.4 us
    ppermute x21, starting transfers between devices: 21 us -> 25.4 us  [xor(): lax.ppermute(array, axis, [(i, i ^ k) for i in range(lax.axis_size(axis))])]
    unnamed x38 -> x28, local copies, waits for them, and re-layouts: 8.73 us -> 11.6 us
    pallas_call x21, Pallas kernels: 64.1 us -> 61.4 us  [call(): pl.pallas_call(body, name=name, out_shape=[*outputs, *far_outputs], in_sp...]
  transfers between devices with their start and end apart: 22 -> 22, of which waited for: 4 -> 4; matrix products, arithmetic and copies ran while one was open for 0% -> 0% of each run, Pallas kernels for 44% -> 40%
where the time goes in v2:
time: 121 us; the launch traced here: 120 us
  Pallas kernels  61.4 us (51%)
  starting transfers between devices  26 us (21%)
  waiting for transfers between devices  20 us (17%)
  local copies, waits for them, and re-layouts  11.6 us (10%)
    pallas_call x21, Pallas kernels, call(): pl.pallas_call(body, name=name, out_shape=[*outputs, *far_outputs], in_sp...  61.4 us
    ppermute x21, starting transfers between devices, xor(): lax.ppermute(array, axis, [(i, i ^ k) for i in range(lax.axis_size(axis))])  25.4 us
    ppermute x21, waiting for transfers between devices, xor(): lax.ppermute(array, axis, [(i, i ^ k) for i in range(lax.axis_size(axis))])  20 us
    unnamed x28, local copies, waits for them, and re-layouts  11.6 us
  transfers between devices with their start and end apart: 22, of which 4 were waited for; matrix products, arithmetic and copies ran while one was open for 0% of the time, Pallas kernels for 40%

profile of v2, /device:TPU:0, one launch (start us, length us, event | category | flops | bytes accessed | tf_op | source)
XLA Modules:
  0.0 120.1 jit_solution(14990571603880957463)
XLA Ops:
  0.6 1.1 copy-done.3
  1.8 1.6 %copy-done.4 = bf16[512,2048]{1,0:T(8,128)(2,1)S(1)} copy-done((bf16[512,2048]{1,0:T(8,128)(2,1)S(1)}, bf16[512,2048]{1,0:T(8,128)(2,1)}, u32[]{:S(2)}) %copy-start.4) | copy-done | bytes 2097176
  3.4 0.9 copy-done.5
  4.3 0.7 copy-done.11
  5.0 0.7 copy-done.12
  5.7 0.7 copy-done.13
  6.4 12.2 %project.1 = (f32[256,128]{1,0:T(8,128)S(1)}, f32[8,256]{1,0:T(8,128)S(1)}, s32[8,512]{1,0:T(8,128)S(1)}, bf16[512,6656]{1,0:T(8,128)(2,1)S(1)}, bf16[512,2048]{...) custom-call(s32[1,512]{1,0:T(1,128)S(1)} %bitcast.3, s32[1,512]{1,0:T(1,128)S(1)} %bitcast.4, ...), custom_call_target="tpu_custom_call" | custom-call | flops 2281701376 | bytes 71374848 | tf_op jit(solution)/shard_map/project/pallas_call | solution.py:77
  18.6 3.0 %collective-permute-start.3 = (f32[8,256]{1,0:T(8,128)S(1)}, f32[8,256]{1,0:T(8,128)S(1)}, u32[]{:S(2)}, u32[]{:S(2)}) collective-permute-start(f32[8,256]{1,0:T(8,128)S(1)} %get-tuple-element.50.refs_5_), channel_id=1, source_target_pairs={{0,8},{8,0},{16,24},{24,16},{1,9},{9,1},{17,25},{25,17},{2,10},{10... | collective-permute-start | bytes 24584 | tf_op jit(solution)/shard_map/ppermute | solution.py:319
  21.6 1.5 %collective-permute-start.4 = (f32[8,256]{1,0:T(8,128)S(1)}, f32[8,256]{1,0:T(8,128)S(1)}, u32[]{:S(2)}, u32[]{:S(2)}) collective-permute-start(f32[8,256]{1,0:T(8,128)S(1)} %get-tuple-element.50.refs_5_), channel_id=1, source_target_pairs={{0,16},{8,24},{16,0},{24,8},{1,17},{9,25},{17,1},{25,9},{2,18},{10... | collective-permute-start | bytes 24584 | tf_op jit(solution)/shard_map/ppermute | solution.py:319
  23.1 0.0 collective-permute-start.5
  23.2 2.9 %copy-done = bf16[512,6656]{1,0:T(8,128)(2,1)S(1)} copy-done((bf16[512,6656]{1,0:T(8,128)(2,1)S(1)}, bf16[512,6656]{1,0:T(8,128)(2,1)}, u32[]{:S(2)}) %copy-start) | copy-done | bytes 6815768
  26.1 2.9 %copy-done.2 = bf16[6656,512]{1,0:T(8,128)(2,1)S(1)} copy-done((bf16[6656,512]{1,0:T(8,128)(2,1)S(1)}, bf16[6656,512]{1,0:T(8,128)(2,1)}, u32[]{:S(2)}) %copy-start.2) | copy-done | bytes 6815768
  29.0 3.7 %rollout31.1 = (bf16[512,512]{1,0:T(8,128)(2,1)S(1)}, bf16[6656,512]{1,0:T(8,128)(2,1)S(1)}) custom-call(bf16[512,6656]{1,0:T(8,128)(2,1)S(1)} %copy-done, bf16[6656,512]{1,0:T(8,128)(2,1)S(1)} %copy-done.2, bf16[6656,4096]{1,0:T(8,128)(2,1)} %refs_2_.13, f32[256,128]{1,0:T(8,128)S(1)} %get-tuple-element.42.refs_3_.refs_0_), custom_call_target="tpu_custom_call" | custom-call | flops 3489660928 | bytes 54525952 | tf_op jit(solution)/shard_map/rollout31/pallas_call | solution.py:77
  32.7 0.6 collective-permute-start.6
  33.3 2.1 %collective-permute-start.1 = (f32[256,128]{1,0:T(8,128)S(1)}, f32[256,128]{1,0:T(8,128)S(1)}, u32[]{:S(2)}, u32[]{:S(2)}) collective-permute-start(f32[256,128]{1,0:T(8,128)S(1)} %join.7.refs_3_.refs_0_), channel_id=1, source_target_pairs={{0,2},{1,3},{2,0},{3,1},{4,6},{5,7},{6,4},{7,5},{8,10},{9,11},{10,... | collective-permute-start | bytes 393224 | tf_op jit(solution)/shard_map/ppermute | solution.py:319
  35.4 6.4 %rollout30.1 = (f32[512,512]{1,0:T(8,128)S(1)}, bf16[6656,512]{1,0:T(8,128)(2,1)S(1)}) custom-call(bf16[512,6656]{1,0:T(8,128)(2,1)S(1)} %copy-done.1, bf16[6656,512]{1,0:T(8,128)(2,1)S(1)} %get-tuple-element.46.refs_1_, bf16[6656,4096]{1,0:T(8,128)(2,1)} %refs_2_.13, f32[256,128]{1,0:T(8,128)S(1)} %join.7.refs_3_.refs_0_), custom_call_target="tpu_custom_call" | custom-call | flops 3489660928 | bytes 54525952 | tf_op jit(solution)/shard_map/rollout30/pallas_call | solution.py:77
  41.9 2.7 %collective-permute-start.2 = (f32[256,128]{1,0:T(8,128)S(1)}, f32[256,128]{1,0:T(8,128)S(1)}, u32[]{:S(2)}, u32[]{:S(2)}) collective-permute-start(f32[256,128]{1,0:T(8,128)S(1)} %join.8.refs_3_.refs_1_), channel_id=1, source_target_pairs={{0,4},{1,5},{2,6},{3,7},{4,0},{5,1},{6,2},{7,3},{8,12},{9,13},{10,... | collective-permute-start | bytes 393224 | tf_op jit(solution)/shard_map/ppermute | solution.py:319
  44.6 3.7 %rollout21.1 = (bf16[512,512]{1,0:T(8,128)(2,1)S(1)}, bf16[6656,512]{1,0:T(8,128)(2,1)S(1)}) custom-call(bf16[512,6656]{1,0:T(8,128)(2,1)S(1)} %copy-done.1, bf16[6656,512]{1,0:T(8,128)(2,1)S(1)} %get-tuple-element.51.refs_1_, bf16[6656,4096]{1,0:T(8,128)(2,1)} %refs_2_.13, f32[256,128]{1,0:T(8,128)S(1)} %join.8.refs_3_.refs_1_), custom_call_target="tpu_custom_call" | custom-call | flops 3489660928 | bytes 54525952 | tf_op jit(solution)/shard_map/rollout21/pallas_call | solution.py:77
  48.3 0.1 collective-permute-start.10
  48.3 0.1 join.9.refs_9_
  48.5 0.8 collective-permute-start.11
  49.3 1.5 %collective-permute-done.2.refs_2_ = f32[256,128]{1,0:T(8,128)S(1)} collective-permute-done((f32[256,128]{1,0:T(8,128)S(1)}, f32[256,128]{1,0:T(8,128)S(1)}, u32[]{:S(2)}, u32[]{:S(2)}) %collective-permute-start.2) | collective-permute-done | bytes 131104 | tf_op jit(solution)/shard_map/ppermute | solution.py:319
  50.8 2.9 %gradient.1 = (f32[8,6656]{1,0:T(8,128)S(1)}, f32[32,2048]{1,0:T(8,128)S(1)}, bf16[16,7424]{1,0:T(8,128)(2,1)S(1)}, bf16[16,7424]{1,0:T(8,128)(2,1)S(1)}, bf16[16,7424]{1,0:T(8,128)(2,1)S(1)}) custom-call(s32[8,512]{1,0:T(8,128)S(1)} %get-tuple-element.41.refs_0_, f32[256,128]{1,0:T(8,128)S(1)} %join.8.refs_3_.refs_1_, ...), custom_call_target="tpu_custom_call" | custom-call | flops 2281701376 | tf_op jit(solution)/shard_map/gradient/pallas_call | solution.py:77
  53.7 1.6 %collective-permute-start.7 = (bf16[16,7424]{1,0:T(8,128)(2,1)S(1)}, bf16[16,7424]{1,0:T(8,128)(2,1)S(1)}, u32[]{:S(2)}, u32[]{:S(2)}) collective-permute-start(bf16[16,7424]{1,0:T(8,128)(2,1)S(1)} %get-tuple-element.55), channel_id=1, source_target_pairs={{0,8},{8,0},{16,24},{24,16},{1,9},{9,1},{17,25},{25,17},{2,10},{10... | collective-permute-start | bytes 712712 | tf_op jit(solution)/shard_map/ppermute | solution.py:319
  55.2 1.5 %collective-permute-start.8 = (bf16[16,7424]{1,0:T(8,128)(2,1)S(1)}, bf16[16,7424]{1,0:T(8,128)(2,1)S(1)}, u32[]{:S(2)}, u32[]{:S(2)}) collective-permute-start(bf16[16,7424]{1,0:T(8,128)(2,1)S(1)} %get-tuple-element.56), channel_id=1, source_target_pairs={{0,16},{8,24},{16,0},{24,8},{1,17},{9,25},{17,1},{25,9},{2,18},{10... | collective-permute-start | bytes 712712 | tf_op jit(solution)/shard_map/ppermute | solution.py:319
  56.8 0.5 collective-permute-start.9
  57.3 6.4 %rollout20.1 = (f32[512,512]{1,0:T(8,128)S(1)}, bf16[6656,512]{1,0:T(8,128)(2,1)S(1)}) custom-call(bf16[512,6656]{1,0:T(8,128)(2,1)S(1)} %copy-done.1, bf16[6656,512]{1,0:T(8,128)(2,1)S(1)} %get-tuple-element.58.refs_1_, bf16[6656,4096]{1,0:T(8,128)(2,1)} %refs_2_.13, f32[8,6656]{1,0:T(8,128)S(1)} %get-tuple-element.53.refs_3_.refs_0_), custom_call_target="tpu_custom_call" | custom-call | flops 3489660928 | bytes 54525952 | tf_op jit(solution)/shard_map/rollout20/pallas_call | solution.py:77
  63.7 0.2 join.10.refs_12_
  63.9 0.1 collective-permute-start.21
  64.0 3.0 %collective-permute-done.8.refs_4_ = bf16[16,7424]{1,0:T(8,128)(2,1)S(1)} collective-permute-done((bf16[16,7424]{1,0:T(8,128)(2,1)S(1)}, bf16[16,7424]{1,0:T(8,128)(2,1)S(1)}, u32[]{:S(2)}, u32[]{:S(2)}) %collective-permute-start.8) | collective-permute-done | bytes 237600 | tf_op jit(solution)/shard_map/ppermute | solution.py:319
  67.0 4.2 %update.1 = (bf16[32,512]{1,0:T(8,128)(2,1)S(1)}, f32[8,512]{1,0:T(8,128)S(1)}, f32[8,6656]{1,0:T(8,128)}, f32[8,6656]{1,0:T(8,128)}, f32[8,6656]{1,0:T(8,128)},...) custom-call(f32[8,6656]{1,0:T(8,128)S(1)} %get-tuple-element.53.refs_3_.refs_0_, ...), custom_call_target="tpu_custom_call" | custom-call | flops 1744830464 | bytes 4177920 | tf_op jit(solution)/shard_map/update/pallas_call | solution.py:77
  71.2 1.3 %collective-permute-start.13 = (f32[8,512]{1,0:T(8,128)S(1)}, f32[8,512]{1,0:T(8,128)S(1)}, u32[]{:S(2)}, u32[]{:S(2)}) collective-permute-start(f32[8,512]{1,0:T(8,128)S(1)} %get-tuple-element.61.refs_3_.refs_0_), channel_id=1, source_target_pairs={{0,8},{8,0},{16,24},{24,16},{1,9},{9,1},{17,25},{25,17},{2,10},{10... | collective-permute-start | bytes 49160 | tf_op jit(solution)/shard_map/ppermute | solution.py:319
  72.5 3.7 %rollout11.1 = (bf16[512,512]{1,0:T(8,128)(2,1)S(1)}, bf16[6656,512]{1,0:T(8,128)(2,1)S(1)}) custom-call(bf16[512,6656]{1,0:T(8,128)(2,1)S(1)} %copy-done.1, bf16[6656,512]{1,0:T(8,128)(2,1)S(1)} %get-tuple-element.62.refs_1_, bf16[6656,4096]{1,0:T(8,128)(2,1)} %refs_2_.13, f32[8,512]{1,0:T(8,128)S(1)} %get-tuple-element.61.refs_3_.refs_0_), custom_call_target="tpu_custom_call" | custom-call | flops 3489660928 | bytes 54525952 | tf_op jit(solution)/shard_map/rollout11/pallas_call | solution.py:77
  76.2 0.7 collective-permute-start.12
  76.9 1.6 %collective-permute-start.17 = (bf16[512,512]{1,0:T(8,128)(2,1)S(1)}, bf16[512,512]{1,0:T(8,128)(2,1)S(1)}, u32[]{:S(2)}, u32[]{:S(2)}) collective-permute-start(bf16[512,512]{1,0:T(8,128)(2,1)S(1)} %get-tuple-element.63.refs_2_), channel_id=1, source_target_pairs={{0,1},{1,0},{2,3},{3,2},{4,5},{5,4},{6,7},{7,6},{8,9},{9,8},{10,11... | collective-permute-start | bytes 1572872 | tf_op jit(solution)/shard_map/ppermute | solution.py:319
  78.6 5.3 %collective-permute-start.14 = (f32[16,512]{1,0:T(8,128)S(1)}, f32[16,512]{1,0:T(8,128)S(1)}, u32[]{:S(2)}, u32[]{:S(2)}) collective-permute-start(f32[16,512]{1,0:T(8,128)S(1)} %gather.2.refs_3_.refs_0_), channel_id=1, source_target_pairs={{0,16},{8,24},{16,0},{24,8},{1,17},{9,25},{17,1},{25,9},{2,18},{10... | collective-permute-start | bytes 98312 | tf_op jit(solution)/shard_map/ppermute | solution.py:319
  83.8 6.4 %rollout10.1 = (f32[512,512]{1,0:T(8,128)S(1)}, bf16[6656,512]{1,0:T(8,128)(2,1)S(1)}) custom-call(bf16[512,6656]{1,0:T(8,128)(2,1)S(1)} %copy-done.1, bf16[6656,512]{1,0:T(8,128)(2,1)S(1)} %get-tuple-element.64.refs_1_, bf16[6656,4096]{1,0:T(8,128)(2,1)} %refs_2_.13, f32[16,512]{1,0:T(8,128)S(1)} %gather.2.refs_3_.refs_0_), custom_call_target="tpu_custom_call" | custom-call | flops 3489660928 | bytes 54525952 | tf_op jit(solution)/shard_map/rollout10/pallas_call | solution.py:77
  90.3 0.1 collective-permute-start.15
  90.4 6.2 %rollout01.1 = (bf16[512,512]{1,0:T(8,128)(2,1)S(1)}, bf16[6656,512]{1,0:T(8,128)(2,1)S(1)}) custom-call(bf16[512,6656]{1,0:T(8,128)(2,1)S(1)} %copy-done.1, bf16[6656,512]{1,0:T(8,128)(2,1)S(1)} %get-tuple-element.66.refs_1_, bf16[6656,4096]{1,0:T(8,128)(2,1)} %refs_2_.13, f32[32,512]{1,0:T(8,128)S(1)} %gather.3.refs_3_.refs_0_), custom_call_target="tpu_custom_call" | custom-call | flops 3489660928 | bytes 54525952 | tf_op jit(solution)/shard_map/rollout01/pallas_call | solution.py:77
  96.6 0.6 collective-permute-start.19
  97.2 0.1 join.12.refs_2_
  97.3 0.9 collective-permute-start.20
  98.2 1.2 %collective-permute-start.16 = (f32[32,512]{1,0:T(8,128)S(1)}, f32[32,512]{1,0:T(8,128)S(1)}, u32[]{:S(2)}, u32[]{:S(2)}) collective-permute-start(f32[32,512]{1,0:T(8,128)S(1)} %join.11.refs_2_.refs_0_), channel_id=1, source_target_pairs={{0,2},{1,3},{2,0},{3,1},{4,6},{5,7},{6,4},{7,5},{8,10},{9,11},{10,... | collective-permute-start | bytes 196616 | tf_op jit(solution)/shard_map/ppermute | solution.py:319
  99.4 3.7 %rollout00.1.refs_2_.refs_3_ = f32[512,512]{1,0:T(8,128)S(1)} custom-call(bf16[512,6656]{1,0:T(8,128)(2,1)S(1)} %copy-done.1, bf16[6656,512]{1,0:T(8,128)(2,1)S(1)} %get-tuple-element.68.refs_1_, bf16[512,512]{1,0:T(8,128)(2,1)S(1)} %join.12.refs_2_), custom_call_target="tpu_custom_call" | custom-call | flops 3489660928 | tf_op jit(solution)/shard_map/rollout00/pallas_call | solution.py:77
  103.1 9.6 %collective-permute-done.16.refs_1_ = f32[32,512]{1,0:T(8,128)S(1)} collective-permute-done((f32[32,512]{1,0:T(8,128)S(1)}, f32[32,512]{1,0:T(8,128)S(1)}, u32[]{:S(2)}, u32[]{:S(2)}) %collective-permute-start.16) | collective-permute-done | bytes 65568 | tf_op jit(solution)/shard_map/ppermute | solution.py:319
  112.7 0.1 collective-permute-start.18
  112.8 5.8 %collective-permute-done.18.refs_2_ = f32[32,512]{1,0:T(8,128)S(1)} collective-permute-done((f32[32,512]{1,0:T(8,128)S(1)}, f32[32,512]{1,0:T(8,128)S(1)}, u32[]{:S(2)}, u32[]{:S(2)}) %collective-permute-start.18) | collective-permute-done | bytes 65568 | tf_op jit(solution)/shard_map/ppermute | solution.py:319
  118.6 1.3 %finish.1 = bf16[512,512]{1,0:T(8,128)(2,1)} custom-call(bf16[32,512]{1,0:T(8,128)(2,1)S(1)} %collective-permute-done.12.refs_3_.refs_0_, f32[32,512]{1,0:T(8,128)S(1)} %join.13.refs_1_, f32[32,512]{1,0:T(8,128)S(1)} %collective-permute-done.18.refs_2_, f32[512,512]{1,0:T(8,128)S(1)} %rollout00.1.refs_2_.refs_3_, ...), custom_call_target="tpu_custom_call" | custom-call | flops 134217728 | bytes 524288 | tf_op jit(solution)/shard_map/finish/pallas_call | solution.py:77
  (45 shorter events, 0.2 us)
Async XLA Ops:
  0.6 1.2 copy-start.3
  1.8 1.6 %copy-start.4 = (bf16[512,2048]{1,0:T(8,128)(2,1)S(1)}, bf16[512,2048]{1,0:T(8,128)(2,1)}, u32[]{:S(2)}) copy-start(bf16[512,2048]{1,0:T(8,128)(2,1)} %refs_5_.1) | copy-start | bytes 6291460
  3.4 0.9 copy-start.5
  4.3 0.7 copy-start.11
  5.0 0.7 copy-start.12
  5.7 0.7 copy-start.13
  18.6 29.8 %collective-permute-start.3 = (f32[8,256]{1,0:T(8,128)S(1)}, f32[8,256]{1,0:T(8,128)S(1)}, u32[]{:S(2)}, u32[]{:S(2)}) collective-permute-start(f32[8,256]{1,0:T(8,128)S(1)} %get-tuple-element.50.refs_5_), channel_id=1, source_target_pairs={{0,8},{8,0},{16,24},{24,16},{1,9},{9,1},{17,25},{25,17},{2,10},{10... | collective-permute-start | bytes 24584 | tf_op jit(solution)/shard_map/ppermute | solution.py:319
  21.6 27.7 %collective-permute-start.4 = (f32[8,256]{1,0:T(8,128)S(1)}, f32[8,256]{1,0:T(8,128)S(1)}, u32[]{:S(2)}, u32[]{:S(2)}) collective-permute-start(f32[8,256]{1,0:T(8,128)S(1)} %get-tuple-element.50.refs_5_), channel_id=1, source_target_pairs={{0,16},{8,24},{16,0},{24,8},{1,17},{9,25},{17,1},{25,9},{2,18},{10... | collective-permute-start | bytes 24584 | tf_op jit(solution)/shard_map/ppermute | solution.py:319
  23.1 26.1 %collective-permute-start.5 = (f32[8,256]{1,0:T(8,128)S(1)}, f32[8,256]{1,0:T(8,128)S(1)}, u32[]{:S(2)}, u32[]{:S(2)}) collective-permute-start(f32[8,256]{1,0:T(8,128)S(1)} %get-tuple-element.50.refs_5_), channel_id=1, source_target_pairs={{0,24},{8,16},{16,8},{24,0},{1,25},{9,17},{17,9},{25,1},{2,26},{10... | collective-permute-start | bytes 24584 | tf_op jit(solution)/shard_map/ppermute | solution.py:319
  23.2 10.1 %collective-permute-start = (f32[256,128]{1,0:T(8,128)S(1)}, f32[256,128]{1,0:T(8,128)S(1)}, u32[]{:S(2)}, u32[]{:S(2)}) collective-permute-start(f32[256,128]{1,0:T(8,128)S(1)} %get-tuple-element.42.refs_3_.refs_0_), channel_id=1, source_target_pairs={{0,1},{1,0},{2,3},{3,2},{4,5},{5,4},{6,7},{7,6},{8,9},{9,8},{10,11... | collective-permute-start | bytes 393224 | tf_op jit(solution)/shard_map/ppermute | solution.py:319
  23.2 2.9 %copy-start = (bf16[512,6656]{1,0:T(8,128)(2,1)S(1)}, bf16[512,6656]{1,0:T(8,128)(2,1)}, u32[]{:S(2)}) copy-start(bf16[512,6656]{1,0:T(8,128)(2,1)} %get-tuple-element.43.refs_0_.refs_2_) | copy-start | bytes 20447236
  26.1 2.9 %copy-start.2 = (bf16[6656,512]{1,0:T(8,128)(2,1)S(1)}, bf16[6656,512]{1,0:T(8,128)(2,1)}, u32[]{:S(2)}) copy-start(bf16[6656,512]{1,0:T(8,128)(2,1)} %get-tuple-element.44.refs_1_) | copy-start | bytes 20447236
  29.0 6.4 %copy-start.1 = (bf16[512,6656]{1,0:T(8,128)(2,1)S(1)}, bf16[512,6656]{1,0:T(8,128)(2,1)}, u32[]{:S(2)}) copy-start(bf16[512,6656]{1,0:T(8,128)(2,1)} %get-tuple-element.43.refs_0_.refs_2_) | copy-start | bytes 20447236
  32.7 15.5 %collective-permute-start.6 = (bf16[512,512]{1,0:T(8,128)(2,1)S(1)}, bf16[512,512]{1,0:T(8,128)(2,1)S(1)}, u32[]{:S(2)}, u32[]{:S(2)}) collective-permute-start(bf16[512,512]{1,0:T(8,128)(2,1)S(1)} %get-tuple-element.45.refs_2_), channel_id=1, source_target_pairs={{0,1},{1,0},{2,3},{3,2},{4,5},{5,4},{6,7},{7,6},{8,9},{9,8},{10,11... | collective-permute-start | bytes 1572872 | tf_op jit(solution)/shard_map/ppermute | solution.py:319
  33.3 8.6 %collective-permute-start.1 = (f32[256,128]{1,0:T(8,128)S(1)}, f32[256,128]{1,0:T(8,128)S(1)}, u32[]{:S(2)}, u32[]{:S(2)}) collective-permute-start(f32[256,128]{1,0:T(8,128)S(1)} %join.7.refs_3_.refs_0_), channel_id=1, source_target_pairs={{0,2},{1,3},{2,0},{3,1},{4,6},{5,7},{6,4},{7,5},{8,10},{9,11},{10,... | collective-permute-start | bytes 393224 | tf_op jit(solution)/shard_map/ppermute | solution.py:319
  41.9 8.9 %collective-permute-start.2 = (f32[256,128]{1,0:T(8,128)S(1)}, f32[256,128]{1,0:T(8,128)S(1)}, u32[]{:S(2)}, u32[]{:S(2)}) collective-permute-start(f32[256,128]{1,0:T(8,128)S(1)} %join.8.refs_3_.refs_1_), channel_id=1, source_target_pairs={{0,4},{1,5},{2,6},{3,7},{4,0},{5,1},{6,2},{7,3},{8,12},{9,13},{10,... | collective-permute-start | bytes 393224 | tf_op jit(solution)/shard_map/ppermute | solution.py:319
  48.3 15.5 %collective-permute-start.10 = (bf16[512,512]{1,0:T(8,128)(2,1)S(1)}, bf16[512,512]{1,0:T(8,128)(2,1)S(1)}, u32[]{:S(2)}, u32[]{:S(2)}) collective-permute-start(bf16[512,512]{1,0:T(8,128)(2,1)S(1)} %get-tuple-element.52.refs_2_), channel_id=1, source_target_pairs={{0,1},{1,0},{2,3},{3,2},{4,5},{5,4},{6,7},{7,6},{8,9},{9,8},{10,11... | collective-permute-start | bytes 1572872 | tf_op jit(solution)/shard_map/ppermute | solution.py:319
  48.5 15.3 %collective-permute-start.11 = (bf16[512,512]{1,0:T(8,128)(2,1)S(1)}, bf16[512,512]{1,0:T(8,128)(2,1)S(1)}, u32[]{:S(2)}, u32[]{:S(2)}) collective-permute-start(bf16[512,512]{1,0:T(8,128)(2,1)S(1)} %join.9.refs_9_), channel_id=1, source_target_pairs={{0,2},{1,3},{2,0},{3,1},{4,6},{5,7},{6,4},{7,5},{8,10},{9,11},{10,... | collective-permute-start | bytes 1572872 | tf_op jit(solution)/shard_map/ppermute | solution.py:319
  53.7 10.3 %collective-permute-start.7 = (bf16[16,7424]{1,0:T(8,128)(2,1)S(1)}, bf16[16,7424]{1,0:T(8,128)(2,1)S(1)}, u32[]{:S(2)}, u32[]{:S(2)}) collective-permute-start(bf16[16,7424]{1,0:T(8,128)(2,1)S(1)} %get-tuple-element.55), channel_id=1, source_target_pairs={{0,8},{8,0},{16,24},{24,16},{1,9},{9,1},{17,25},{25,17},{2,10},{10... | collective-permute-start | bytes 712712 | tf_op jit(solution)/shard_map/ppermute | solution.py:319
  55.2 11.8 %collective-permute-start.8 = (bf16[16,7424]{1,0:T(8,128)(2,1)S(1)}, bf16[16,7424]{1,0:T(8,128)(2,1)S(1)}, u32[]{:S(2)}, u32[]{:S(2)}) collective-permute-start(bf16[16,7424]{1,0:T(8,128)(2,1)S(1)} %get-tuple-element.56), channel_id=1, source_target_pairs={{0,16},{8,24},{16,0},{24,8},{1,17},{9,25},{17,1},{25,9},{2,18},{10... | collective-permute-start | bytes 712712 | tf_op jit(solution)/shard_map/ppermute | solution.py:319
  56.8 10.2 %collective-permute-start.9 = (bf16[16,7424]{1,0:T(8,128)(2,1)S(1)}, bf16[16,7424]{1,0:T(8,128)(2,1)S(1)}, u32[]{:S(2)}, u32[]{:S(2)}) collective-permute-start(bf16[16,7424]{1,0:T(8,128)(2,1)S(1)} %get-tuple-element.57), channel_id=1, source_target_pairs={{0,24},{8,16},{16,8},{24,0},{1,25},{9,17},{17,9},{25,1},{2,26},{10... | collective-permute-start | bytes 712712 | tf_op jit(solution)/shard_map/ppermute | solution.py:319
  57.2 9.8 %copy-start.6 = (f32[32,2048]{1,0:T(8,128)S(1)}, f32[32,2048]{1,0:T(8,128)}, u32[]{:S(2)}) copy-start(f32[32,2048]{1,0:T(8,128)} %refs_9_.1) | copy-start | bytes 786436
  57.2 9.8 %copy-start.7 = (f32[32,6656]{1,0:T(8,128)S(1)}, f32[32,6656]{1,0:T(8,128)}, u32[]{:S(2)}) copy-start(f32[32,6656]{1,0:T(8,128)} %refs_7_.3) | copy-start | bytes 2555908
  57.2 9.8 %copy-start.8 = (f32[32,6656]{1,0:T(8,128)S(1)}, f32[32,6656]{1,0:T(8,128)}, u32[]{:S(2)}) copy-start(f32[32,6656]{1,0:T(8,128)} %refs_8_.3) | copy-start | bytes 2555908
  57.2 9.8 %copy-start.9 = (f32[32,2048]{1,0:T(8,128)S(1)}, f32[32,2048]{1,0:T(8,128)}, u32[]{:S(2)}) copy-start(f32[32,2048]{1,0:T(8,128)} %refs_10_.1) | copy-start | bytes 786436
  57.3 9.8 %copy-start.10 = (f32[32,2048]{1,0:T(8,128)S(1)}, f32[32,2048]{1,0:T(8,128)}, u32[]{:S(2)}) copy-start(f32[32,2048]{1,0:T(8,128)} %refs_11_.1) | copy-start | bytes 786436
  63.9 48.8 %collective-permute-start.21 = (bf16[512,512]{1,0:T(8,128)(2,1)S(1)}, bf16[512,512]{1,0:T(8,128)(2,1)S(1)}, u32[]{:S(2)}, u32[]{:S(2)}) collective-permute-start(bf16[512,512]{1,0:T(8,128)(2,1)S(1)} %join.10.refs_12_), channel_id=1, source_target_pairs={{0,4},{1,5},{2,6},{3,7},{4,0},{5,1},{6,2},{7,3},{8,12},{9,13},{10,... | collective-permute-start | bytes 1572872 | tf_op jit(solution)/shard_map/ppermute | solution.py:319
  71.2 7.3 %collective-permute-start.13 = (f32[8,512]{1,0:T(8,128)S(1)}, f32[8,512]{1,0:T(8,128)S(1)}, u32[]{:S(2)}, u32[]{:S(2)}) collective-permute-start(f32[8,512]{1,0:T(8,128)S(1)} %get-tuple-element.61.refs_3_.refs_0_), channel_id=1, source_target_pairs={{0,8},{8,0},{16,24},{24,16},{1,9},{9,1},{17,25},{25,17},{2,10},{10... | collective-permute-start | bytes 49160 | tf_op jit(solution)/shard_map/ppermute | solution.py:319
  76.2 14.0 %collective-permute-start.12 = (bf16[32,512]{1,0:T(8,128)(2,1)S(1)}, bf16[32,512]{1,0:T(8,128)(2,1)S(1)}, u32[]{:S(2)}, u32[]{:S(2)}) collective-permute-start(bf16[32,512]{1,0:T(8,128)(2,1)S(1)} %get-tuple-element.60), channel_id=1, source_target_pairs={{0,0},{1,4},{2,8},{3,12},{4,16},{5,20},{6,24},{7,28},{8,1},{9,5},{... | collective-permute-start | bytes 98312 | tf_op jit(solution)/shard_map/ppermute | solution.py:449
  76.9 20.3 %collective-permute-start.17 = (bf16[512,512]{1,0:T(8,128)(2,1)S(1)}, bf16[512,512]{1,0:T(8,128)(2,1)S(1)}, u32[]{:S(2)}, u32[]{:S(2)}) collective-permute-start(bf16[512,512]{1,0:T(8,128)(2,1)S(1)} %get-tuple-element.63.refs_2_), channel_id=1, source_target_pairs={{0,1},{1,0},{2,3},{3,2},{4,5},{5,4},{6,7},{7,6},{8,9},{9,8},{10,11... | collective-permute-start | bytes 1572872 | tf_op jit(solution)/shard_map/ppermute | solution.py:319
  78.6 11.7 %collective-permute-start.14 = (f32[16,512]{1,0:T(8,128)S(1)}, f32[16,512]{1,0:T(8,128)S(1)}, u32[]{:S(2)}, u32[]{:S(2)}) collective-permute-start(f32[16,512]{1,0:T(8,128)S(1)} %gather.2.refs_3_.refs_0_), channel_id=1, source_target_pairs={{0,16},{8,24},{16,0},{24,8},{1,17},{9,25},{17,1},{25,9},{2,18},{10... | collective-permute-start | bytes 98312 | tf_op jit(solution)/shard_map/ppermute | solution.py:319
  90.3 6.9 %collective-permute-start.15 = (f32[32,512]{1,0:T(8,128)S(1)}, f32[32,512]{1,0:T(8,128)S(1)}, u32[]{:S(2)}, u32[]{:S(2)}) collective-permute-start(f32[32,512]{1,0:T(8,128)S(1)} %gather.3.refs_3_.refs_0_), channel_id=1, source_target_pairs={{0,1},{1,0},{2,3},{3,2},{4,5},{5,4},{6,7},{7,6},{8,9},{9,8},{10,11... | collective-permute-start | bytes 196616 | tf_op jit(solution)/shard_map/ppermute | solution.py:319
  96.6 16.1 %collective-permute-start.19 = (bf16[512,512]{1,0:T(8,128)(2,1)S(1)}, bf16[512,512]{1,0:T(8,128)(2,1)S(1)}, u32[]{:S(2)}, u32[]{:S(2)}) collective-permute-start(bf16[512,512]{1,0:T(8,128)(2,1)S(1)} %get-tuple-element.67.refs_2_), channel_id=1, source_target_pairs={{0,1},{1,0},{2,3},{3,2},{4,5},{5,4},{6,7},{7,6},{8,9},{9,8},{10,11... | collective-permute-start | bytes 1572872 | tf_op jit(solution)/shard_map/ppermute | solution.py:319
  97.3 21.3 %collective-permute-start.20 = (bf16[512,512]{1,0:T(8,128)(2,1)S(1)}, bf16[512,512]{1,0:T(8,128)(2,1)S(1)}, u32[]{:S(2)}, u32[]{:S(2)}) collective-permute-start(bf16[512,512]{1,0:T(8,128)(2,1)S(1)} %join.12.refs_2_), channel_id=1, source_target_pairs={{0,2},{1,3},{2,0},{3,1},{4,6},{5,7},{6,4},{7,5},{8,10},{9,11},{10,... | collective-permute-start | bytes 1572872 | tf_op jit(solution)/shard_map/ppermute | solution.py:319
  98.2 14.5 %collective-permute-start.16 = (f32[32,512]{1,0:T(8,128)S(1)}, f32[32,512]{1,0:T(8,128)S(1)}, u32[]{:S(2)}, u32[]{:S(2)}) collective-permute-start(f32[32,512]{1,0:T(8,128)S(1)} %join.11.refs_2_.refs_0_), channel_id=1, source_target_pairs={{0,2},{1,3},{2,0},{3,1},{4,6},{5,7},{6,4},{7,5},{8,10},{9,11},{10,... | collective-permute-start | bytes 196616 | tf_op jit(solution)/shard_map/ppermute | solution.py:319
  112.7 5.9 %collective-permute-start.18 = (f32[32,512]{1,0:T(8,128)S(1)}, f32[32,512]{1,0:T(8,128)S(1)}, u32[]{:S(2)}, u32[]{:S(2)}) collective-permute-start(f32[32,512]{1,0:T(8,128)S(1)} %join.13.refs_1_), channel_id=1, source_target_pairs={{0,4},{1,5},{2,6},{3,7},{4,0},{5,1},{6,2},{7,3},{8,12},{9,13},{10,... | collective-permute-start | bytes 196616 | tf_op jit(solution)/shard_map/ppermute | solution.py:319

commit v3 on v1

--- a/solution.py
+++ b/solution.py
@@ -81,7 +81,7 @@
         in_specs=[VMEM] * len(held) + [HBM] * len(far) + [ANY] * len(after),
         out_specs=[VMEM] * len(outputs) + [HBM] * len(far_outputs),
         scratch_shapes=scratch,
-        compiler_params=pltpu.CompilerParams(vmem_limit_bytes=vmem * MIB),
+        compiler_params=pltpu.CompilerParams(vmem_limit_bytes=int(vmem * MIB)),
         cost_estimate=pl.CostEstimate(flops=flops, bytes_accessed=moved, transcendentals=0),
     )(*held, *far, *after)
 
@@ -100,17 +100,17 @@
     return arrive
 
 
-def project_kernel(index, mask, order, far_hidden, far_a, far_cot, far_b, far_x, *rest):
-    packed, stats, hidden, cot, x, a, b, arrived = rest
+def project_kernel(index, mask, order, far_hidden, far_a, far_cot, far_b, packed, stats, *rest):
+    hidden, a, cot, b, arrived = rest
     rank = a.shape[0]
     inner = hidden.shape[1]
-    chunks = arrived.shape[0] - 4
+    chunks = arrived.shape[0] - 3
     width = inner // chunks
     pairs = [(far_a, a)]
     for at in range(chunks):
         columns = slice(at * width, (at + 1) * width)
         pairs.append((far_hidden.at[:, columns], hidden.at[:, columns]))
-    pairs += [(far_cot, cot), (far_b, b), (far_x, x)]
+    pairs += [(far_cot, cot), (far_b, b)]
     fetches = [pltpu.make_async_copy(*pair, arrived.at[at]) for at, pair in enumerate(pairs)]
     arrive = in_turn(fetches, 3)
     arrive()
@@ -135,7 +135,6 @@
     values = jnp.where(row == 1, mask[...] * order[...], values)
     values = jnp.where(row == 2, mask[...] * order[...] * order[...], values)
     stats[...] = dot_nt(values.astype(F32).astype(BF16), member.astype(BF16))
-    arrive()
 
 
 def gradient_kernel(replicas, rank, all_index, all_mask, all_order, packed, arrived, hidden, cot, *rest):
@@ -244,21 +243,27 @@
         given, w, out, after, arrived = rest
     me = lax.axis_index("tensor")
     width = out.shape[1]
-
-    def fetch(differs, held, at):
+    parts = 4
+    height = x.shape[1] // parts
+
+    def fetch(differs, held, row):
         start = pl.multiple_of(lax.bitwise_xor(me, differs) * width, width)
-        return pltpu.make_async_copy(w.at[:, pl.ds(start, width)], held, arrived.at[at])
+        copies = []
+        for at in range(parts):
+            rows = slice(at * height, (at + 1) * height)
+            source = w.at[rows, pl.ds(start, width)]
+            copies.append(pltpu.make_async_copy(source, held.at[rows, :], arrived.at[row, at]))
+        for copy in copies:
+            copy.start()
+        return copies
 
     if first:
-        own = fetch(differs, given, 0)
-        own.start()
-        own.wait()
-    if following is not None:
-        next_one = fetch(following, after, 1)
-        next_one.start()
+        for copy in fetch(differs, given, 0):
+            copy.wait()
+    copies = [] if following is None else fetch(following, after, 1)
     out[...] = dot(x[...], given[...]).astype(out.dtype)
-    if following is not None:
-        next_one.wait()
+    for copy in copies:
+        copy.wait()
 
 
 def gather_kernel(bit, mine, arrived, out):
@@ -335,21 +340,20 @@
         for _ in range(eighths * len(todo_all) // 8):
             m, other = todo.pop(0)
             following = 2 * todo[0][0] + todo[0][1] if todo else None
-            result = shape((rollout, own_width), BF16 if other else F32)
+            first = handed is None
+            outputs = [shape((rollout, own_width), BF16 if other else F32)]
             block = shape((inner, own_width), BF16)
-            held = [x_held] if handed is None else [x_held, handed]
-            scratch = [pltpu.VMEM(block.shape, BF16)] if handed is None else []
-            scratch += [pltpu.SemaphoreType.DMA((2,))] if following is not None else []
             result, *handed = call(
-                functools.partial(rollout_kernel, 2 * m + other, following, handed is None),
+                functools.partial(rollout_kernel, 2 * m + other, following, first),
                 "rollout%d%d" % (m, other),
-                held,
-                [w] if following is not None else [],
-                [result] + ([block] if following is not None else []),
+                [x] if first else [x, handed],
+                [] if following is None else [w],
+                outputs + ([] if following is None else [block]),
                 [],
-                scratch,
+                ([pltpu.VMEM(block.shape, BF16)] if first else [])
+                + ([] if following is None else [pltpu.SemaphoreType.DMA((2, 4))]),
                 2 * rollout * inner * own_width,
-                20,
+                12,
                 after,
             )
             handed = handed[0] if handed else None
@@ -379,26 +383,22 @@
     tok = [
         array.reshape(1, tokens) for array in (prompt_group_index, answer_token_mask, token_reward_order)
     ]
-    packed, stats, hidden_held, cot_held, x_held = call(
+    packed, stats = call(
         project_kernel,
         "project",
         tok,
-        [hidden, source_lowdim_matrix, cotangent, target_lowdim_matrix, x],
-        [
-            shape((tokens // 2, LANES), F32),
-            shape((8, groups), F32),
-            shape(hidden.shape, BF16),
-            shape(cotangent.shape, BF16),
-            shape(x.shape, BF16),
-        ],
+        [hidden, source_lowdim_matrix, cotangent, target_lowdim_matrix],
+        [shape((tokens // 2, LANES), F32), shape((8, groups), F32)],
         [],
         [
+            pltpu.VMEM((tokens, inner), BF16),
             pltpu.VMEM((rank, inner), F32),
+            pltpu.VMEM((tokens, columns), BF16),
             pltpu.VMEM((rank, columns), F32),
-            pltpu.SemaphoreType.DMA((inner // deep + 4,)),
+            pltpu.SemaphoreType.DMA((inner // deep + 3,)),
         ],
         2 * tokens * (inner + columns) * 256,
-        45,
+        54,
     )
     all_stats = [stats] + [xor(stats, k, "dp") for k in range(1, replicas)]
     tensor_bits = [1 << at for at in range(peers.bit_length() - 1)]
@@ -413,7 +413,7 @@
     own_a, own_b, *sent = call(
         functools.partial(gradient_kernel, replicas, rank),
         "gradient",
-        [*tok, packed, received, hidden_held, cot_held, *all_stats],
+        [*tok, packed, received, hidden, cotangent, *all_stats],
         [],
         [shape((rows, inner), F32), shape((rank, columns), F32)]
         + [shape((2 * rows, inner // 2 + columns * replicas // 2), BF16)] * (replicas - 1),
@@ -424,7 +424,7 @@
         after,
     )
     received = [xor(array, k + 1, "dp") for k, array in enumerate(sent)]
-    after = form(1, send_on(form(1, [own_a])))
+    after = send_on(form(1, [own_a]))
 
     left = [source_lowdim_matrix, running_mean_source_matrix, running_variance_source_matrix]
     right = [target_lowdim_matrix, running_mean_target_matrix, running_variance_target_matrix]
@@ -434,7 +434,7 @@
     sent_b, product, *updated = call(
         functools.partial(update_kernel, replicas),
         "update",
-        [own_a, own_b, x_held, *received],
+        [own_a, own_b, x, *received],
         [*left, *right],
         [shape((rank, columns // replicas), BF16), shape((rows, rollout), F32)],
         [own_left] * 3 + [own_right] * 3,
@@ -453,23 +453,24 @@
     for at in range(replicas.bit_length() - 1):
         received = xor(product, 1 << at, "dp")
         if at < 2:
-            after = form(1, after) if todo else after
+            after = form(1, after)
+            if at:
+                after = send_on(after)
+        if at == replicas.bit_length() - 2:
+            after = after + [factor]
         both = shape((2 * product.shape[0], rollout), F32)
         (product,) = call(
             functools.partial(gather_kernel, at), "gather", [product, received], [], [both], [], [], 0, 8, after
         )
         after = [product]
-        if at < 1:
-            after = send_on(after)
     for at, bit in enumerate(tensor_bits):
         received = xor(product, bit)
-        if at == 0 and todo:
-            after = form(len(todo) * 8 // len(todo_all), after)
+        if at < 2 and todo:
+            after = form(1 if at == 0 else len(todo) * 8 // len(todo_all), after)
         if at < len(tensor_bits) - 1:
-            product = add([product, received], after + [factor] * (at == len(tensor_bits) - 2))
+            product = add([product, received], after)
             after = [product]
-    send_on_last = [m for m in waiting if m]
-    waiting[:] = send_on_last
+    waiting.remove(0)
     send_on(after)
 
     (result,) = call(

time: 115 us -> 126 us (1.096)
  starting transfers between devices: 21.6 us -> 36.2 us
  local copies, waits for them, and re-layouts: 8.73 us -> 0.97 us
  Pallas kernels: 64.1 us -> 68.1 us
    ppermute x21, starting transfers between devices: 21 us -> 35.6 us  [xor(): lax.ppermute(array, axis, [(i, i ^ k) for i in range(lax.axis_size(axis))])]
    unnamed x38 -> x32, local copies, waits for them, and re-layouts: 8.73 us -> 0.97 us
    pallas_call x21, Pallas kernels: 64.1 us -> 68.1 us  [call(): pl.pallas_call(body, name=name, out_shape=[*outputs, *far_outputs], in_sp...]
  transfers between devices with their start and end apart: 22 -> 22, of which waited for: 4 -> 6; matrix products, arithmetic and copies ran while one was open for 0% -> 0% of each run, Pallas kernels for 44% -> 39%
where the time goes in v3:
time: 126 us; the launch traced here: 125 us
  Pallas kernels  68.1 us (54%)
  starting transfers between devices  36.2 us (29%)
  waiting for transfers between devices  18.2 us (14%)
    pallas_call x21, Pallas kernels, call(): pl.pallas_call(body, name=name, out_shape=[*outputs, *far_outputs], in_sp...  68.1 us
    ppermute x21, starting transfers between devices, xor(): lax.ppermute(array, axis, [(i, i ^ k) for i in range(lax.axis_size(axis))])  35.6 us
    ppermute x21, waiting for transfers between devices, xor(): lax.ppermute(array, axis, [(i, i ^ k) for i in range(lax.axis_size(axis))])  18.2 us
  transfers between devices with their start and end apart: 22, of which 6 were waited for; matrix products, arithmetic and copies ran while one was open for 0% of the time, Pallas kernels for 39%

profile of v3, /device:TPU:0, one launch (start us, length us, event | category | flops | bytes accessed | tf_op | source)
XLA Modules:
  0.0 124.7 jit_solution(2125831127928924860)
XLA Ops:
  0.6 7.7 %project.1 = (f32[256,128]{1,0:T(8,128)}, f32[8,256]{1,0:T(8,128)}) custom-call(s32[1,512]{1,0:T(1,128)} %bitcast.5, s32[1,512]{1,0:T(1,128)} %bitcast.7, s32[1,512]{1,0:T(1,128)} %bitcast.9, bf16[512,6656]{1,0:T(8,128)(2,1)} %refs_5_.3, f32[32,6656]{1,0:T(8,128)} %refs_6_.5, bf16[512,2048]{1,0:T(8,128)(2,1)} %refs_6_.4, f32[32,2048]{1,0:T(8,128)} %refs_9_.1), custom_call_target="tpu_custom_call" | custom-call | flops 2281701376 | bytes 10027008 | tf_op jit(solution)/shard_map/project/pallas_call | solution.py:77
  8.4 4.0 %collective-permute-start.5 = (f32[8,256]{1,0:T(8,128)}, f32[8,256]{1,0:T(8,128)S(1)}, u32[]{:S(2)}, u32[]{:S(2)}) collective-permute-start(f32[8,256]{1,0:T(8,128)} %get-tuple-element.40.refs_7_), channel_id=1, source_target_pairs={{0,24},{8,16},{16,8},{24,0},{1,25},{9,17},{17,9},{25,1},{2,26},{10... | collective-permute-start | bytes 24584 | tf_op jit(solution)/shard_map/ppermute | solution.py:326
  12.4 0.5 collective-permute-start.4
  12.9 0.1 collective-permute-start.3
  13.0 0.0 collective-permute-start
  13.0 0.9 copy-done.6
  13.9 9.2 %rollout31.1 = (bf16[512,512]{1,0:T(8,128)(2,1)S(1)}, bf16[6656,512]{1,0:T(8,128)(2,1)S(1)}) custom-call(bf16[512,6656]{1,0:T(8,128)(2,1)S(1)} %copy-done, bf16[6656,4096]{1,0:T(8,128)(2,1)} %refs_2_.13, f32[256,128]{1,0:T(8,128)S(1)} %copy-done.6), custom_call_target="tpu_custom_call" | custom-call | flops 3489660928 | bytes 54525952 | tf_op jit(solution)/shard_map/rollout31/pallas_call | solution.py:77
  23.1 0.6 collective-permute-start.6
  23.7 0.0 collective-permute-done.refs_1_
  23.7 2.0 %collective-permute-start.1 = (f32[256,128]{1,0:T(8,128)S(1)}, f32[256,128]{1,0:T(8,128)S(1)}, u32[]{:S(2)}, u32[]{:S(2)}) collective-permute-start(f32[256,128]{1,0:T(8,128)S(1)} %join.7.refs_3_.refs_0_), channel_id=1, source_target_pairs={{0,2},{1,3},{2,0},{3,1},{4,6},{5,7},{6,4},{7,5},{8,10},{9,11},{10,... | collective-permute-start | bytes 393224 | tf_op jit(solution)/shard_map/ppermute | solution.py:326
  25.7 6.6 %rollout30.1 = (f32[512,512]{1,0:T(8,128)S(1)}, bf16[6656,512]{1,0:T(8,128)(2,1)S(1)}) custom-call(bf16[512,6656]{1,0:T(8,128)(2,1)S(1)} %copy-done, bf16[6656,512]{1,0:T(8,128)(2,1)S(1)} %get-tuple-element.38.refs_1_, bf16[6656,4096]{1,0:T(8,128)(2,1)} %refs_2_.13, f32[256,128]{1,0:T(8,128)S(1)} %join.7.refs_3_.refs_0_), custom_call_target="tpu_custom_call" | custom-call | flops 3489660928 | bytes 54525952 | tf_op jit(solution)/shard_map/rollout30/pallas_call | solution.py:77
  32.4 2.7 %collective-permute-start.2 = (f32[256,128]{1,0:T(8,128)S(1)}, f32[256,128]{1,0:T(8,128)S(1)}, u32[]{:S(2)}, u32[]{:S(2)}) collective-permute-start(f32[256,128]{1,0:T(8,128)S(1)} %join.8.refs_3_), channel_id=1, source_target_pairs={{0,4},{1,5},{2,6},{3,7},{4,0},{5,1},{6,2},{7,3},{8,12},{9,13},{10,... | collective-permute-start | bytes 393224 | tf_op jit(solution)/shard_map/ppermute | solution.py:326
  35.0 0.0 copy-start.12
  35.1 0.0 copy-start.13
  35.1 6.1 %rollout21.1 = (bf16[512,512]{1,0:T(8,128)(2,1)S(1)}, bf16[6656,512]{1,0:T(8,128)(2,1)S(1)}) custom-call(bf16[512,6656]{1,0:T(8,128)(2,1)S(1)} %copy-done, bf16[6656,512]{1,0:T(8,128)(2,1)S(1)} %get-tuple-element.41.refs_1_, bf16[6656,4096]{1,0:T(8,128)(2,1)} %refs_2_.13, f32[256,128]{1,0:T(8,128)S(1)} %join.8.refs_3_), custom_call_target="tpu_custom_call" | custom-call | flops 3489660928 | bytes 54525952 | tf_op jit(solution)/shard_map/rollout21/pallas_call | solution.py:77
  41.2 0.1 collective-permute-start.10
  41.3 0.1 join.9.refs_11_
  41.4 0.5 collective-permute-start.11
  42.1 2.9 %gradient.1 = (f32[8,6656]{1,0:T(8,128)S(1)}, f32[32,2048]{1,0:T(8,128)S(1)}, bf16[16,7424]{1,0:T(8,128)(2,1)S(1)}, bf16[16,7424]{1,0:T(8,128)(2,1)S(1)}, bf16[16,7424]{1,0:T(8,128)(2,1)S(1)}) custom-call(s32[1,512]{1,0:T(1,128)S(1)} %bitcast.6, s32[1,512]{1,0:T(1,128)S(1)} %bitcast.8, s32[1,512]{1,0:T(1,128)S(1)} %bitcast.10, f32[256,128]{1,0:T(8,128)S(1)} %join.8.refs_3_, ...), custom_call_target="tpu_custom_call" | custom-call | flops 2281701376 | tf_op jit(solution)/shard_map/gradient/pallas_call | solution.py:77
  44.9 1.6 %collective-permute-start.7 = (bf16[16,7424]{1,0:T(8,128)(2,1)S(1)}, bf16[16,7424]{1,0:T(8,128)(2,1)S(1)}, u32[]{:S(2)}, u32[]{:S(2)}) collective-permute-start(bf16[16,7424]{1,0:T(8,128)(2,1)S(1)} %get-tuple-element.45), channel_id=1, source_target_pairs={{0,8},{8,0},{16,24},{24,16},{1,9},{9,1},{17,25},{25,17},{2,10},{10... | collective-permute-start | bytes 712712 | tf_op jit(solution)/shard_map/ppermute | solution.py:326
  46.5 1.5 %collective-permute-start.8 = (bf16[16,7424]{1,0:T(8,128)(2,1)S(1)}, bf16[16,7424]{1,0:T(8,128)(2,1)S(1)}, u32[]{:S(2)}, u32[]{:S(2)}) collective-permute-start(bf16[16,7424]{1,0:T(8,128)(2,1)S(1)} %get-tuple-element.46), channel_id=1, source_target_pairs={{0,16},{8,24},{16,0},{24,8},{1,17},{9,25},{17,1},{25,9},{2,18},{10... | collective-permute-start | bytes 712712 | tf_op jit(solution)/shard_map/ppermute | solution.py:326
  48.0 0.5 collective-permute-start.9
  48.5 0.0 copy-start.8
  48.5 0.0 copy-start.9
  48.5 6.6 %rollout20.1 = (f32[512,512]{1,0:T(8,128)S(1)}, bf16[6656,512]{1,0:T(8,128)(2,1)S(1)}) custom-call(bf16[512,6656]{1,0:T(8,128)(2,1)S(1)} %copy-done, bf16[6656,512]{1,0:T(8,128)(2,1)S(1)} %get-tuple-element.48.refs_1_, bf16[6656,4096]{1,0:T(8,128)(2,1)} %refs_2_.13, f32[8,6656]{1,0:T(8,128)S(1)} %get-tuple-element.43.refs_3_.refs_0_), custom_call_target="tpu_custom_call" | custom-call | flops 3489660928 | bytes 54525952 | tf_op jit(solution)/shard_map/rollout20/pallas_call | solution.py:77
  55.2 0.7 collective-permute-done.11.refs_2_
  55.8 0.2 join.10.refs_12_
  56.0 3.2 %collective-permute-done.8.refs_4_ = bf16[16,7424]{1,0:T(8,128)(2,1)S(1)} collective-permute-done((bf16[16,7424]{1,0:T(8,128)(2,1)S(1)}, bf16[16,7424]{1,0:T(8,128)(2,1)S(1)}, u32[]{:S(2)}, u32[]{:S(2)}) %collective-permute-start.8) | collective-permute-done | bytes 237600 | tf_op jit(solution)/shard_map/ppermute | solution.py:326
  59.2 4.2 %update.1 = (bf16[32,512]{1,0:T(8,128)(2,1)S(1)}, f32[8,512]{1,0:T(8,128)S(1)}, f32[8,6656]{1,0:T(8,128)}, f32[8,6656]{1,0:T(8,128)}, f32[8,6656]{1,0:T(8,128)},...) custom-call(f32[8,6656]{1,0:T(8,128)S(1)} %get-tuple-element.43.refs_3_.refs_0_, ...), custom_call_target="tpu_custom_call" | custom-call | flops 1744830464 | bytes 4177920 | tf_op jit(solution)/shard_map/update/pallas_call | solution.py:77
  63.4 6.1 %rollout11.1 = (bf16[512,512]{1,0:T(8,128)(2,1)S(1)}, bf16[6656,512]{1,0:T(8,128)(2,1)S(1)}) custom-call(bf16[512,6656]{1,0:T(8,128)(2,1)S(1)} %copy-done, bf16[6656,512]{1,0:T(8,128)(2,1)S(1)} %get-tuple-element.52.refs_1_, bf16[6656,4096]{1,0:T(8,128)(2,1)} %refs_2_.13, f32[8,512]{1,0:T(8,128)S(1)} %get-tuple-element.51.refs_3_.refs_0_), custom_call_target="tpu_custom_call" | custom-call | flops 3489660928 | bytes 54525952 | tf_op jit(solution)/shard_map/rollout11/pallas_call | solution.py:77
  69.6 0.1 collective-permute-start.15
  69.7 1.3 %collective-permute-start.13 = (f32[8,512]{1,0:T(8,128)S(1)}, f32[8,512]{1,0:T(8,128)S(1)}, u32[]{:S(2)}, u32[]{:S(2)}) collective-permute-start(f32[8,512]{1,0:T(8,128)S(1)} %get-tuple-element.51.refs_3_.refs_0_), channel_id=1, source_target_pairs={{0,8},{8,0},{16,24},{24,16},{1,9},{9,1},{17,25},{25,17},{2,10},{10... | collective-permute-start | bytes 49160 | tf_op jit(solution)/shard_map/ppermute | solution.py:326
  70.9 0.3 collective-permute-start.21
  71.3 0.7 collective-permute-start.12
  71.9 1.5 %collective-permute-done.13.refs_1_ = f32[8,512]{1,0:T(8,128)S(1)} collective-permute-done((f32[8,512]{1,0:T(8,128)S(1)}, f32[8,512]{1,0:T(8,128)S(1)}, u32[]{:S(2)}, u32[]{:S(2)}) %collective-permute-start.13) | collective-permute-done | bytes 16416 | tf_op jit(solution)/shard_map/ppermute | solution.py:326
  73.5 2.9 %collective-permute-start.14 = (f32[16,512]{1,0:T(8,128)S(1)}, f32[16,512]{1,0:T(8,128)S(1)}, u32[]{:S(2)}, u32[]{:S(2)}) collective-permute-start(f32[16,512]{1,0:T(8,128)S(1)} %gather.2.refs_3_.refs_0_), channel_id=1, source_target_pairs={{0,16},{8,24},{16,0},{24,8},{1,17},{9,25},{17,1},{25,9},{2,18},{10... | collective-permute-start | bytes 98312 | tf_op jit(solution)/shard_map/ppermute | solution.py:326
  76.3 6.6 %rollout10.1 = (f32[512,512]{1,0:T(8,128)S(1)}, bf16[6656,512]{1,0:T(8,128)(2,1)S(1)}) custom-call(bf16[512,6656]{1,0:T(8,128)(2,1)S(1)} %copy-done, bf16[6656,512]{1,0:T(8,128)(2,1)S(1)} %get-tuple-element.54.refs_1_, bf16[6656,4096]{1,0:T(8,128)(2,1)} %refs_2_.13, f32[16,512]{1,0:T(8,128)S(1)} %gather.2.refs_3_.refs_0_), custom_call_target="tpu_custom_call" | custom-call | flops 3489660928 | bytes 54525952 | tf_op jit(solution)/shard_map/rollout10/pallas_call | solution.py:77
  82.9 0.1 join.11.refs_2_
  83.1 6.6 %rollout01.1 = (bf16[512,512]{1,0:T(8,128)(2,1)S(1)}, bf16[6656,512]{1,0:T(8,128)(2,1)S(1)}) custom-call(bf16[512,6656]{1,0:T(8,128)(2,1)S(1)} %copy-done, bf16[6656,512]{1,0:T(8,128)(2,1)S(1)} %get-tuple-element.56.refs_1_, bf16[6656,4096]{1,0:T(8,128)(2,1)} %refs_2_.13, f32[32,512]{1,0:T(8,128)S(1)} %gather.3.refs_3_.refs_0_), custom_call_target="tpu_custom_call" | custom-call | flops 3489660928 | bytes 54525952 | tf_op jit(solution)/shard_map/rollout01/pallas_call | solution.py:77
  89.7 1.9 %collective-permute-start.19 = (bf16[512,512]{1,0:T(8,128)(2,1)S(1)}, bf16[512,512]{1,0:T(8,128)(2,1)S(1)}, u32[]{:S(2)}, u32[]{:S(2)}) collective-permute-start(bf16[512,512]{1,0:T(8,128)(2,1)S(1)} %get-tuple-element.57.refs_2_), channel_id=1, source_target_pairs={{0,1},{1,0},{2,3},{3,2},{4,5},{5,4},{6,7},{7,6},{8,9},{9,8},{10,11... | collective-permute-start | bytes 1572872 | tf_op jit(solution)/shard_map/ppermute | solution.py:326
  91.7 11.4 %collective-permute-start.20 = (bf16[512,512]{1,0:T(8,128)(2,1)S(1)}, bf16[512,512]{1,0:T(8,128)(2,1)S(1)}, u32[]{:S(2)}, u32[]{:S(2)}) collective-permute-start(bf16[512,512]{1,0:T(8,128)(2,1)S(1)} %join.11.refs_2_), channel_id=1, source_target_pairs={{0,2},{1,3},{2,0},{3,1},{4,6},{5,7},{6,4},{7,5},{8,10},{9,11},{10,... | collective-permute-start | bytes 1572872 | tf_op jit(solution)/shard_map/ppermute | solution.py:326
  103.0 1.3 %collective-permute-done.16.refs_1_ = f32[32,512]{1,0:T(8,128)S(1)} collective-permute-done((f32[32,512]{1,0:T(8,128)S(1)}, f32[32,512]{1,0:T(8,128)S(1)}, u32[]{:S(2)}, u32[]{:S(2)}) %collective-permute-start.16) | collective-permute-done | bytes 65568 | tf_op jit(solution)/shard_map/ppermute | solution.py:326
  104.3 0.5 collective-permute-start.17
  104.8 3.7 %rollout00.1.refs_2_.refs_3_ = f32[512,512]{1,0:T(8,128)S(1)} custom-call(bf16[512,6656]{1,0:T(8,128)(2,1)S(1)} %copy-done, bf16[6656,512]{1,0:T(8,128)(2,1)S(1)} %get-tuple-element.58.refs_1_, f32[32,512]{1,0:T(8,128)S(1)} %join.12.refs_2_.refs_0_), custom_call_target="tpu_custom_call" | custom-call | flops 3489660928 | tf_op jit(solution)/shard_map/rollout00/pallas_call | solution.py:77
  108.4 8.2 %collective-permute-done.17.refs_1_ = f32[32,512]{1,0:T(8,128)S(1)} collective-permute-done((f32[32,512]{1,0:T(8,128)S(1)}, f32[32,512]{1,0:T(8,128)S(1)}, u32[]{:S(2)}, u32[]{:S(2)}) %collective-permute-start.17) | collective-permute-done | bytes 65568 | tf_op jit(solution)/shard_map/ppermute | solution.py:326
  116.6 3.3 %collective-permute-start.18 = (f32[32,512]{1,0:T(8,128)S(1)}, f32[32,512]{1,0:T(8,128)S(1)}, u32[]{:S(2)}, u32[]{:S(2)}) collective-permute-start(f32[32,512]{1,0:T(8,128)S(1)} %join.13.refs_1_), channel_id=1, source_target_pairs={{0,4},{1,5},{2,6},{3,7},{4,0},{5,1},{6,2},{7,3},{8,12},{9,13},{10,... | collective-permute-start | bytes 196616 | tf_op jit(solution)/shard_map/ppermute | solution.py:326
  119.9 3.3 %collective-permute-done.18.refs_2_ = f32[32,512]{1,0:T(8,128)S(1)} collective-permute-done((f32[32,512]{1,0:T(8,128)S(1)}, f32[32,512]{1,0:T(8,128)S(1)}, u32[]{:S(2)}, u32[]{:S(2)}) %collective-permute-start.18) | collective-permute-done | bytes 65568 | tf_op jit(solution)/shard_map/ppermute | solution.py:326
  123.2 1.3 %finish.1 = bf16[512,512]{1,0:T(8,128)(2,1)} custom-call(bf16[32,512]{1,0:T(8,128)(2,1)S(1)} %collective-permute-done.12.refs_3_.refs_0_, f32[32,512]{1,0:T(8,128)S(1)} %join.13.refs_1_, f32[32,512]{1,0:T(8,128)S(1)} %collective-permute-done.18.refs_2_, f32[512,512]{1,0:T(8,128)S(1)} %rollout00.1.refs_2_.refs_3_, ...), custom_call_target="tpu_custom_call" | custom-call | flops 134217728 | bytes 524288 | tf_op jit(solution)/shard_map/finish/pallas_call | solution.py:77
  (50 shorter events, 0.2 us)
Async XLA Ops:
  0.6 12.4 %copy-start = (bf16[512,6656]{1,0:T(8,128)(2,1)S(1)}, bf16[512,6656]{1,0:T(8,128)(2,1)}, u32[]{:S(2)}) copy-start(bf16[512,6656]{1,0:T(8,128)(2,1)} %refs_0_.15) | copy-start | bytes 20447236
  8.4 33.0 %collective-permute-start.5 = (f32[8,256]{1,0:T(8,128)}, f32[8,256]{1,0:T(8,128)S(1)}, u32[]{:S(2)}, u32[]{:S(2)}) collective-permute-start(f32[8,256]{1,0:T(8,128)} %get-tuple-element.40.refs_7_), channel_id=1, source_target_pairs={{0,24},{8,16},{16,8},{24,0},{1,25},{9,17},{17,9},{25,1},{2,26},{10... | collective-permute-start | bytes 24584 | tf_op jit(solution)/shard_map/ppermute | solution.py:326
  12.4 29.6 %collective-permute-start.4 = (f32[8,256]{1,0:T(8,128)}, f32[8,256]{1,0:T(8,128)S(1)}, u32[]{:S(2)}, u32[]{:S(2)}) collective-permute-start(f32[8,256]{1,0:T(8,128)} %get-tuple-element.40.refs_7_), channel_id=1, source_target_pairs={{0,16},{8,24},{16,0},{24,8},{1,17},{9,25},{17,1},{25,9},{2,18},{10... | collective-permute-start | bytes 24584 | tf_op jit(solution)/shard_map/ppermute | solution.py:326
  12.9 29.1 %collective-permute-start.3 = (f32[8,256]{1,0:T(8,128)}, f32[8,256]{1,0:T(8,128)S(1)}, u32[]{:S(2)}, u32[]{:S(2)}) collective-permute-start(f32[8,256]{1,0:T(8,128)} %get-tuple-element.40.refs_7_), channel_id=1, source_target_pairs={{0,8},{8,0},{16,24},{24,16},{1,9},{9,1},{17,25},{25,17},{2,10},{10... | collective-permute-start | bytes 24584 | tf_op jit(solution)/shard_map/ppermute | solution.py:326
  13.0 10.7 %collective-permute-start = (f32[256,128]{1,0:T(8,128)}, f32[256,128]{1,0:T(8,128)S(1)}, u32[]{:S(2)}, u32[]{:S(2)}) collective-permute-start(f32[256,128]{1,0:T(8,128)} %get-tuple-element.36.refs_2_.refs_0_), channel_id=1, source_target_pairs={{0,1},{1,0},{2,3},{3,2},{4,5},{5,4},{6,7},{7,6},{8,9},{9,8},{10,11... | collective-permute-start | bytes 393224 | tf_op jit(solution)/shard_map/ppermute | solution.py:326
  13.0 0.9 copy-start.6
  13.9 9.8 %copy-start.7 = (f32[256,128]{1,0:T(8,128)S(1)}, f32[256,128]{1,0:T(8,128)}, u32[]{:S(2)}) copy-start(f32[256,128]{1,0:T(8,128)} %get-tuple-element.36.refs_2_.refs_0_) | copy-start | bytes 393220
  23.1 18.1 %collective-permute-start.6 = (bf16[512,512]{1,0:T(8,128)(2,1)S(1)}, bf16[512,512]{1,0:T(8,128)(2,1)S(1)}, u32[]{:S(2)}, u32[]{:S(2)}) collective-permute-start(bf16[512,512]{1,0:T(8,128)(2,1)S(1)} %get-tuple-element.37.refs_2_), channel_id=1, source_target_pairs={{0,1},{1,0},{2,3},{3,2},{4,5},{5,4},{6,7},{7,6},{8,9},{9,8},{10,11... | collective-permute-start | bytes 1572872 | tf_op jit(solution)/shard_map/ppermute | solution.py:326
  23.7 8.7 %collective-permute-start.1 = (f32[256,128]{1,0:T(8,128)S(1)}, f32[256,128]{1,0:T(8,128)S(1)}, u32[]{:S(2)}, u32[]{:S(2)}) collective-permute-start(f32[256,128]{1,0:T(8,128)S(1)} %join.7.refs_3_.refs_0_), channel_id=1, source_target_pairs={{0,2},{1,3},{2,0},{3,1},{4,6},{5,7},{6,4},{7,5},{8,10},{9,11},{10,... | collective-permute-start | bytes 393224 | tf_op jit(solution)/shard_map/ppermute | solution.py:326
  25.7 16.2 %slice-start = ((s8[6815744]{0:T(1024)(128)(4,1)}), s8[2621440]{0:T(1024)(128)(4,1)S(1)}, s32[]{:S(2)}) async-start(s8[6815744]{0:T(1024)(128)(4,1)} %bitcast.3), calls=%async_computation | async-start | bytes 5242880
  32.4 9.6 %collective-permute-start.2 = (f32[256,128]{1,0:T(8,128)S(1)}, f32[256,128]{1,0:T(8,128)S(1)}, u32[]{:S(2)}, u32[]{:S(2)}) collective-permute-start(f32[256,128]{1,0:T(8,128)S(1)} %join.8.refs_3_), channel_id=1, source_target_pairs={{0,4},{1,5},{2,6},{3,7},{4,0},{5,1},{6,2},{7,3},{8,12},{9,13},{10,... | collective-permute-start | bytes 393224 | tf_op jit(solution)/shard_map/ppermute | solution.py:326
  35.0 6.9 %slice-start.1 = ((s8[6815744]{0:T(1024)(128)(4,1)}), s8[4194304]{0:T(1024)(128)(4,1)S(1)}, s32[]{:S(2)}) async-start(s8[6815744]{0:T(1024)(128)(4,1)} %bitcast.3), calls=%async_computation.1 | async-start | bytes 8388608
  35.0 7.0 %copy-start.1 = (bf16[512,2048]{1,0:T(8,128)(2,1)S(1)}, bf16[512,2048]{1,0:T(8,128)(2,1)}, u32[]{:S(2)}) copy-start(bf16[512,2048]{1,0:T(8,128)(2,1)} %refs_6_.4) | copy-start | bytes 6291460
  35.0 7.0 %copy-start.10 = (f32[8,256]{1,0:T(8,128)S(1)}, f32[8,256]{1,0:T(8,128)}, u32[]{:S(2)}) copy-start(f32[8,256]{1,0:T(8,128)} %get-tuple-element.40.refs_7_) | copy-start | bytes 24580
  35.0 7.0 %copy-start.11 = (s32[512]{0:T(512)S(1)}, s32[512]{0:T(512)}, u32[]{:S(2)}) copy-start(s32[512]{0:T(512)} %param.15) | copy-start | bytes 6148
  35.0 7.0 %copy-start.12 = (s32[512]{0:T(512)S(1)}, s32[512]{0:T(512)}, u32[]{:S(2)}) copy-start(s32[512]{0:T(512)} %param.16) | copy-start | bytes 6148
  35.1 7.0 %copy-start.13 = (s32[512]{0:T(512)S(1)}, s32[512]{0:T(512)}, u32[]{:S(2)}) copy-start(s32[512]{0:T(512)} %param.17) | copy-start | bytes 6148
  41.2 13.9 %collective-permute-start.10 = (bf16[512,512]{1,0:T(8,128)(2,1)S(1)}, bf16[512,512]{1,0:T(8,128)(2,1)S(1)}, u32[]{:S(2)}, u32[]{:S(2)}) collective-permute-start(bf16[512,512]{1,0:T(8,128)(2,1)S(1)} %get-tuple-element.42.refs_2_), channel_id=1, source_target_pairs={{0,1},{1,0},{2,3},{3,2},{4,5},{5,4},{6,7},{7,6},{8,9},{9,8},{10,11... | collective-permute-start | bytes 1572872 | tf_op jit(solution)/shard_map/ppermute | solution.py:326
  41.4 14.4 %collective-permute-start.11 = (bf16[512,512]{1,0:T(8,128)(2,1)S(1)}, bf16[512,512]{1,0:T(8,128)(2,1)S(1)}, u32[]{:S(2)}, u32[]{:S(2)}) collective-permute-start(bf16[512,512]{1,0:T(8,128)(2,1)S(1)} %join.9.refs_11_), channel_id=1, source_target_pairs={{0,2},{1,3},{2,0},{3,1},{4,6},{5,7},{6,4},{7,5},{8,10},{9,11},{10,... | collective-permute-start | bytes 1572872 | tf_op jit(solution)/shard_map/ppermute | solution.py:326
  44.9 11.1 %collective-permute-start.7 = (bf16[16,7424]{1,0:T(8,128)(2,1)S(1)}, bf16[16,7424]{1,0:T(8,128)(2,1)S(1)}, u32[]{:S(2)}, u32[]{:S(2)}) collective-permute-start(bf16[16,7424]{1,0:T(8,128)(2,1)S(1)} %get-tuple-element.45), channel_id=1, source_target_pairs={{0,8},{8,0},{16,24},{24,16},{1,9},{9,1},{17,25},{25,17},{2,10},{10... | collective-permute-start | bytes 712712 | tf_op jit(solution)/shard_map/ppermute | solution.py:326
  46.5 12.7 %collective-permute-start.8 = (bf16[16,7424]{1,0:T(8,128)(2,1)S(1)}, bf16[16,7424]{1,0:T(8,128)(2,1)S(1)}, u32[]{:S(2)}, u32[]{:S(2)}) collective-permute-start(bf16[16,7424]{1,0:T(8,128)(2,1)S(1)} %get-tuple-element.46), channel_id=1, source_target_pairs={{0,16},{8,24},{16,0},{24,8},{1,17},{9,25},{17,1},{25,9},{2,18},{10... | collective-permute-start | bytes 712712 | tf_op jit(solution)/shard_map/ppermute | solution.py:326
  48.0 11.2 %collective-permute-start.9 = (bf16[16,7424]{1,0:T(8,128)(2,1)S(1)}, bf16[16,7424]{1,0:T(8,128)(2,1)S(1)}, u32[]{:S(2)}, u32[]{:S(2)}) collective-permute-start(bf16[16,7424]{1,0:T(8,128)(2,1)S(1)} %get-tuple-element.47), channel_id=1, source_target_pairs={{0,24},{8,16},{16,8},{24,0},{1,25},{9,17},{17,9},{25,1},{2,26},{10... | collective-permute-start | bytes 712712 | tf_op jit(solution)/shard_map/ppermute | solution.py:326
  48.5 10.7 %copy-start.2 = (f32[32,6656]{1,0:T(8,128)S(1)}, f32[32,6656]{1,0:T(8,128)}, u32[]{:S(2)}) copy-start(f32[32,6656]{1,0:T(8,128)} %refs_6_.5) | copy-start | bytes 2555908
  48.5 10.7 %copy-start.3 = (f32[32,2048]{1,0:T(8,128)S(1)}, f32[32,2048]{1,0:T(8,128)}, u32[]{:S(2)}) copy-start(f32[32,2048]{1,0:T(8,128)} %refs_9_.1) | copy-start | bytes 786436
  48.5 10.7 %copy-start.4 = (f32[32,6656]{1,0:T(8,128)S(1)}, f32[32,6656]{1,0:T(8,128)}, u32[]{:S(2)}) copy-start(f32[32,6656]{1,0:T(8,128)} %refs_7_.1) | copy-start | bytes 2555908
  48.5 10.7 %copy-start.5 = (f32[32,6656]{1,0:T(8,128)S(1)}, f32[32,6656]{1,0:T(8,128)}, u32[]{:S(2)}) copy-start(f32[32,6656]{1,0:T(8,128)} %refs_8_.1) | copy-start | bytes 2555908
  48.5 10.7 %copy-start.8 = (f32[32,2048]{1,0:T(8,128)S(1)}, f32[32,2048]{1,0:T(8,128)}, u32[]{:S(2)}) copy-start(f32[32,2048]{1,0:T(8,128)} %refs_10_.1) | copy-start | bytes 786436
  48.5 10.7 %copy-start.9 = (f32[32,2048]{1,0:T(8,128)S(1)}, f32[32,2048]{1,0:T(8,128)}, u32[]{:S(2)}) copy-start(f32[32,2048]{1,0:T(8,128)} %refs_11_.1) | copy-start | bytes 786436
  69.6 13.4 %collective-permute-start.15 = (bf16[512,512]{1,0:T(8,128)(2,1)S(1)}, bf16[512,512]{1,0:T(8,128)(2,1)S(1)}, u32[]{:S(2)}, u32[]{:S(2)}) collective-permute-start(bf16[512,512]{1,0:T(8,128)(2,1)S(1)} %get-tuple-element.53.refs_2_), channel_id=1, source_target_pairs={{0,1},{1,0},{2,3},{3,2},{4,5},{5,4},{6,7},{7,6},{8,9},{9,8},{10,11... | collective-permute-start | bytes 1572872 | tf_op jit(solution)/shard_map/ppermute | solution.py:326
  69.7 3.8 %collective-permute-start.13 = (f32[8,512]{1,0:T(8,128)S(1)}, f32[8,512]{1,0:T(8,128)S(1)}, u32[]{:S(2)}, u32[]{:S(2)}) collective-permute-start(f32[8,512]{1,0:T(8,128)S(1)} %get-tuple-element.51.refs_3_.refs_0_), channel_id=1, source_target_pairs={{0,8},{8,0},{16,24},{24,16},{1,9},{9,1},{17,25},{25,17},{2,10},{10... | collective-permute-start | bytes 49160 | tf_op jit(solution)/shard_map/ppermute | solution.py:326
  70.9 48.9 %collective-permute-start.21 = (bf16[512,512]{1,0:T(8,128)(2,1)S(1)}, bf16[512,512]{1,0:T(8,128)(2,1)S(1)}, u32[]{:S(2)}, u32[]{:S(2)}) collective-permute-start(bf16[512,512]{1,0:T(8,128)(2,1)S(1)} %join.10.refs_12_), channel_id=1, source_target_pairs={{0,4},{1,5},{2,6},{3,7},{4,0},{5,1},{6,2},{7,3},{8,12},{9,13},{10,... | collective-permute-start | bytes 1572872 | tf_op jit(solution)/shard_map/ppermute | solution.py:326
  71.3 11.8 %collective-permute-start.12 = (bf16[32,512]{1,0:T(8,128)(2,1)S(1)}, bf16[32,512]{1,0:T(8,128)(2,1)S(1)}, u32[]{:S(2)}, u32[]{:S(2)}) collective-permute-start(bf16[32,512]{1,0:T(8,128)(2,1)S(1)} %get-tuple-element.50), channel_id=1, source_target_pairs={{0,0},{1,4},{2,8},{3,12},{4,16},{5,20},{6,24},{7,28},{8,1},{9,5},{... | collective-permute-start | bytes 98312 | tf_op jit(solution)/shard_map/ppermute | solution.py:451
  73.5 9.6 %collective-permute-start.14 = (f32[16,512]{1,0:T(8,128)S(1)}, f32[16,512]{1,0:T(8,128)S(1)}, u32[]{:S(2)}, u32[]{:S(2)}) collective-permute-start(f32[16,512]{1,0:T(8,128)S(1)} %gather.2.refs_3_.refs_0_), channel_id=1, source_target_pairs={{0,16},{8,24},{16,0},{24,8},{1,17},{9,25},{17,1},{25,9},{2,18},{10... | collective-permute-start | bytes 98312 | tf_op jit(solution)/shard_map/ppermute | solution.py:326
  89.7 33.5 %collective-permute-start.19 = (bf16[512,512]{1,0:T(8,128)(2,1)S(1)}, bf16[512,512]{1,0:T(8,128)(2,1)S(1)}, u32[]{:S(2)}, u32[]{:S(2)}) collective-permute-start(bf16[512,512]{1,0:T(8,128)(2,1)S(1)} %get-tuple-element.57.refs_2_), channel_id=1, source_target_pairs={{0,1},{1,0},{2,3},{3,2},{4,5},{5,4},{6,7},{7,6},{8,9},{9,8},{10,11... | collective-permute-start | bytes 1572872 | tf_op jit(solution)/shard_map/ppermute | solution.py:326
  91.7 31.6 %collective-permute-start.20 = (bf16[512,512]{1,0:T(8,128)(2,1)S(1)}, bf16[512,512]{1,0:T(8,128)(2,1)S(1)}, u32[]{:S(2)}, u32[]{:S(2)}) collective-permute-start(bf16[512,512]{1,0:T(8,128)(2,1)S(1)} %join.11.refs_2_), channel_id=1, source_target_pairs={{0,2},{1,3},{2,0},{3,1},{4,6},{5,7},{6,4},{7,5},{8,10},{9,11},{10,... | collective-permute-start | bytes 1572872 | tf_op jit(solution)/shard_map/ppermute | solution.py:326
  103.0 1.3 %collective-permute-start.16 = (f32[32,512]{1,0:T(8,128)S(1)}, f32[32,512]{1,0:T(8,128)S(1)}, u32[]{:S(2)}, u32[]{:S(2)}) collective-permute-start(f32[32,512]{1,0:T(8,128)S(1)} %gather.3.refs_3_.refs_0_), channel_id=1, source_target_pairs={{0,1},{1,0},{2,3},{3,2},{4,5},{5,4},{6,7},{7,6},{8,9},{9,8},{10,11... | collective-permute-start | bytes 196616 | tf_op jit(solution)/shard_map/ppermute | solution.py:326
  104.3 12.3 %collective-permute-start.17 = (f32[32,512]{1,0:T(8,128)S(1)}, f32[32,512]{1,0:T(8,128)S(1)}, u32[]{:S(2)}, u32[]{:S(2)}) collective-permute-start(f32[32,512]{1,0:T(8,128)S(1)} %join.12.refs_2_.refs_0_), channel_id=1, source_target_pairs={{0,2},{1,3},{2,0},{3,1},{4,6},{5,7},{6,4},{7,5},{8,10},{9,11},{10,... | collective-permute-start | bytes 196616 | tf_op jit(solution)/shard_map/ppermute | solution.py:326
  116.6 6.6 %collective-permute-start.18 = (f32[32,512]{1,0:T(8,128)S(1)}, f32[32,512]{1,0:T(8,128)S(1)}, u32[]{:S(2)}, u32[]{:S(2)}) collective-permute-start(f32[32,512]{1,0:T(8,128)S(1)} %join.13.refs_1_), channel_id=1, source_target_pairs={{0,4},{1,5},{2,6},{3,7},{4,0},{5,1},{6,2},{7,3},{8,12},{9,13},{10,... | collective-permute-start | bytes 196616 | tf_op jit(solution)/shard_map/ppermute | solution.py:326

commit v4 on v3

--- a/solution.py
+++ b/solution.py
@@ -243,27 +243,24 @@
         given, w, out, after, arrived = rest
     me = lax.axis_index("tensor")
     width = out.shape[1]
-    parts = 4
-    height = x.shape[1] // parts
-
-    def fetch(differs, held, row):
+
+    def fetch(differs, held, at):
         start = pl.multiple_of(lax.bitwise_xor(me, differs) * width, width)
-        copies = []
-        for at in range(parts):
-            rows = slice(at * height, (at + 1) * height)
-            source = w.at[rows, pl.ds(start, width)]
-            copies.append(pltpu.make_async_copy(source, held.at[rows, :], arrived.at[row, at]))
-        for copy in copies:
-            copy.start()
-        return copies
+        return pltpu.make_async_copy(w.at[:, pl.ds(start, width)], held, arrived.at[at])
 
     if first:
-        for copy in fetch(differs, given, 0):
-            copy.wait()
-    copies = [] if following is None else fetch(following, after, 1)
-    out[...] = dot(x[...], given[...]).astype(out.dtype)
-    for copy in copies:
-        copy.wait()
+        own = fetch(differs, given, 0)
+        own.start()
+        own.wait()
+    if following is not None:
+        fetch(following, after, 1).start()
+
+    @pl.when(me >= 0)
+    def _():
+        out[...] = dot(x[...], given[...]).astype(out.dtype)
+
+    if following is not None:
+        fetch(following, after, 1).wait()
 
 
 def gather_kernel(bit, mine, arrived, out):
@@ -351,7 +348,7 @@
                 outputs + ([] if following is None else [block]),
                 [],
                 ([pltpu.VMEM(block.shape, BF16)] if first else [])
-                + ([] if following is None else [pltpu.SemaphoreType.DMA((2, 4))]),
+                + ([] if following is None else [pltpu.SemaphoreType.DMA((2,))]),
                 2 * rollout * inner * own_width,
                 12,
                 after,
@@ -454,8 +451,6 @@
         received = xor(product, 1 << at, "dp")
         if at < 2:
             after = form(1, after)
-            if at:
-                after = send_on(after)
         if at == replicas.bit_length() - 2:
             after = after + [factor]
         both = shape((2 * product.shape[0], rollout), F32)
@@ -470,6 +465,8 @@
         if at < len(tensor_bits) - 1:
             product = add([product, received], after)
             after = [product]
+        if at == 0:
+            after = send_on(after)
     waiting.remove(0)
     send_on(after)
 

time: 126 us -> 102 us (0.81)
  Pallas kernels: 68.1 us -> 49.1 us
  starting transfers between devices: 36.2 us -> 28.4 us
  waiting for transfers between devices: 18.2 us -> 20 us
    pallas_call x21, Pallas kernels: 68.1 us -> 49.1 us  [call(): pl.pallas_call(body, name=name, out_shape=[*outputs, *far_outputs], in_sp...]
    ppermute x21, starting transfers between devices: 35.6 us -> 27.7 us  [xor(): lax.ppermute(array, axis, [(i, i ^ k) for i in range(lax.axis_size(axis))])]
    ppermute x21, waiting for transfers between devices: 18.2 us -> 20 us  [xor(): lax.ppermute(array, axis, [(i, i ^ k) for i in range(lax.axis_size(axis))])]
  transfers between devices with their start and end apart: 22 -> 22, of which waited for: 6 -> 5; matrix products, arithmetic and copies ran while one was open for 0% -> 0% of each run, Pallas kernels for 39% -> 40%
where the time goes in v4:
time: 102 us; the launch traced here: 99.5 us
  Pallas kernels  49.1 us (48%)
  starting transfers between devices  28.4 us (28%)
  waiting for transfers between devices  20 us (20%)
  between operations  1.14 us (1%)
    pallas_call x21, Pallas kernels, call(): pl.pallas_call(body, name=name, out_shape=[*outputs, *far_outputs], in_sp...  49.1 us
    ppermute x21, starting transfers between devices, xor(): lax.ppermute(array, axis, [(i, i ^ k) for i in range(lax.axis_size(axis))])  27.7 us
    ppermute x21, waiting for transfers between devices, xor(): lax.ppermute(array, axis, [(i, i ^ k) for i in range(lax.axis_size(axis))])  20 us
  transfers between devices with their start and end apart: 22, of which 5 were waited for; matrix products, arithmetic and copies ran while one was open for 0% of the time, Pallas kernels for 40%

profile of v4, /device:TPU:0, one launch (start us, length us, event | category | flops | bytes accessed | tf_op | source)
XLA Modules:
  0.0 99.5 jit_solution(5265083429887687925)
XLA Ops:
  0.6 7.7 %project.1 = (f32[256,128]{1,0:T(8,128)}, f32[8,256]{1,0:T(8,128)}) custom-call(s32[1,512]{1,0:T(1,128)} %bitcast.5, s32[1,512]{1,0:T(1,128)} %bitcast.7, s32[1,512]{1,0:T(1,128)} %bitcast.9, bf16[512,6656]{1,0:T(8,128)(2,1)} %refs_5_.3, f32[32,6656]{1,0:T(8,128)} %refs_6_.5, bf16[512,2048]{1,0:T(8,128)(2,1)} %refs_6_.4, f32[32,2048]{1,0:T(8,128)} %refs_9_.1), custom_call_target="tpu_custom_call" | custom-call | flops 2281701376 | bytes 10027008 | tf_op jit(solution)/shard_map/project/pallas_call | solution.py:77
  8.4 3.0 %collective-permute-start.3 = (f32[8,256]{1,0:T(8,128)}, f32[8,256]{1,0:T(8,128)S(1)}, u32[]{:S(2)}, u32[]{:S(2)}) collective-permute-start(f32[8,256]{1,0:T(8,128)} %get-tuple-element.40.refs_7_), channel_id=1, source_target_pairs={{0,8},{8,0},{16,24},{24,16},{1,9},{9,1},{17,25},{25,17},{2,10},{10... | collective-permute-start | bytes 24584 | tf_op jit(solution)/shard_map/ppermute | solution.py:323
  11.4 1.5 %collective-permute-start.4 = (f32[8,256]{1,0:T(8,128)}, f32[8,256]{1,0:T(8,128)S(1)}, u32[]{:S(2)}, u32[]{:S(2)}) collective-permute-start(f32[8,256]{1,0:T(8,128)} %get-tuple-element.40.refs_7_), channel_id=1, source_target_pairs={{0,16},{8,24},{16,0},{24,8},{1,17},{9,25},{17,1},{25,9},{2,18},{10... | collective-permute-start | bytes 24584 | tf_op jit(solution)/shard_map/ppermute | solution.py:323
  12.9 0.0 collective-permute-start.5
  13.0 0.9 copy-done.6
  13.9 6.7 %rollout31.1 = (bf16[512,512]{1,0:T(8,128)(2,1)S(1)}, bf16[6656,512]{1,0:T(8,128)(2,1)S(1)}) custom-call(bf16[512,6656]{1,0:T(8,128)(2,1)S(1)} %copy-done, bf16[6656,4096]{1,0:T(8,128)(2,1)} %refs_2_.13, f32[256,128]{1,0:T(8,128)S(1)} %copy-done.6), custom_call_target="tpu_custom_call" | custom-call | flops 3489660928 | bytes 54525952 | tf_op jit(solution)/shard_map/rollout31/pallas_call | solution.py:77
  20.5 0.6 collective-permute-start.6
  21.1 0.0 collective-permute-done.refs_1_
  21.1 2.1 %collective-permute-start.1 = (f32[256,128]{1,0:T(8,128)S(1)}, f32[256,128]{1,0:T(8,128)S(1)}, u32[]{:S(2)}, u32[]{:S(2)}) collective-permute-start(f32[256,128]{1,0:T(8,128)S(1)} %join.7.refs_3_.refs_0_), channel_id=1, source_target_pairs={{0,2},{1,3},{2,0},{3,1},{4,6},{5,7},{6,4},{7,5},{8,10},{9,11},{10,... | collective-permute-start | bytes 393224 | tf_op jit(solution)/shard_map/ppermute | solution.py:323
  23.2 3.7 %rollout30.1 = (f32[512,512]{1,0:T(8,128)S(1)}, bf16[6656,512]{1,0:T(8,128)(2,1)S(1)}) custom-call(bf16[512,6656]{1,0:T(8,128)(2,1)S(1)} %copy-done, bf16[6656,512]{1,0:T(8,128)(2,1)S(1)} %get-tuple-element.38.refs_1_, bf16[6656,4096]{1,0:T(8,128)(2,1)} %refs_2_.13, f32[256,128]{1,0:T(8,128)S(1)} %join.7.refs_3_.refs_0_), custom_call_target="tpu_custom_call" | custom-call | flops 3489660928 | bytes 54525952 | tf_op jit(solution)/shard_map/rollout30/pallas_call | solution.py:77
  27.0 2.8 %collective-permute-start.2 = (f32[256,128]{1,0:T(8,128)S(1)}, f32[256,128]{1,0:T(8,128)S(1)}, u32[]{:S(2)}, u32[]{:S(2)}) collective-permute-start(f32[256,128]{1,0:T(8,128)S(1)} %join.8.refs_3_), channel_id=1, source_target_pairs={{0,4},{1,5},{2,6},{3,7},{4,0},{5,1},{6,2},{7,3},{8,12},{9,13},{10,... | collective-permute-start | bytes 393224 | tf_op jit(solution)/shard_map/ppermute | solution.py:323
  29.8 0.0 copy-start.12
  29.8 0.0 copy-start.13
  29.8 3.7 %rollout21.1 = (bf16[512,512]{1,0:T(8,128)(2,1)S(1)}, bf16[6656,512]{1,0:T(8,128)(2,1)S(1)}) custom-call(bf16[512,6656]{1,0:T(8,128)(2,1)S(1)} %copy-done, bf16[6656,512]{1,0:T(8,128)(2,1)S(1)} %get-tuple-element.41.refs_1_, bf16[6656,4096]{1,0:T(8,128)(2,1)} %refs_2_.13, f32[256,128]{1,0:T(8,128)S(1)} %join.8.refs_3_), custom_call_target="tpu_custom_call" | custom-call | flops 3489660928 | bytes 54525952 | tf_op jit(solution)/shard_map/rollout21/pallas_call | solution.py:77
  33.5 0.0 collective-permute-done.6.refs_1_
  33.5 0.1 collective-permute-start.10
  33.6 0.1 join.9.refs_11_
  33.7 1.6 %collective-permute-start.11 = (bf16[512,512]{1,0:T(8,128)(2,1)S(1)}, bf16[512,512]{1,0:T(8,128)(2,1)S(1)}, u32[]{:S(2)}, u32[]{:S(2)}) collective-permute-start(bf16[512,512]{1,0:T(8,128)(2,1)S(1)} %join.9.refs_11_), channel_id=1, source_target_pairs={{0,2},{1,3},{2,0},{3,1},{4,6},{5,7},{6,4},{7,5},{8,10},{9,11},{10,... | collective-permute-start | bytes 1572872 | tf_op jit(solution)/shard_map/ppermute | solution.py:323
  35.4 0.5 collective-permute-done.2.refs_4_
  35.9 2.9 %gradient.1 = (f32[8,6656]{1,0:T(8,128)S(1)}, f32[32,2048]{1,0:T(8,128)S(1)}, bf16[16,7424]{1,0:T(8,128)(2,1)S(1)}, bf16[16,7424]{1,0:T(8,128)(2,1)S(1)}, bf16[16,7424]{1,0:T(8,128)(2,1)S(1)}) custom-call(s32[1,512]{1,0:T(1,128)S(1)} %bitcast.6, s32[1,512]{1,0:T(1,128)S(1)} %bitcast.8, s32[1,512]{1,0:T(1,128)S(1)} %bitcast.10, f32[256,128]{1,0:T(8,128)S(1)} %join.8.refs_3_, ...), custom_call_target="tpu_custom_call" | custom-call | flops 2281701376 | tf_op jit(solution)/shard_map/gradient/pallas_call | solution.py:77
  38.8 1.6 %collective-permute-start.7 = (bf16[16,7424]{1,0:T(8,128)(2,1)S(1)}, bf16[16,7424]{1,0:T(8,128)(2,1)S(1)}, u32[]{:S(2)}, u32[]{:S(2)}) collective-permute-start(bf16[16,7424]{1,0:T(8,128)(2,1)S(1)} %get-tuple-element.45), channel_id=1, source_target_pairs={{0,8},{8,0},{16,24},{24,16},{1,9},{9,1},{17,25},{25,17},{2,10},{10... | collective-permute-start | bytes 712712 | tf_op jit(solution)/shard_map/ppermute | solution.py:323
  40.4 1.5 %collective-permute-start.8 = (bf16[16,7424]{1,0:T(8,128)(2,1)S(1)}, bf16[16,7424]{1,0:T(8,128)(2,1)S(1)}, u32[]{:S(2)}, u32[]{:S(2)}) collective-permute-start(bf16[16,7424]{1,0:T(8,128)(2,1)S(1)} %get-tuple-element.46), channel_id=1, source_target_pairs={{0,16},{8,24},{16,0},{24,8},{1,17},{9,25},{17,1},{25,9},{2,18},{10... | collective-permute-start | bytes 712712 | tf_op jit(solution)/shard_map/ppermute | solution.py:323
  41.9 0.5 collective-permute-start.9
  42.4 0.0 copy-start.8
  42.4 0.0 copy-start.9
  42.4 3.9 %rollout20.1 = (f32[512,512]{1,0:T(8,128)S(1)}, bf16[6656,512]{1,0:T(8,128)(2,1)S(1)}) custom-call(bf16[512,6656]{1,0:T(8,128)(2,1)S(1)} %copy-done, bf16[6656,512]{1,0:T(8,128)(2,1)S(1)} %get-tuple-element.48.refs_1_, bf16[6656,4096]{1,0:T(8,128)(2,1)} %refs_2_.13, f32[8,6656]{1,0:T(8,128)S(1)} %get-tuple-element.43.refs_3_.refs_0_), custom_call_target="tpu_custom_call" | custom-call | flops 3489660928 | bytes 54525952 | tf_op jit(solution)/shard_map/rollout20/pallas_call | solution.py:77
  46.3 1.8 %collective-permute-done.11.refs_2_ = bf16[512,512]{1,0:T(8,128)(2,1)S(1)} collective-permute-done((bf16[512,512]{1,0:T(8,128)(2,1)S(1)}, bf16[512,512]{1,0:T(8,128)(2,1)S(1)}, u32[]{:S(2)}, u32[]{:S(2)}) %collective-permute-start.11) | collective-permute-done | bytes 524320 | tf_op jit(solution)/shard_map/ppermute | solution.py:323
  48.1 0.2 join.10.refs_12_
  48.3 0.3 collective-permute-start.21
  48.6 4.0 %collective-permute-done.8.refs_4_ = bf16[16,7424]{1,0:T(8,128)(2,1)S(1)} collective-permute-done((bf16[16,7424]{1,0:T(8,128)(2,1)S(1)}, bf16[16,7424]{1,0:T(8,128)(2,1)S(1)}, u32[]{:S(2)}, u32[]{:S(2)}) %collective-permute-start.8) | collective-permute-done | bytes 237600 | tf_op jit(solution)/shard_map/ppermute | solution.py:323
  52.7 4.0 %update.1 = (bf16[32,512]{1,0:T(8,128)(2,1)S(1)}, f32[8,512]{1,0:T(8,128)S(1)}, f32[8,6656]{1,0:T(8,128)}, f32[8,6656]{1,0:T(8,128)}, f32[8,6656]{1,0:T(8,128)},...) custom-call(f32[8,6656]{1,0:T(8,128)S(1)} %get-tuple-element.43.refs_3_.refs_0_, ...), custom_call_target="tpu_custom_call" | custom-call | flops 1744830464 | bytes 4177920 | tf_op jit(solution)/shard_map/update/pallas_call | solution.py:77
  56.7 1.3 %collective-permute-start.13 = (f32[8,512]{1,0:T(8,128)S(1)}, f32[8,512]{1,0:T(8,128)S(1)}, u32[]{:S(2)}, u32[]{:S(2)}) collective-permute-start(f32[8,512]{1,0:T(8,128)S(1)} %get-tuple-element.51.refs_3_.refs_0_), channel_id=1, source_target_pairs={{0,8},{8,0},{16,24},{24,16},{1,9},{9,1},{17,25},{25,17},{2,10},{10... | collective-permute-start | bytes 49160 | tf_op jit(solution)/shard_map/ppermute | solution.py:323
  58.0 3.7 %rollout11.1 = (bf16[512,512]{1,0:T(8,128)(2,1)S(1)}, bf16[6656,512]{1,0:T(8,128)(2,1)S(1)}) custom-call(bf16[512,6656]{1,0:T(8,128)(2,1)S(1)} %copy-done, bf16[6656,512]{1,0:T(8,128)(2,1)S(1)} %get-tuple-element.52.refs_1_, bf16[6656,4096]{1,0:T(8,128)(2,1)} %refs_2_.13, f32[8,512]{1,0:T(8,128)S(1)} %get-tuple-element.51.refs_3_.refs_0_), custom_call_target="tpu_custom_call" | custom-call | flops 3489660928 | bytes 54525952 | tf_op jit(solution)/shard_map/rollout11/pallas_call | solution.py:77
  61.7 0.7 collective-permute-start.12
  62.4 1.8 %collective-permute-start.17 = (bf16[512,512]{1,0:T(8,128)(2,1)S(1)}, bf16[512,512]{1,0:T(8,128)(2,1)S(1)}, u32[]{:S(2)}, u32[]{:S(2)}) collective-permute-start(bf16[512,512]{1,0:T(8,128)(2,1)S(1)} %get-tuple-element.53.refs_2_), channel_id=1, source_target_pairs={{0,1},{1,0},{2,3},{3,2},{4,5},{5,4},{6,7},{7,6},{8,9},{9,8},{10,11... | collective-permute-start | bytes 1572872 | tf_op jit(solution)/shard_map/ppermute | solution.py:323
  64.1 4.3 %collective-permute-start.14 = (f32[16,512]{1,0:T(8,128)S(1)}, f32[16,512]{1,0:T(8,128)S(1)}, u32[]{:S(2)}, u32[]{:S(2)}) collective-permute-start(f32[16,512]{1,0:T(8,128)S(1)} %gather.2.refs_3_.refs_0_), channel_id=1, source_target_pairs={{0,16},{8,24},{16,0},{24,8},{1,17},{9,25},{17,1},{25,9},{2,18},{10... | collective-permute-start | bytes 98312 | tf_op jit(solution)/shard_map/ppermute | solution.py:323
  68.4 3.7 %rollout10.1 = (f32[512,512]{1,0:T(8,128)S(1)}, bf16[6656,512]{1,0:T(8,128)(2,1)S(1)}) custom-call(bf16[512,6656]{1,0:T(8,128)(2,1)S(1)} %copy-done, bf16[6656,512]{1,0:T(8,128)(2,1)S(1)} %get-tuple-element.54.refs_1_, bf16[6656,4096]{1,0:T(8,128)(2,1)} %refs_2_.13, f32[16,512]{1,0:T(8,128)S(1)} %gather.2.refs_3_.refs_0_), custom_call_target="tpu_custom_call" | custom-call | flops 3489660928 | bytes 54525952 | tf_op jit(solution)/shard_map/rollout10/pallas_call | solution.py:77
  72.1 0.1 collective-permute-start.15
  72.2 3.7 %rollout01.1 = (bf16[512,512]{1,0:T(8,128)(2,1)S(1)}, bf16[6656,512]{1,0:T(8,128)(2,1)S(1)}) custom-call(bf16[512,6656]{1,0:T(8,128)(2,1)S(1)} %copy-done, bf16[6656,512]{1,0:T(8,128)(2,1)S(1)} %get-tuple-element.56.refs_1_, bf16[6656,4096]{1,0:T(8,128)(2,1)} %refs_2_.13, f32[32,512]{1,0:T(8,128)S(1)} %gather.3.refs_3_.refs_0_), custom_call_target="tpu_custom_call" | custom-call | flops 3489660928 | bytes 54525952 | tf_op jit(solution)/shard_map/rollout01/pallas_call | solution.py:77
  75.9 0.6 collective-permute-start.19
  76.5 0.1 join.12.refs_2_
  76.6 2.6 %collective-permute-start.20 = (bf16[512,512]{1,0:T(8,128)(2,1)S(1)}, bf16[512,512]{1,0:T(8,128)(2,1)S(1)}, u32[]{:S(2)}, u32[]{:S(2)}) collective-permute-start(bf16[512,512]{1,0:T(8,128)(2,1)S(1)} %join.12.refs_2_), channel_id=1, source_target_pairs={{0,2},{1,3},{2,0},{3,1},{4,6},{5,7},{6,4},{7,5},{8,10},{9,11},{10,... | collective-permute-start | bytes 1572872 | tf_op jit(solution)/shard_map/ppermute | solution.py:323
  79.2 0.1 collective-permute-start.16
  79.3 3.7 %rollout00.1.refs_2_.refs_3_ = f32[512,512]{1,0:T(8,128)S(1)} custom-call(bf16[512,6656]{1,0:T(8,128)(2,1)S(1)} %copy-done, bf16[6656,512]{1,0:T(8,128)(2,1)S(1)} %get-tuple-element.58.refs_1_, bf16[512,512]{1,0:T(8,128)(2,1)S(1)} %join.12.refs_2_), custom_call_target="tpu_custom_call" | custom-call | flops 3489660928 | tf_op jit(solution)/shard_map/rollout00/pallas_call | solution.py:77
  83.0 9.8 %collective-permute-done.16.refs_1_ = f32[32,512]{1,0:T(8,128)S(1)} collective-permute-done((f32[32,512]{1,0:T(8,128)S(1)}, f32[32,512]{1,0:T(8,128)S(1)}, u32[]{:S(2)}, u32[]{:S(2)}) %collective-permute-start.16) | collective-permute-done | bytes 65568 | tf_op jit(solution)/shard_map/ppermute | solution.py:323
  92.8 1.5 %collective-permute-start.18 = (f32[32,512]{1,0:T(8,128)S(1)}, f32[32,512]{1,0:T(8,128)S(1)}, u32[]{:S(2)}, u32[]{:S(2)}) collective-permute-start(f32[32,512]{1,0:T(8,128)S(1)} %join.13.refs_1_), channel_id=1, source_target_pairs={{0,4},{1,5},{2,6},{3,7},{4,0},{5,1},{6,2},{7,3},{8,12},{9,13},{10,... | collective-permute-start | bytes 196616 | tf_op jit(solution)/shard_map/ppermute | solution.py:323
  94.2 3.8 %collective-permute-done.18.refs_2_ = f32[32,512]{1,0:T(8,128)S(1)} collective-permute-done((f32[32,512]{1,0:T(8,128)S(1)}, f32[32,512]{1,0:T(8,128)S(1)}, u32[]{:S(2)}, u32[]{:S(2)}) %collective-permute-start.18) | collective-permute-done | bytes 65568 | tf_op jit(solution)/shard_map/ppermute | solution.py:323
  98.1 1.3 %finish.1 = bf16[512,512]{1,0:T(8,128)(2,1)} custom-call(bf16[32,512]{1,0:T(8,128)(2,1)S(1)} %collective-permute-done.12.refs_3_.refs_0_, f32[32,512]{1,0:T(8,128)S(1)} %join.13.refs_1_, f32[32,512]{1,0:T(8,128)S(1)} %collective-permute-done.18.refs_2_, f32[512,512]{1,0:T(8,128)S(1)} %rollout00.1.refs_2_.refs_3_, ...), custom_call_target="tpu_custom_call" | custom-call | flops 134217728 | bytes 524288 | tf_op jit(solution)/shard_map/finish/pallas_call | solution.py:77
  (50 shorter events, 0.2 us)
Async XLA Ops:
  0.6 12.3 %copy-start = (bf16[512,6656]{1,0:T(8,128)(2,1)S(1)}, bf16[512,6656]{1,0:T(8,128)(2,1)}, u32[]{:S(2)}) copy-start(bf16[512,6656]{1,0:T(8,128)(2,1)} %refs_0_.15) | copy-start | bytes 20447236
  8.4 25.3 %collective-permute-start.3 = (f32[8,256]{1,0:T(8,128)}, f32[8,256]{1,0:T(8,128)S(1)}, u32[]{:S(2)}, u32[]{:S(2)}) collective-permute-start(f32[8,256]{1,0:T(8,128)} %get-tuple-element.40.refs_7_), channel_id=1, source_target_pairs={{0,8},{8,0},{16,24},{24,16},{1,9},{9,1},{17,25},{25,17},{2,10},{10... | collective-permute-start | bytes 24584 | tf_op jit(solution)/shard_map/ppermute | solution.py:323
  11.4 24.0 %collective-permute-start.4 = (f32[8,256]{1,0:T(8,128)}, f32[8,256]{1,0:T(8,128)S(1)}, u32[]{:S(2)}, u32[]{:S(2)}) collective-permute-start(f32[8,256]{1,0:T(8,128)} %get-tuple-element.40.refs_7_), channel_id=1, source_target_pairs={{0,16},{8,24},{16,0},{24,8},{1,17},{9,25},{17,1},{25,9},{2,18},{10... | collective-permute-start | bytes 24584 | tf_op jit(solution)/shard_map/ppermute | solution.py:323
  12.9 22.5 %collective-permute-start.5 = (f32[8,256]{1,0:T(8,128)}, f32[8,256]{1,0:T(8,128)S(1)}, u32[]{:S(2)}, u32[]{:S(2)}) collective-permute-start(f32[8,256]{1,0:T(8,128)} %get-tuple-element.40.refs_7_), channel_id=1, source_target_pairs={{0,24},{8,16},{16,8},{24,0},{1,25},{9,17},{17,9},{25,1},{2,26},{10... | collective-permute-start | bytes 24584 | tf_op jit(solution)/shard_map/ppermute | solution.py:323
  12.9 8.2 %collective-permute-start = (f32[256,128]{1,0:T(8,128)}, f32[256,128]{1,0:T(8,128)S(1)}, u32[]{:S(2)}, u32[]{:S(2)}) collective-permute-start(f32[256,128]{1,0:T(8,128)} %get-tuple-element.36.refs_2_.refs_0_), channel_id=1, source_target_pairs={{0,1},{1,0},{2,3},{3,2},{4,5},{5,4},{6,7},{7,6},{8,9},{9,8},{10,11... | collective-permute-start | bytes 393224 | tf_op jit(solution)/shard_map/ppermute | solution.py:323
  12.9 0.9 copy-start.6
  13.9 7.2 %copy-start.7 = (f32[256,128]{1,0:T(8,128)S(1)}, f32[256,128]{1,0:T(8,128)}, u32[]{:S(2)}) copy-start(f32[256,128]{1,0:T(8,128)} %get-tuple-element.36.refs_2_.refs_0_) | copy-start | bytes 393220
  20.5 13.0 %collective-permute-start.6 = (bf16[512,512]{1,0:T(8,128)(2,1)S(1)}, bf16[512,512]{1,0:T(8,128)(2,1)S(1)}, u32[]{:S(2)}, u32[]{:S(2)}) collective-permute-start(bf16[512,512]{1,0:T(8,128)(2,1)S(1)} %get-tuple-element.37.refs_2_), channel_id=1, source_target_pairs={{0,1},{1,0},{2,3},{3,2},{4,5},{5,4},{6,7},{7,6},{8,9},{9,8},{10,11... | collective-permute-start | bytes 1572872 | tf_op jit(solution)/shard_map/ppermute | solution.py:323
  21.1 5.8 %collective-permute-start.1 = (f32[256,128]{1,0:T(8,128)S(1)}, f32[256,128]{1,0:T(8,128)S(1)}, u32[]{:S(2)}, u32[]{:S(2)}) collective-permute-start(f32[256,128]{1,0:T(8,128)S(1)} %join.7.refs_3_.refs_0_), channel_id=1, source_target_pairs={{0,2},{1,3},{2,0},{3,1},{4,6},{5,7},{6,4},{7,5},{8,10},{9,11},{10,... | collective-permute-start | bytes 393224 | tf_op jit(solution)/shard_map/ppermute | solution.py:323
  23.2 12.7 %slice-start = ((s8[6815744]{0:T(1024)(128)(4,1)}), s8[2621440]{0:T(1024)(128)(4,1)S(1)}, s32[]{:S(2)}) async-start(s8[6815744]{0:T(1024)(128)(4,1)} %bitcast.3), calls=%async_computation | async-start | bytes 5242880
  27.0 8.9 %collective-permute-start.2 = (f32[256,128]{1,0:T(8,128)S(1)}, f32[256,128]{1,0:T(8,128)S(1)}, u32[]{:S(2)}, u32[]{:S(2)}) collective-permute-start(f32[256,128]{1,0:T(8,128)S(1)} %join.8.refs_3_), channel_id=1, source_target_pairs={{0,4},{1,5},{2,6},{3,7},{4,0},{5,1},{6,2},{7,3},{8,12},{9,13},{10,... | collective-permute-start | bytes 393224 | tf_op jit(solution)/shard_map/ppermute | solution.py:323
  29.8 6.1 %slice-start.1 = ((s8[6815744]{0:T(1024)(128)(4,1)}), s8[4194304]{0:T(1024)(128)(4,1)S(1)}, s32[]{:S(2)}) async-start(s8[6815744]{0:T(1024)(128)(4,1)} %bitcast.3), calls=%async_computation.1 | async-start | bytes 8388608
  29.8 6.1 %copy-start.1 = (bf16[512,2048]{1,0:T(8,128)(2,1)S(1)}, bf16[512,2048]{1,0:T(8,128)(2,1)}, u32[]{:S(2)}) copy-start(bf16[512,2048]{1,0:T(8,128)(2,1)} %refs_6_.4) | copy-start | bytes 6291460
  29.8 6.1 %copy-start.10 = (f32[8,256]{1,0:T(8,128)S(1)}, f32[8,256]{1,0:T(8,128)}, u32[]{:S(2)}) copy-start(f32[8,256]{1,0:T(8,128)} %get-tuple-element.40.refs_7_) | copy-start | bytes 24580
  29.8 6.1 %copy-start.11 = (s32[512]{0:T(512)S(1)}, s32[512]{0:T(512)}, u32[]{:S(2)}) copy-start(s32[512]{0:T(512)} %param.15) | copy-start | bytes 6148
  29.8 6.2 %copy-start.12 = (s32[512]{0:T(512)S(1)}, s32[512]{0:T(512)}, u32[]{:S(2)}) copy-start(s32[512]{0:T(512)} %param.16) | copy-start | bytes 6148
  29.8 6.1 %copy-start.13 = (s32[512]{0:T(512)S(1)}, s32[512]{0:T(512)}, u32[]{:S(2)}) copy-start(s32[512]{0:T(512)} %param.17) | copy-start | bytes 6148
  33.5 12.8 %collective-permute-start.10 = (bf16[512,512]{1,0:T(8,128)(2,1)S(1)}, bf16[512,512]{1,0:T(8,128)(2,1)S(1)}, u32[]{:S(2)}, u32[]{:S(2)}) collective-permute-start(bf16[512,512]{1,0:T(8,128)(2,1)S(1)} %get-tuple-element.42.refs_2_), channel_id=1, source_target_pairs={{0,1},{1,0},{2,3},{3,2},{4,5},{5,4},{6,7},{7,6},{8,9},{9,8},{10,11... | collective-permute-start | bytes 1572872 | tf_op jit(solution)/shard_map/ppermute | solution.py:323
  33.7 14.4 %collective-permute-start.11 = (bf16[512,512]{1,0:T(8,128)(2,1)S(1)}, bf16[512,512]{1,0:T(8,128)(2,1)S(1)}, u32[]{:S(2)}, u32[]{:S(2)}) collective-permute-start(bf16[512,512]{1,0:T(8,128)(2,1)S(1)} %join.9.refs_11_), channel_id=1, source_target_pairs={{0,2},{1,3},{2,0},{3,1},{4,6},{5,7},{6,4},{7,5},{8,10},{9,11},{10,... | collective-permute-start | bytes 1572872 | tf_op jit(solution)/shard_map/ppermute | solution.py:323
  38.8 9.8 %collective-permute-start.7 = (bf16[16,7424]{1,0:T(8,128)(2,1)S(1)}, bf16[16,7424]{1,0:T(8,128)(2,1)S(1)}, u32[]{:S(2)}, u32[]{:S(2)}) collective-permute-start(bf16[16,7424]{1,0:T(8,128)(2,1)S(1)} %get-tuple-element.45), channel_id=1, source_target_pairs={{0,8},{8,0},{16,24},{24,16},{1,9},{9,1},{17,25},{25,17},{2,10},{10... | collective-permute-start | bytes 712712 | tf_op jit(solution)/shard_map/ppermute | solution.py:323
  40.4 12.2 %collective-permute-start.8 = (bf16[16,7424]{1,0:T(8,128)(2,1)S(1)}, bf16[16,7424]{1,0:T(8,128)(2,1)S(1)}, u32[]{:S(2)}, u32[]{:S(2)}) collective-permute-start(bf16[16,7424]{1,0:T(8,128)(2,1)S(1)} %get-tuple-element.46), channel_id=1, source_target_pairs={{0,16},{8,24},{16,0},{24,8},{1,17},{9,25},{17,1},{25,9},{2,18},{10... | collective-permute-start | bytes 712712 | tf_op jit(solution)/shard_map/ppermute | solution.py:323
  41.9 10.7 %collective-permute-start.9 = (bf16[16,7424]{1,0:T(8,128)(2,1)S(1)}, bf16[16,7424]{1,0:T(8,128)(2,1)S(1)}, u32[]{:S(2)}, u32[]{:S(2)}) collective-permute-start(bf16[16,7424]{1,0:T(8,128)(2,1)S(1)} %get-tuple-element.47), channel_id=1, source_target_pairs={{0,24},{8,16},{16,8},{24,0},{1,25},{9,17},{17,9},{25,1},{2,26},{10... | collective-permute-start | bytes 712712 | tf_op jit(solution)/shard_map/ppermute | solution.py:323
  42.4 10.3 %copy-start.2 = (f32[32,6656]{1,0:T(8,128)S(1)}, f32[32,6656]{1,0:T(8,128)}, u32[]{:S(2)}) copy-start(f32[32,6656]{1,0:T(8,128)} %refs_6_.5) | copy-start | bytes 2555908
  42.4 10.3 %copy-start.3 = (f32[32,2048]{1,0:T(8,128)S(1)}, f32[32,2048]{1,0:T(8,128)}, u32[]{:S(2)}) copy-start(f32[32,2048]{1,0:T(8,128)} %refs_9_.1) | copy-start | bytes 786436
  42.4 10.3 %copy-start.4 = (f32[32,6656]{1,0:T(8,128)S(1)}, f32[32,6656]{1,0:T(8,128)}, u32[]{:S(2)}) copy-start(f32[32,6656]{1,0:T(8,128)} %refs_7_.1) | copy-start | bytes 2555908
  42.4 10.3 %copy-start.5 = (f32[32,6656]{1,0:T(8,128)S(1)}, f32[32,6656]{1,0:T(8,128)}, u32[]{:S(2)}) copy-start(f32[32,6656]{1,0:T(8,128)} %refs_8_.1) | copy-start | bytes 2555908
  42.4 10.3 %copy-start.8 = (f32[32,2048]{1,0:T(8,128)S(1)}, f32[32,2048]{1,0:T(8,128)}, u32[]{:S(2)}) copy-start(f32[32,2048]{1,0:T(8,128)} %refs_10_.1) | copy-start | bytes 786436
  42.4 10.3 %copy-start.9 = (f32[32,2048]{1,0:T(8,128)S(1)}, f32[32,2048]{1,0:T(8,128)}, u32[]{:S(2)}) copy-start(f32[32,2048]{1,0:T(8,128)} %refs_11_.1) | copy-start | bytes 786436
  48.3 45.9 %collective-permute-start.21 = (bf16[512,512]{1,0:T(8,128)(2,1)S(1)}, bf16[512,512]{1,0:T(8,128)(2,1)S(1)}, u32[]{:S(2)}, u32[]{:S(2)}) collective-permute-start(bf16[512,512]{1,0:T(8,128)(2,1)S(1)} %join.10.refs_12_), channel_id=1, source_target_pairs={{0,4},{1,5},{2,6},{3,7},{4,0},{5,1},{6,2},{7,3},{8,12},{9,13},{10,... | collective-permute-start | bytes 1572872 | tf_op jit(solution)/shard_map/ppermute | solution.py:323
  56.7 7.4 %collective-permute-start.13 = (f32[8,512]{1,0:T(8,128)S(1)}, f32[8,512]{1,0:T(8,128)S(1)}, u32[]{:S(2)}, u32[]{:S(2)}) collective-permute-start(f32[8,512]{1,0:T(8,128)S(1)} %get-tuple-element.51.refs_3_.refs_0_), channel_id=1, source_target_pairs={{0,8},{8,0},{16,24},{24,16},{1,9},{9,1},{17,25},{25,17},{2,10},{10... | collective-permute-start | bytes 49160 | tf_op jit(solution)/shard_map/ppermute | solution.py:323
  61.7 10.4 %collective-permute-start.12 = (bf16[32,512]{1,0:T(8,128)(2,1)S(1)}, bf16[32,512]{1,0:T(8,128)(2,1)S(1)}, u32[]{:S(2)}, u32[]{:S(2)}) collective-permute-start(bf16[32,512]{1,0:T(8,128)(2,1)S(1)} %get-tuple-element.50), channel_id=1, source_target_pairs={{0,0},{1,4},{2,8},{3,12},{4,16},{5,20},{6,24},{7,28},{8,1},{9,5},{... | collective-permute-start | bytes 98312 | tf_op jit(solution)/shard_map/ppermute | solution.py:448
  62.4 14.1 %collective-permute-start.17 = (bf16[512,512]{1,0:T(8,128)(2,1)S(1)}, bf16[512,512]{1,0:T(8,128)(2,1)S(1)}, u32[]{:S(2)}, u32[]{:S(2)}) collective-permute-start(bf16[512,512]{1,0:T(8,128)(2,1)S(1)} %get-tuple-element.53.refs_2_), channel_id=1, source_target_pairs={{0,1},{1,0},{2,3},{3,2},{4,5},{5,4},{6,7},{7,6},{8,9},{9,8},{10,11... | collective-permute-start | bytes 1572872 | tf_op jit(solution)/shard_map/ppermute | solution.py:323
  64.1 8.0 %collective-permute-start.14 = (f32[16,512]{1,0:T(8,128)S(1)}, f32[16,512]{1,0:T(8,128)S(1)}, u32[]{:S(2)}, u32[]{:S(2)}) collective-permute-start(f32[16,512]{1,0:T(8,128)S(1)} %gather.2.refs_3_.refs_0_), channel_id=1, source_target_pairs={{0,16},{8,24},{16,0},{24,8},{1,17},{9,25},{17,1},{25,9},{2,18},{10... | collective-permute-start | bytes 98312 | tf_op jit(solution)/shard_map/ppermute | solution.py:323
  72.1 4.3 %collective-permute-start.15 = (f32[32,512]{1,0:T(8,128)S(1)}, f32[32,512]{1,0:T(8,128)S(1)}, u32[]{:S(2)}, u32[]{:S(2)}) collective-permute-start(f32[32,512]{1,0:T(8,128)S(1)} %gather.3.refs_3_.refs_0_), channel_id=1, source_target_pairs={{0,1},{1,0},{2,3},{3,2},{4,5},{5,4},{6,7},{7,6},{8,9},{9,8},{10,11... | collective-permute-start | bytes 196616 | tf_op jit(solution)/shard_map/ppermute | solution.py:323
  75.9 18.3 %collective-permute-start.19 = (bf16[512,512]{1,0:T(8,128)(2,1)S(1)}, bf16[512,512]{1,0:T(8,128)(2,1)S(1)}, u32[]{:S(2)}, u32[]{:S(2)}) collective-permute-start(bf16[512,512]{1,0:T(8,128)(2,1)S(1)} %get-tuple-element.57.refs_2_), channel_id=1, source_target_pairs={{0,1},{1,0},{2,3},{3,2},{4,5},{5,4},{6,7},{7,6},{8,9},{9,8},{10,11... | collective-permute-start | bytes 1572872 | tf_op jit(solution)/shard_map/ppermute | solution.py:323
  76.6 21.5 %collective-permute-start.20 = (bf16[512,512]{1,0:T(8,128)(2,1)S(1)}, bf16[512,512]{1,0:T(8,128)(2,1)S(1)}, u32[]{:S(2)}, u32[]{:S(2)}) collective-permute-start(bf16[512,512]{1,0:T(8,128)(2,1)S(1)} %join.12.refs_2_), channel_id=1, source_target_pairs={{0,2},{1,3},{2,0},{3,1},{4,6},{5,7},{6,4},{7,5},{8,10},{9,11},{10,... | collective-permute-start | bytes 1572872 | tf_op jit(solution)/shard_map/ppermute | solution.py:323
  79.2 13.5 %collective-permute-start.16 = (f32[32,512]{1,0:T(8,128)S(1)}, f32[32,512]{1,0:T(8,128)S(1)}, u32[]{:S(2)}, u32[]{:S(2)}) collective-permute-start(f32[32,512]{1,0:T(8,128)S(1)} %join.11.refs_2_.refs_0_), channel_id=1, source_target_pairs={{0,2},{1,3},{2,0},{3,1},{4,6},{5,7},{6,4},{7,5},{8,10},{9,11},{10,... | collective-permute-start | bytes 196616 | tf_op jit(solution)/shard_map/ppermute | solution.py:323
  92.8 5.3 %collective-permute-start.18 = (f32[32,512]{1,0:T(8,128)S(1)}, f32[32,512]{1,0:T(8,128)S(1)}, u32[]{:S(2)}, u32[]{:S(2)}) collective-permute-start(f32[32,512]{1,0:T(8,128)S(1)} %join.13.refs_1_), channel_id=1, source_target_pairs={{0,4},{1,5},{2,6},{3,7},{4,0},{5,1},{6,2},{7,3},{8,12},{9,13},{10,... | collective-permute-start | bytes 196616 | tf_op jit(solution)/shard_map/ppermute | solution.py:323

commit v5 on v4

--- a/solution.py
+++ b/solution.py
@@ -465,10 +465,9 @@
         if at < len(tensor_bits) - 1:
             product = add([product, received], after)
             after = [product]
-        if at == 0:
-            after = send_on(after)
-    waiting.remove(0)
-    send_on(after)
+        if at == 1:
+            waiting.remove(0)
+            send_on(after)
 
     (result,) = call(
         functools.partial(finish_kernel, rank),

time: 102 us -> 100 us (0.980); the launches traced: 99.5 us -> 99.4 us
  no operation moved by 1% of the time
where the time goes in v5:
time: 100 us; the launch traced here: 99.4 us
  Pallas kernels  49.1 us (49%)
  starting transfers between devices  28.6 us (29%)
  waiting for transfers between devices  19.6 us (20%)
  between operations  1.15 us (1%)
    pallas_call x21, Pallas kernels, call(): pl.pallas_call(body, name=name, out_shape=[*outputs, *far_outputs], in_sp...  49.1 us
    ppermute x21, starting transfers between devices, xor(): lax.ppermute(array, axis, [(i, i ^ k) for i in range(lax.axis_size(axis))])  27.9 us
    ppermute x21, waiting for transfers between devices, xor(): lax.ppermute(array, axis, [(i, i ^ k) for i in range(lax.axis_size(axis))])  19.6 us
  transfers between devices with their start and end apart: 22, of which 5 were waited for; matrix products, arithmetic and copies ran while one was open for 0% of the time, Pallas kernels for 40%

profile of v5, /device:TPU:0, one launch (start us, length us, event | category | flops | bytes accessed | tf_op | source)
XLA Modules:
  0.0 99.4 jit_solution(430022806514877025)
XLA Ops:
  0.6 7.7 %project.1 = (f32[256,128]{1,0:T(8,128)}, f32[8,256]{1,0:T(8,128)}) custom-call(s32[1,512]{1,0:T(1,128)} %bitcast.5, s32[1,512]{1,0:T(1,128)} %bitcast.7, s32[1,512]{1,0:T(1,128)} %bitcast.9, bf16[512,6656]{1,0:T(8,128)(2,1)} %refs_5_.3, f32[32,6656]{1,0:T(8,128)} %refs_6_.5, bf16[512,2048]{1,0:T(8,128)(2,1)} %refs_6_.4, f32[32,2048]{1,0:T(8,128)} %refs_9_.1), custom_call_target="tpu_custom_call" | custom-call | flops 2281701376 | bytes 10027008 | tf_op jit(solution)/shard_map/project/pallas_call | solution.py:77
  8.4 3.0 %collective-permute-start.3 = (f32[8,256]{1,0:T(8,128)}, f32[8,256]{1,0:T(8,128)S(1)}, u32[]{:S(2)}, u32[]{:S(2)}) collective-permute-start(f32[8,256]{1,0:T(8,128)} %get-tuple-element.40.refs_7_), channel_id=1, source_target_pairs={{0,8},{8,0},{16,24},{24,16},{1,9},{9,1},{17,25},{25,17},{2,10},{10... | collective-permute-start | bytes 24584 | tf_op jit(solution)/shard_map/ppermute | solution.py:323
  11.4 1.5 %collective-permute-start.4 = (f32[8,256]{1,0:T(8,128)}, f32[8,256]{1,0:T(8,128)S(1)}, u32[]{:S(2)}, u32[]{:S(2)}) collective-permute-start(f32[8,256]{1,0:T(8,128)} %get-tuple-element.40.refs_7_), channel_id=1, source_target_pairs={{0,16},{8,24},{16,0},{24,8},{1,17},{9,25},{17,1},{25,9},{2,18},{10... | collective-permute-start | bytes 24584 | tf_op jit(solution)/shard_map/ppermute | solution.py:323
  12.9 0.0 collective-permute-start.5
  12.9 0.0 collective-permute-start
  13.0 0.9 copy-done.6
  13.9 6.7 %rollout31.1 = (bf16[512,512]{1,0:T(8,128)(2,1)S(1)}, bf16[6656,512]{1,0:T(8,128)(2,1)S(1)}) custom-call(bf16[512,6656]{1,0:T(8,128)(2,1)S(1)} %copy-done, bf16[6656,4096]{1,0:T(8,128)(2,1)} %refs_2_.13, f32[256,128]{1,0:T(8,128)S(1)} %copy-done.6), custom_call_target="tpu_custom_call" | custom-call | flops 3489660928 | bytes 54525952 | tf_op jit(solution)/shard_map/rollout31/pallas_call | solution.py:77
  20.5 0.6 collective-permute-start.6
  21.1 0.0 collective-permute-done.refs_1_
  21.1 2.1 %collective-permute-start.1 = (f32[256,128]{1,0:T(8,128)S(1)}, f32[256,128]{1,0:T(8,128)S(1)}, u32[]{:S(2)}, u32[]{:S(2)}) collective-permute-start(f32[256,128]{1,0:T(8,128)S(1)} %join.7.refs_3_.refs_0_), channel_id=1, source_target_pairs={{0,2},{1,3},{2,0},{3,1},{4,6},{5,7},{6,4},{7,5},{8,10},{9,11},{10,... | collective-permute-start | bytes 393224 | tf_op jit(solution)/shard_map/ppermute | solution.py:323
  23.2 3.7 %rollout30.1 = (f32[512,512]{1,0:T(8,128)S(1)}, bf16[6656,512]{1,0:T(8,128)(2,1)S(1)}) custom-call(bf16[512,6656]{1,0:T(8,128)(2,1)S(1)} %copy-done, bf16[6656,512]{1,0:T(8,128)(2,1)S(1)} %get-tuple-element.38.refs_1_, bf16[6656,4096]{1,0:T(8,128)(2,1)} %refs_2_.13, f32[256,128]{1,0:T(8,128)S(1)} %join.7.refs_3_.refs_0_), custom_call_target="tpu_custom_call" | custom-call | flops 3489660928 | bytes 54525952 | tf_op jit(solution)/shard_map/rollout30/pallas_call | solution.py:77
  27.0 2.8 %collective-permute-start.2 = (f32[256,128]{1,0:T(8,128)S(1)}, f32[256,128]{1,0:T(8,128)S(1)}, u32[]{:S(2)}, u32[]{:S(2)}) collective-permute-start(f32[256,128]{1,0:T(8,128)S(1)} %join.8.refs_3_), channel_id=1, source_target_pairs={{0,4},{1,5},{2,6},{3,7},{4,0},{5,1},{6,2},{7,3},{8,12},{9,13},{10,... | collective-permute-start | bytes 393224 | tf_op jit(solution)/shard_map/ppermute | solution.py:323
  29.8 0.0 copy-start.12
  29.8 0.0 copy-start.13
  29.8 3.7 %rollout21.1 = (bf16[512,512]{1,0:T(8,128)(2,1)S(1)}, bf16[6656,512]{1,0:T(8,128)(2,1)S(1)}) custom-call(bf16[512,6656]{1,0:T(8,128)(2,1)S(1)} %copy-done, bf16[6656,512]{1,0:T(8,128)(2,1)S(1)} %get-tuple-element.41.refs_1_, bf16[6656,4096]{1,0:T(8,128)(2,1)} %refs_2_.13, f32[256,128]{1,0:T(8,128)S(1)} %join.8.refs_3_), custom_call_target="tpu_custom_call" | custom-call | flops 3489660928 | bytes 54525952 | tf_op jit(solution)/shard_map/rollout21/pallas_call | solution.py:77
  33.5 0.1 collective-permute-start.10
  33.6 0.1 join.9.refs_11_
  33.7 1.6 %collective-permute-start.11 = (bf16[512,512]{1,0:T(8,128)(2,1)S(1)}, bf16[512,512]{1,0:T(8,128)(2,1)S(1)}, u32[]{:S(2)}, u32[]{:S(2)}) collective-permute-start(bf16[512,512]{1,0:T(8,128)(2,1)S(1)} %join.9.refs_11_), channel_id=1, source_target_pairs={{0,2},{1,3},{2,0},{3,1},{4,6},{5,7},{6,4},{7,5},{8,10},{9,11},{10,... | collective-permute-start | bytes 1572872 | tf_op jit(solution)/shard_map/ppermute | solution.py:323
  35.4 0.5 collective-permute-done.2.refs_4_
  35.9 2.9 %gradient.1 = (f32[8,6656]{1,0:T(8,128)S(1)}, f32[32,2048]{1,0:T(8,128)S(1)}, bf16[16,7424]{1,0:T(8,128)(2,1)S(1)}, bf16[16,7424]{1,0:T(8,128)(2,1)S(1)}, bf16[16,7424]{1,0:T(8,128)(2,1)S(1)}) custom-call(s32[1,512]{1,0:T(1,128)S(1)} %bitcast.6, s32[1,512]{1,0:T(1,128)S(1)} %bitcast.8, s32[1,512]{1,0:T(1,128)S(1)} %bitcast.10, f32[256,128]{1,0:T(8,128)S(1)} %join.8.refs_3_, ...), custom_call_target="tpu_custom_call" | custom-call | flops 2281701376 | tf_op jit(solution)/shard_map/gradient/pallas_call | solution.py:77
  38.8 1.6 %collective-permute-start.7 = (bf16[16,7424]{1,0:T(8,128)(2,1)S(1)}, bf16[16,7424]{1,0:T(8,128)(2,1)S(1)}, u32[]{:S(2)}, u32[]{:S(2)}) collective-permute-start(bf16[16,7424]{1,0:T(8,128)(2,1)S(1)} %get-tuple-element.45), channel_id=1, source_target_pairs={{0,8},{8,0},{16,24},{24,16},{1,9},{9,1},{17,25},{25,17},{2,10},{10... | collective-permute-start | bytes 712712 | tf_op jit(solution)/shard_map/ppermute | solution.py:323
  40.4 1.5 %collective-permute-start.8 = (bf16[16,7424]{1,0:T(8,128)(2,1)S(1)}, bf16[16,7424]{1,0:T(8,128)(2,1)S(1)}, u32[]{:S(2)}, u32[]{:S(2)}) collective-permute-start(bf16[16,7424]{1,0:T(8,128)(2,1)S(1)} %get-tuple-element.46), channel_id=1, source_target_pairs={{0,16},{8,24},{16,0},{24,8},{1,17},{9,25},{17,1},{25,9},{2,18},{10... | collective-permute-start | bytes 712712 | tf_op jit(solution)/shard_map/ppermute | solution.py:323
  41.9 0.5 collective-permute-start.9
  42.4 0.0 copy-start.8
  42.4 0.0 copy-start.9
  42.4 3.9 %rollout20.1 = (f32[512,512]{1,0:T(8,128)S(1)}, bf16[6656,512]{1,0:T(8,128)(2,1)S(1)}) custom-call(bf16[512,6656]{1,0:T(8,128)(2,1)S(1)} %copy-done, bf16[6656,512]{1,0:T(8,128)(2,1)S(1)} %get-tuple-element.48.refs_1_, bf16[6656,4096]{1,0:T(8,128)(2,1)} %refs_2_.13, f32[8,6656]{1,0:T(8,128)S(1)} %get-tuple-element.43.refs_3_.refs_0_), custom_call_target="tpu_custom_call" | custom-call | flops 3489660928 | bytes 54525952 | tf_op jit(solution)/shard_map/rollout20/pallas_call | solution.py:77
  46.3 1.8 %collective-permute-done.11.refs_2_ = bf16[512,512]{1,0:T(8,128)(2,1)S(1)} collective-permute-done((bf16[512,512]{1,0:T(8,128)(2,1)S(1)}, bf16[512,512]{1,0:T(8,128)(2,1)S(1)}, u32[]{:S(2)}, u32[]{:S(2)}) %collective-permute-start.11) | collective-permute-done | bytes 524320 | tf_op jit(solution)/shard_map/ppermute | solution.py:323
  48.1 0.2 join.10.refs_12_
  48.3 0.3 collective-permute-start.21
  48.6 4.0 %collective-permute-done.8.refs_4_ = bf16[16,7424]{1,0:T(8,128)(2,1)S(1)} collective-permute-done((bf16[16,7424]{1,0:T(8,128)(2,1)S(1)}, bf16[16,7424]{1,0:T(8,128)(2,1)S(1)}, u32[]{:S(2)}, u32[]{:S(2)}) %collective-permute-start.8) | collective-permute-done | bytes 237600 | tf_op jit(solution)/shard_map/ppermute | solution.py:323
  52.7 4.0 %update.1 = (bf16[32,512]{1,0:T(8,128)(2,1)S(1)}, f32[8,512]{1,0:T(8,128)S(1)}, f32[8,6656]{1,0:T(8,128)}, f32[8,6656]{1,0:T(8,128)}, f32[8,6656]{1,0:T(8,128)},...) custom-call(f32[8,6656]{1,0:T(8,128)S(1)} %get-tuple-element.43.refs_3_.refs_0_, ...), custom_call_target="tpu_custom_call" | custom-call | flops 1744830464 | bytes 4177920 | tf_op jit(solution)/shard_map/update/pallas_call | solution.py:77
  56.7 1.3 %collective-permute-start.13 = (f32[8,512]{1,0:T(8,128)S(1)}, f32[8,512]{1,0:T(8,128)S(1)}, u32[]{:S(2)}, u32[]{:S(2)}) collective-permute-start(f32[8,512]{1,0:T(8,128)S(1)} %get-tuple-element.51.refs_3_.refs_0_), channel_id=1, source_target_pairs={{0,8},{8,0},{16,24},{24,16},{1,9},{9,1},{17,25},{25,17},{2,10},{10... | collective-permute-start | bytes 49160 | tf_op jit(solution)/shard_map/ppermute | solution.py:323
  58.0 3.7 %rollout11.1 = (bf16[512,512]{1,0:T(8,128)(2,1)S(1)}, bf16[6656,512]{1,0:T(8,128)(2,1)S(1)}) custom-call(bf16[512,6656]{1,0:T(8,128)(2,1)S(1)} %copy-done, bf16[6656,512]{1,0:T(8,128)(2,1)S(1)} %get-tuple-element.52.refs_1_, bf16[6656,4096]{1,0:T(8,128)(2,1)} %refs_2_.13, f32[8,512]{1,0:T(8,128)S(1)} %get-tuple-element.51.refs_3_.refs_0_), custom_call_target="tpu_custom_call" | custom-call | flops 3489660928 | bytes 54525952 | tf_op jit(solution)/shard_map/rollout11/pallas_call | solution.py:77
  61.7 0.7 collective-permute-start.12
  62.4 1.8 %collective-permute-start.19 = (bf16[512,512]{1,0:T(8,128)(2,1)S(1)}, bf16[512,512]{1,0:T(8,128)(2,1)S(1)}, u32[]{:S(2)}, u32[]{:S(2)}) collective-permute-start(bf16[512,512]{1,0:T(8,128)(2,1)S(1)} %get-tuple-element.53.refs_2_), channel_id=1, source_target_pairs={{0,1},{1,0},{2,3},{3,2},{4,5},{5,4},{6,7},{7,6},{8,9},{9,8},{10,11... | collective-permute-start | bytes 1572872 | tf_op jit(solution)/shard_map/ppermute | solution.py:323
  64.1 4.3 %collective-permute-start.14 = (f32[16,512]{1,0:T(8,128)S(1)}, f32[16,512]{1,0:T(8,128)S(1)}, u32[]{:S(2)}, u32[]{:S(2)}) collective-permute-start(f32[16,512]{1,0:T(8,128)S(1)} %gather.2.refs_3_.refs_0_), channel_id=1, source_target_pairs={{0,16},{8,24},{16,0},{24,8},{1,17},{9,25},{17,1},{25,9},{2,18},{10... | collective-permute-start | bytes 98312 | tf_op jit(solution)/shard_map/ppermute | solution.py:323
  68.4 3.7 %rollout10.1 = (f32[512,512]{1,0:T(8,128)S(1)}, bf16[6656,512]{1,0:T(8,128)(2,1)S(1)}) custom-call(bf16[512,6656]{1,0:T(8,128)(2,1)S(1)} %copy-done, bf16[6656,512]{1,0:T(8,128)(2,1)S(1)} %get-tuple-element.54.refs_1_, bf16[6656,4096]{1,0:T(8,128)(2,1)} %refs_2_.13, f32[16,512]{1,0:T(8,128)S(1)} %gather.2.refs_3_.refs_0_), custom_call_target="tpu_custom_call" | custom-call | flops 3489660928 | bytes 54525952 | tf_op jit(solution)/shard_map/rollout10/pallas_call | solution.py:77
  72.1 0.1 collective-permute-start.15
  72.2 3.7 %rollout01.1 = (bf16[512,512]{1,0:T(8,128)(2,1)S(1)}, bf16[6656,512]{1,0:T(8,128)(2,1)S(1)}) custom-call(bf16[512,6656]{1,0:T(8,128)(2,1)S(1)} %copy-done, bf16[6656,512]{1,0:T(8,128)(2,1)S(1)} %get-tuple-element.56.refs_1_, bf16[6656,4096]{1,0:T(8,128)(2,1)} %refs_2_.13, f32[32,512]{1,0:T(8,128)S(1)} %gather.3.refs_3_.refs_0_), custom_call_target="tpu_custom_call" | custom-call | flops 3489660928 | bytes 54525952 | tf_op jit(solution)/shard_map/rollout01/pallas_call | solution.py:77
  75.9 0.6 collective-permute-start.18
  76.5 2.6 %collective-permute-start.16 = (f32[32,512]{1,0:T(8,128)S(1)}, f32[32,512]{1,0:T(8,128)S(1)}, u32[]{:S(2)}, u32[]{:S(2)}) collective-permute-start(f32[32,512]{1,0:T(8,128)S(1)} %join.11.refs_2_.refs_0_), channel_id=1, source_target_pairs={{0,2},{1,3},{2,0},{3,1},{4,6},{5,7},{6,4},{7,5},{8,10},{9,11},{10,... | collective-permute-start | bytes 196616 | tf_op jit(solution)/shard_map/ppermute | solution.py:323
  79.1 3.7 %rollout00.1.refs_2_.refs_3_ = f32[512,512]{1,0:T(8,128)S(1)} custom-call(bf16[512,6656]{1,0:T(8,128)(2,1)S(1)} %copy-done, bf16[6656,512]{1,0:T(8,128)(2,1)S(1)} %get-tuple-element.58.refs_1_, f32[32,512]{1,0:T(8,128)S(1)} %join.11.refs_2_.refs_0_), custom_call_target="tpu_custom_call" | custom-call | flops 3489660928 | tf_op jit(solution)/shard_map/rollout00/pallas_call | solution.py:77
  82.8 0.1 join.13
  82.9 0.6 collective-permute-start.20
  83.6 1.1 %collective-permute-start.17 = (f32[32,512]{1,0:T(8,128)S(1)}, f32[32,512]{1,0:T(8,128)S(1)}, u32[]{:S(2)}, u32[]{:S(2)}) collective-permute-start(f32[32,512]{1,0:T(8,128)S(1)} %join.12.refs_2_.refs_1_), channel_id=1, source_target_pairs={{0,4},{1,5},{2,6},{3,7},{4,0},{5,1},{6,2},{7,3},{8,12},{9,13},{10,... | collective-permute-start | bytes 196616 | tf_op jit(solution)/shard_map/ppermute | solution.py:323
  84.7 11.1 %collective-permute-done.17.refs_2_ = f32[32,512]{1,0:T(8,128)S(1)} collective-permute-done((f32[32,512]{1,0:T(8,128)S(1)}, f32[32,512]{1,0:T(8,128)S(1)}, u32[]{:S(2)}, u32[]{:S(2)}) %collective-permute-start.17) | collective-permute-done | bytes 65568 | tf_op jit(solution)/shard_map/ppermute | solution.py:323
  95.8 2.2 %collective-permute-done.20.refs_5_ = bf16[512,512]{1,0:T(8,128)(2,1)S(1)} collective-permute-done((bf16[512,512]{1,0:T(8,128)(2,1)S(1)}, bf16[512,512]{1,0:T(8,128)(2,1)S(1)}, u32[]{:S(2)}, u32[]{:S(2)}) %collective-permute-start.20) | collective-permute-done | bytes 524320 | tf_op jit(solution)/shard_map/ppermute | solution.py:323
  98.0 1.3 %finish.1 = bf16[512,512]{1,0:T(8,128)(2,1)} custom-call(bf16[32,512]{1,0:T(8,128)(2,1)S(1)} %collective-permute-done.12.refs_3_.refs_0_, f32[32,512]{1,0:T(8,128)S(1)} %join.12.refs_2_.refs_1_, f32[32,512]{1,0:T(8,128)S(1)} %collective-permute-done.17.refs_2_, f32[512,512]{1,0:T(8,128)S(1)} %rollout00.1.refs_2_.refs_3_, ...), custom_call_target="tpu_custom_call" | custom-call | flops 134217728 | bytes 524288 | tf_op jit(solution)/shard_map/finish/pallas_call | solution.py:77
  (50 shorter events, 0.2 us)
Async XLA Ops:
  0.6 12.3 %copy-start = (bf16[512,6656]{1,0:T(8,128)(2,1)S(1)}, bf16[512,6656]{1,0:T(8,128)(2,1)}, u32[]{:S(2)}) copy-start(bf16[512,6656]{1,0:T(8,128)(2,1)} %refs_0_.15) | copy-start | bytes 20447236
  8.4 25.3 %collective-permute-start.3 = (f32[8,256]{1,0:T(8,128)}, f32[8,256]{1,0:T(8,128)S(1)}, u32[]{:S(2)}, u32[]{:S(2)}) collective-permute-start(f32[8,256]{1,0:T(8,128)} %get-tuple-element.40.refs_7_), channel_id=1, source_target_pairs={{0,8},{8,0},{16,24},{24,16},{1,9},{9,1},{17,25},{25,17},{2,10},{10... | collective-permute-start | bytes 24584 | tf_op jit(solution)/shard_map/ppermute | solution.py:323
  11.4 24.0 %collective-permute-start.4 = (f32[8,256]{1,0:T(8,128)}, f32[8,256]{1,0:T(8,128)S(1)}, u32[]{:S(2)}, u32[]{:S(2)}) collective-permute-start(f32[8,256]{1,0:T(8,128)} %get-tuple-element.40.refs_7_), channel_id=1, source_target_pairs={{0,16},{8,24},{16,0},{24,8},{1,17},{9,25},{17,1},{25,9},{2,18},{10... | collective-permute-start | bytes 24584 | tf_op jit(solution)/shard_map/ppermute | solution.py:323
  12.9 22.5 %collective-permute-start.5 = (f32[8,256]{1,0:T(8,128)}, f32[8,256]{1,0:T(8,128)S(1)}, u32[]{:S(2)}, u32[]{:S(2)}) collective-permute-start(f32[8,256]{1,0:T(8,128)} %get-tuple-element.40.refs_7_), channel_id=1, source_target_pairs={{0,24},{8,16},{16,8},{24,0},{1,25},{9,17},{17,9},{25,1},{2,26},{10... | collective-permute-start | bytes 24584 | tf_op jit(solution)/shard_map/ppermute | solution.py:323
  12.9 8.2 %collective-permute-start = (f32[256,128]{1,0:T(8,128)}, f32[256,128]{1,0:T(8,128)S(1)}, u32[]{:S(2)}, u32[]{:S(2)}) collective-permute-start(f32[256,128]{1,0:T(8,128)} %get-tuple-element.36.refs_2_.refs_0_), channel_id=1, source_target_pairs={{0,1},{1,0},{2,3},{3,2},{4,5},{5,4},{6,7},{7,6},{8,9},{9,8},{10,11... | collective-permute-start | bytes 393224 | tf_op jit(solution)/shard_map/ppermute | solution.py:323
  12.9 0.9 copy-start.6
  13.9 7.2 %copy-start.7 = (f32[256,128]{1,0:T(8,128)S(1)}, f32[256,128]{1,0:T(8,128)}, u32[]{:S(2)}) copy-start(f32[256,128]{1,0:T(8,128)} %get-tuple-element.36.refs_2_.refs_0_) | copy-start | bytes 393220
  20.5 13.0 %collective-permute-start.6 = (bf16[512,512]{1,0:T(8,128)(2,1)S(1)}, bf16[512,512]{1,0:T(8,128)(2,1)S(1)}, u32[]{:S(2)}, u32[]{:S(2)}) collective-permute-start(bf16[512,512]{1,0:T(8,128)(2,1)S(1)} %get-tuple-element.37.refs_2_), channel_id=1, source_target_pairs={{0,1},{1,0},{2,3},{3,2},{4,5},{5,4},{6,7},{7,6},{8,9},{9,8},{10,11... | collective-permute-start | bytes 1572872 | tf_op jit(solution)/shard_map/ppermute | solution.py:323
  21.1 5.8 %collective-permute-start.1 = (f32[256,128]{1,0:T(8,128)S(1)}, f32[256,128]{1,0:T(8,128)S(1)}, u32[]{:S(2)}, u32[]{:S(2)}) collective-permute-start(f32[256,128]{1,0:T(8,128)S(1)} %join.7.refs_3_.refs_0_), channel_id=1, source_target_pairs={{0,2},{1,3},{2,0},{3,1},{4,6},{5,7},{6,4},{7,5},{8,10},{9,11},{10,... | collective-permute-start | bytes 393224 | tf_op jit(solution)/shard_map/ppermute | solution.py:323
  23.2 12.7 %slice-start = ((s8[6815744]{0:T(1024)(128)(4,1)}), s8[2621440]{0:T(1024)(128)(4,1)S(1)}, s32[]{:S(2)}) async-start(s8[6815744]{0:T(1024)(128)(4,1)} %bitcast.3), calls=%async_computation | async-start | bytes 5242880
  27.0 8.9 %collective-permute-start.2 = (f32[256,128]{1,0:T(8,128)S(1)}, f32[256,128]{1,0:T(8,128)S(1)}, u32[]{:S(2)}, u32[]{:S(2)}) collective-permute-start(f32[256,128]{1,0:T(8,128)S(1)} %join.8.refs_3_), channel_id=1, source_target_pairs={{0,4},{1,5},{2,6},{3,7},{4,0},{5,1},{6,2},{7,3},{8,12},{9,13},{10,... | collective-permute-start | bytes 393224 | tf_op jit(solution)/shard_map/ppermute | solution.py:323
  29.8 6.1 %slice-start.1 = ((s8[6815744]{0:T(1024)(128)(4,1)}), s8[4194304]{0:T(1024)(128)(4,1)S(1)}, s32[]{:S(2)}) async-start(s8[6815744]{0:T(1024)(128)(4,1)} %bitcast.3), calls=%async_computation.1 | async-start | bytes 8388608
  29.8 6.1 %copy-start.1 = (bf16[512,2048]{1,0:T(8,128)(2,1)S(1)}, bf16[512,2048]{1,0:T(8,128)(2,1)}, u32[]{:S(2)}) copy-start(bf16[512,2048]{1,0:T(8,128)(2,1)} %refs_6_.4) | copy-start | bytes 6291460
  29.8 6.1 %copy-start.10 = (f32[8,256]{1,0:T(8,128)S(1)}, f32[8,256]{1,0:T(8,128)}, u32[]{:S(2)}) copy-start(f32[8,256]{1,0:T(8,128)} %get-tuple-element.40.refs_7_) | copy-start | bytes 24580
  29.8 6.1 %copy-start.11 = (s32[512]{0:T(512)S(1)}, s32[512]{0:T(512)}, u32[]{:S(2)}) copy-start(s32[512]{0:T(512)} %param.15) | copy-start | bytes 6148
  29.8 6.2 %copy-start.12 = (s32[512]{0:T(512)S(1)}, s32[512]{0:T(512)}, u32[]{:S(2)}) copy-start(s32[512]{0:T(512)} %param.16) | copy-start | bytes 6148
  29.8 6.1 %copy-start.13 = (s32[512]{0:T(512)S(1)}, s32[512]{0:T(512)}, u32[]{:S(2)}) copy-start(s32[512]{0:T(512)} %param.17) | copy-start | bytes 6148
  33.5 12.8 %collective-permute-start.10 = (bf16[512,512]{1,0:T(8,128)(2,1)S(1)}, bf16[512,512]{1,0:T(8,128)(2,1)S(1)}, u32[]{:S(2)}, u32[]{:S(2)}) collective-permute-start(bf16[512,512]{1,0:T(8,128)(2,1)S(1)} %get-tuple-element.42.refs_2_), channel_id=1, source_target_pairs={{0,1},{1,0},{2,3},{3,2},{4,5},{5,4},{6,7},{7,6},{8,9},{9,8},{10,11... | collective-permute-start | bytes 1572872 | tf_op jit(solution)/shard_map/ppermute | solution.py:323
  33.7 14.4 %collective-permute-start.11 = (bf16[512,512]{1,0:T(8,128)(2,1)S(1)}, bf16[512,512]{1,0:T(8,128)(2,1)S(1)}, u32[]{:S(2)}, u32[]{:S(2)}) collective-permute-start(bf16[512,512]{1,0:T(8,128)(2,1)S(1)} %join.9.refs_11_), channel_id=1, source_target_pairs={{0,2},{1,3},{2,0},{3,1},{4,6},{5,7},{6,4},{7,5},{8,10},{9,11},{10,... | collective-permute-start | bytes 1572872 | tf_op jit(solution)/shard_map/ppermute | solution.py:323
  38.8 9.8 %collective-permute-start.7 = (bf16[16,7424]{1,0:T(8,128)(2,1)S(1)}, bf16[16,7424]{1,0:T(8,128)(2,1)S(1)}, u32[]{:S(2)}, u32[]{:S(2)}) collective-permute-start(bf16[16,7424]{1,0:T(8,128)(2,1)S(1)} %get-tuple-element.45), channel_id=1, source_target_pairs={{0,8},{8,0},{16,24},{24,16},{1,9},{9,1},{17,25},{25,17},{2,10},{10... | collective-permute-start | bytes 712712 | tf_op jit(solution)/shard_map/ppermute | solution.py:323
  40.4 12.2 %collective-permute-start.8 = (bf16[16,7424]{1,0:T(8,128)(2,1)S(1)}, bf16[16,7424]{1,0:T(8,128)(2,1)S(1)}, u32[]{:S(2)}, u32[]{:S(2)}) collective-permute-start(bf16[16,7424]{1,0:T(8,128)(2,1)S(1)} %get-tuple-element.46), channel_id=1, source_target_pairs={{0,16},{8,24},{16,0},{24,8},{1,17},{9,25},{17,1},{25,9},{2,18},{10... | collective-permute-start | bytes 712712 | tf_op jit(solution)/shard_map/ppermute | solution.py:323
  41.9 10.7 %collective-permute-start.9 = (bf16[16,7424]{1,0:T(8,128)(2,1)S(1)}, bf16[16,7424]{1,0:T(8,128)(2,1)S(1)}, u32[]{:S(2)}, u32[]{:S(2)}) collective-permute-start(bf16[16,7424]{1,0:T(8,128)(2,1)S(1)} %get-tuple-element.47), channel_id=1, source_target_pairs={{0,24},{8,16},{16,8},{24,0},{1,25},{9,17},{17,9},{25,1},{2,26},{10... | collective-permute-start | bytes 712712 | tf_op jit(solution)/shard_map/ppermute | solution.py:323
  42.4 10.3 %copy-start.2 = (f32[32,6656]{1,0:T(8,128)S(1)}, f32[32,6656]{1,0:T(8,128)}, u32[]{:S(2)}) copy-start(f32[32,6656]{1,0:T(8,128)} %refs_6_.5) | copy-start | bytes 2555908
  42.4 10.3 %copy-start.3 = (f32[32,2048]{1,0:T(8,128)S(1)}, f32[32,2048]{1,0:T(8,128)}, u32[]{:S(2)}) copy-start(f32[32,2048]{1,0:T(8,128)} %refs_9_.1) | copy-start | bytes 786436
  42.4 10.3 %copy-start.4 = (f32[32,6656]{1,0:T(8,128)S(1)}, f32[32,6656]{1,0:T(8,128)}, u32[]{:S(2)}) copy-start(f32[32,6656]{1,0:T(8,128)} %refs_7_.1) | copy-start | bytes 2555908
  42.4 10.3 %copy-start.5 = (f32[32,6656]{1,0:T(8,128)S(1)}, f32[32,6656]{1,0:T(8,128)}, u32[]{:S(2)}) copy-start(f32[32,6656]{1,0:T(8,128)} %refs_8_.1) | copy-start | bytes 2555908
  42.4 10.3 %copy-start.8 = (f32[32,2048]{1,0:T(8,128)S(1)}, f32[32,2048]{1,0:T(8,128)}, u32[]{:S(2)}) copy-start(f32[32,2048]{1,0:T(8,128)} %refs_10_.1) | copy-start | bytes 786436
  42.4 10.3 %copy-start.9 = (f32[32,2048]{1,0:T(8,128)S(1)}, f32[32,2048]{1,0:T(8,128)}, u32[]{:S(2)}) copy-start(f32[32,2048]{1,0:T(8,128)} %refs_11_.1) | copy-start | bytes 786436
  48.3 47.5 %collective-permute-start.21 = (bf16[512,512]{1,0:T(8,128)(2,1)S(1)}, bf16[512,512]{1,0:T(8,128)(2,1)S(1)}, u32[]{:S(2)}, u32[]{:S(2)}) collective-permute-start(bf16[512,512]{1,0:T(8,128)(2,1)S(1)} %join.10.refs_12_), channel_id=1, source_target_pairs={{0,4},{1,5},{2,6},{3,7},{4,0},{5,1},{6,2},{7,3},{8,12},{9,13},{10,... | collective-permute-start | bytes 1572872 | tf_op jit(solution)/shard_map/ppermute | solution.py:323
  56.7 7.4 %collective-permute-start.13 = (f32[8,512]{1,0:T(8,128)S(1)}, f32[8,512]{1,0:T(8,128)S(1)}, u32[]{:S(2)}, u32[]{:S(2)}) collective-permute-start(f32[8,512]{1,0:T(8,128)S(1)} %get-tuple-element.51.refs_3_.refs_0_), channel_id=1, source_target_pairs={{0,8},{8,0},{16,24},{24,16},{1,9},{9,1},{17,25},{25,17},{2,10},{10... | collective-permute-start | bytes 49160 | tf_op jit(solution)/shard_map/ppermute | solution.py:323
  61.7 10.4 %collective-permute-start.12 = (bf16[32,512]{1,0:T(8,128)(2,1)S(1)}, bf16[32,512]{1,0:T(8,128)(2,1)S(1)}, u32[]{:S(2)}, u32[]{:S(2)}) collective-permute-start(bf16[32,512]{1,0:T(8,128)(2,1)S(1)} %get-tuple-element.50), channel_id=1, source_target_pairs={{0,0},{1,4},{2,8},{3,12},{4,16},{5,20},{6,24},{7,28},{8,1},{9,5},{... | collective-permute-start | bytes 98312 | tf_op jit(solution)/shard_map/ppermute | solution.py:448
  62.4 20.5 %collective-permute-start.19 = (bf16[512,512]{1,0:T(8,128)(2,1)S(1)}, bf16[512,512]{1,0:T(8,128)(2,1)S(1)}, u32[]{:S(2)}, u32[]{:S(2)}) collective-permute-start(bf16[512,512]{1,0:T(8,128)(2,1)S(1)} %get-tuple-element.53.refs_2_), channel_id=1, source_target_pairs={{0,1},{1,0},{2,3},{3,2},{4,5},{5,4},{6,7},{7,6},{8,9},{9,8},{10,11... | collective-permute-start | bytes 1572872 | tf_op jit(solution)/shard_map/ppermute | solution.py:323
  64.1 8.0 %collective-permute-start.14 = (f32[16,512]{1,0:T(8,128)S(1)}, f32[16,512]{1,0:T(8,128)S(1)}, u32[]{:S(2)}, u32[]{:S(2)}) collective-permute-start(f32[16,512]{1,0:T(8,128)S(1)} %gather.2.refs_3_.refs_0_), channel_id=1, source_target_pairs={{0,16},{8,24},{16,0},{24,8},{1,17},{9,25},{17,1},{25,9},{2,18},{10... | collective-permute-start | bytes 98312 | tf_op jit(solution)/shard_map/ppermute | solution.py:323
  72.1 4.3 %collective-permute-start.15 = (f32[32,512]{1,0:T(8,128)S(1)}, f32[32,512]{1,0:T(8,128)S(1)}, u32[]{:S(2)}, u32[]{:S(2)}) collective-permute-start(f32[32,512]{1,0:T(8,128)S(1)} %gather.3.refs_3_.refs_0_), channel_id=1, source_target_pairs={{0,1},{1,0},{2,3},{3,2},{4,5},{5,4},{6,7},{7,6},{8,9},{9,8},{10,11... | collective-permute-start | bytes 196616 | tf_op jit(solution)/shard_map/ppermute | solution.py:323
  75.9 19.9 %collective-permute-start.18 = (bf16[512,512]{1,0:T(8,128)(2,1)S(1)}, bf16[512,512]{1,0:T(8,128)(2,1)S(1)}, u32[]{:S(2)}, u32[]{:S(2)}) collective-permute-start(bf16[512,512]{1,0:T(8,128)(2,1)S(1)} %get-tuple-element.57.refs_2_), channel_id=1, source_target_pairs={{0,1},{1,0},{2,3},{3,2},{4,5},{5,4},{6,7},{7,6},{8,9},{9,8},{10,11... | collective-permute-start | bytes 1572872 | tf_op jit(solution)/shard_map/ppermute | solution.py:323
  76.5 6.3 %collective-permute-start.16 = (f32[32,512]{1,0:T(8,128)S(1)}, f32[32,512]{1,0:T(8,128)S(1)}, u32[]{:S(2)}, u32[]{:S(2)}) collective-permute-start(f32[32,512]{1,0:T(8,128)S(1)} %join.11.refs_2_.refs_0_), channel_id=1, source_target_pairs={{0,2},{1,3},{2,0},{3,1},{4,6},{5,7},{6,4},{7,5},{8,10},{9,11},{10,... | collective-permute-start | bytes 196616 | tf_op jit(solution)/shard_map/ppermute | solution.py:323
  82.9 15.0 %collective-permute-start.20 = (bf16[512,512]{1,0:T(8,128)(2,1)S(1)}, bf16[512,512]{1,0:T(8,128)(2,1)S(1)}, u32[]{:S(2)}, u32[]{:S(2)}) collective-permute-start(bf16[512,512]{1,0:T(8,128)(2,1)S(1)} %join.13), channel_id=1, source_target_pairs={{0,2},{1,3},{2,0},{3,1},{4,6},{5,7},{6,4},{7,5},{8,10},{9,11},{10,... | collective-permute-start | bytes 1572872 | tf_op jit(solution)/shard_map/ppermute | solution.py:323
  83.6 12.2 %collective-permute-start.17 = (f32[32,512]{1,0:T(8,128)S(1)}, f32[32,512]{1,0:T(8,128)S(1)}, u32[]{:S(2)}, u32[]{:S(2)}) collective-permute-start(f32[32,512]{1,0:T(8,128)S(1)} %join.12.refs_2_.refs_1_), channel_id=1, source_target_pairs={{0,4},{1,5},{2,6},{3,7},{4,0},{5,1},{6,2},{7,3},{8,12},{9,13},{10,... | collective-permute-start | bytes 196616 | tf_op jit(solution)/shard_map/ppermute | solution.py:323
